TPU v7x, 32 devices: a whole 2x2x4 slice. The times are simulated.
32 devices in a mesh: rep: 2 (over core), row: 4 (over y, x), col: 4 (over z).
Axes of the slice: x: 2, y: 2, z: 4, core: 2. Of those that a mesh axis runs over, the one named last changes fastest.
Arguments:
- residual: bfloat16 [4096, 2048], P(('rep', 'row'), 'col'), may hold values from -6 to 6
- post_gain: float32 [2048], replicated, may hold values from 0.25 to 1.75
- w_gate: bfloat16 [2048, 6144], P('row', 'col'), may hold values from -0.125 to 0.125
- w_up: bfloat16 [2048, 6144], P('row', 'col'), may hold values from -0.125 to 0.125
- w_down: bfloat16 [6144, 2048], P('col', 'row'), may hold values from -0.078125 to 0.078125
- next_gain: float32 [2048], replicated, may hold values from 0.25 to 1.75
- w_qkv: bfloat16 [2048, 4096], P('row', 'col'), may hold values from -0.125 to 0.125
- q_gain: float32 [128], replicated, may hold values from 0.25 to 1.75
- k_gain: float32 [128], replicated, may hold values from 0.25 to 1.75
- source: int32 [4096], P(('rep', 'row')), may hold values from 0 to 4095, as said below
Outputs:
- moved_residual: bfloat16 [4096, 2048], P(('rep', 'row'), 'col')
- moved_qkv: bfloat16 [4096, 4096], P(('rep', 'row'), 'col')
Inputs may be any that keep to these rules, and one draw needn't show every extreme that they name: source is a permutation of all rows. Rows are grouped in blocks of 512 (block b holds rows b * 512 to (b + 1) * 512 - 1, blocks of replica 0 first); output block b takes its rows from input block b or from the block of the same row index in the other replica, at most 128 of them from the other replica, and some block takes exactly 128. A block takes as many rows from the other replica as it gives to it.
All inputs are finite; a program needn't handle non-finite values.
Results may differ from a plain program's by a relative error of at most 0.0065.
Values may be sent and summed in bfloat16 or wider, within the bound.
No kernel may reach another device: no remote copies, remote signals or barrier semaphores. Data moves between devices by JAX's collectives and lax.ppermute only.
A program may use at most 64 MiB of HBM per device.

v0:
```python
import jax
import jax.numpy as jnp
from jax import lax
from jax.sharding import PartitionSpec as P

HEADS = 16
KV_HEADS = 8
HD = 128


epsilon = 1e-06


def swapped(x, axis, apart):
    return lax.ppermute(x, axis, [(i, i ^ 1 << apart) for i in range(lax.axis_size(axis))])


def normalize(values, gain):
    scale = lax.rsqrt(jnp.mean(values * values, axis=-1, keepdims=True) + epsilon)
    return values * scale * gain


def per_device(residual, post_gain, w_gate, w_up, w_down, next_gain, w_qkv, q_gain, k_gain, source):
    tok_rows = residual.shape[0]
    col_index = lax.axis_index("col")
    gathered = lax.all_gather(residual, "col", axis=1, tiled=True)
    stream = gathered.astype(jnp.float32)
    normed = normalize(stream, post_gain).astype(jnp.bfloat16)
    columns = normed
    gate_proj = jnp.dot(
        columns,
        lax.all_gather(w_gate, "row", axis=0, tiled=True),
        preferred_element_type=jnp.float32,
    )
    up_proj = jnp.dot(
        columns, lax.all_gather(w_up, "row", axis=0, tiled=True), preferred_element_type=jnp.float32
    )
    hidden = (jax.nn.silu(gate_proj) * up_proj).astype(jnp.bfloat16)
    partial_value = jnp.dot(
        hidden,
        lax.all_gather(w_down, "row", axis=1, tiled=True),
        preferred_element_type=jnp.float32,
    )
    mlp_share = lax.psum_scatter(partial_value, "col", scatter_dimension=1, tiled=True)
    resid_own = (residual.astype(jnp.float32) + mlp_share).astype(jnp.bfloat16)
    resid_full = lax.all_gather(resid_own, "col", axis=1, tiled=True)
    next_normed = normalize(resid_full.astype(jnp.float32), next_gain).astype(jnp.bfloat16)
    proj_width = w_qkv.shape[1]
    columns = next_normed
    projected = jnp.dot(
        columns,
        lax.all_gather(w_qkv, "row", axis=0, tiled=True),
        preferred_element_type=jnp.float32,
    )
    head_count = proj_width // HD
    per_head = projected.reshape(tok_rows, head_count, HD)
    head_number = col_index * head_count + jnp.arange(head_count, dtype=jnp.int32)
    is_query = head_number < HEADS
    is_key = jnp.logical_and(head_number >= HEADS, head_number < HEADS + KV_HEADS)
    head_gain = jnp.where(is_query[:, None], q_gain[None, :], k_gain[None, :])
    head_scaled = normalize(per_head, head_gain)
    keep_norm = jnp.logical_or(is_query, is_key)[None, :, None]
    qkv_own = (
        jnp.where(keep_norm, head_scaled, per_head)
        .reshape(tok_rows, proj_width)
        .astype(jnp.bfloat16)
    )
    my_block = lax.axis_index("rep") * lax.axis_size("row") + lax.axis_index("row")
    from_peer = source // tok_rows != my_block
    local_row = source % tok_rows
    peer_resid, peer_qkv = swapped((resid_own, qkv_own), "rep", 0)
    picked = local_row + tok_rows * from_peer.astype(jnp.int32)
    moved_residual = jnp.take(jnp.concatenate([resid_own, peer_resid], axis=0), picked, axis=0)
    moved_qkv = jnp.take(jnp.concatenate([qkv_own, peer_qkv], axis=0), picked, axis=0)
    return (moved_residual, moved_qkv)


def solution(mesh):
    return jax.shard_map(
        per_device,
        mesh=mesh,
        in_specs=(
            P(("rep", "row"), "col"),
            P(),
            P("row", "col"),
            P("row", "col"),
            P("col", "row"),
            P(),
            P("row", "col"),
            P(),
            P(),
            P(("rep", "row")),
        ),
        out_specs=(P(("rep", "row"), "col"), P(("rep", "row"), "col")),
        check_vma=False,
    )
```

profile of v0, /device:TPU:0, one launch (start us, length us, event | category | flops | bytes accessed | tf_op | source)
XLA Modules:
  0.0 494.2 jit_solution(3728169770718953824)
XLA Ops:
  7.2 0.7 all-gather.7.cloned.1.call-update
  8.0 0.7 all-gather.9.cloned.1.call-update
  8.7 0.7 all-gather.11.cloned.1.call-update
  10.0 48.2 %all-gather.7.cloned.1.call-done = bf16[512,2048]{1,0:T(8,128)(2,1)} async-done(((bf16[512,512]{1,0:T(8,128)(2,1)}), bf16[512,2048]{1,0:T(8,128)(2,1)}) %all-gather.7.cloned.1.call-update) | async-done | bytes 2097168 | tf_op jit(solution)/shard_map/all_gather | solution.py:26
  58.2 2.1 fusion
  60.3 68.7 %all-gather.9.cloned.1.call-done = bf16[2048,1536]{1,0:T(8,128)(2,1)} async-done(((bf16[512,1536]{1,0:T(8,128)(2,1)}), bf16[2048,1536]{1,0:T(8,128)(2,1)}) %all-gather.9.cloned.1.call-update) | async-done | bytes 6291472 | tf_op jit(solution)/shard_map/all_gather | solution.py:32
  129.0 8.6 %fusion.17 = f32[512,1536]{1,0:T(8,128)} fusion(bf16[2048,1536]{1,0:T(8,128)(2,1)} %all-gather.9.cloned.1.call-done, bf16[512,2048]{1,0:T(8,128)(2,1)} %all-gather.7.cloned.1.call-done, f32[2048]{0:T(1024)S(1)} %copy-done.8, f32[512]{0:T(512)S(1)} %add_rsqrt_fusion.2), kind=kOutput, calls=%fused_computation.27 | convolution fusion | flops 3225419776 | bytes 11544576 | tf_op jit(solution)/shard_map/dot_general | solution.py:30
  137.6 63.5 %all-gather.11.cloned.1.call-done = bf16[2048,1536]{1,0:T(8,128)(2,1)} async-done(((bf16[512,1536]{1,0:T(8,128)(2,1)}), bf16[2048,1536]{1,0:T(8,128)(2,1)}) %all-gather.11.cloned.1.call-update) | async-done | bytes 6291472 | tf_op jit(solution)/shard_map/all_gather | solution.py:36
  201.0 71.7 %all-gather.13.cloned.1.call-done = bf16[1536,2048]{1,0:T(8,128)(2,1)} async-done(((bf16[1536,512]{1,0:T(8,128)(2,1)}), bf16[1536,2048]{1,0:T(8,128)(2,1)}) %all-gather.13.cloned.1.call-update) | async-done | bytes 6291472 | tf_op jit(solution)/shard_map/all_gather | solution.py:41
  272.8 14.3 %fusion.14 = f32[512,2048]{1,0:T(8,128)} fusion(bf16[1536,2048]{1,0:T(8,128)(2,1)} %all-gather.13.cloned.1.call-done, bf16[2048,1536]{1,0:T(8,128)(2,1)} %all-gather.11.cloned.1.call-done, f32[512,1536]{1,0:T(8,128)} %fusion.17, bf16[512,2048]{1,0:T(8,128)(2,1)S(1)} %copy-done.3, f32[2048]{0:T(1024)S(1)} %copy-done.8, f32[512]{0:T(512)S(1)} %add_rsqrt_fusion.2), kind=kOutput, calls=%fused_computation.26 | convolution fusion | flops 6451363840 | bytes 22030336 | tf_op jit(solution)/shard_map/dot_general | solution.py:39
  287.1 76.9 %reduce-scatter.2.cloned.1.call-done = f32[512,512]{1,0:T(8,128)} async-done(((f32[512,2048]{1,0:T(8,128)}), f32[512,512]{1,0:T(8,128)}) %reduce-scatter.2.cloned.1.call-update) | async-done | bytes 1048592 | tf_op jit(solution)/shard_map/reduce_scatter | solution.py:44
  364.0 2.2 add_convert_fusion
  367.1 45.7 %all-gather.15.cloned.1.call-done = bf16[512,2048]{1,0:T(8,128)(2,1)} async-done(((bf16[512,512]{1,0:T(8,128)(2,1)}), bf16[512,2048]{1,0:T(8,128)(2,1)}) %all-gather.15.cloned.1.call-update) | async-done | bytes 2097168 | tf_op jit(solution)/shard_map/all_gather | solution.py:46
  412.8 2.1 fusion.3
  414.9 51.4 %all-gather.17.cloned.1.call-done = bf16[2048,1024]{1,0:T(8,128)(2,1)} async-done(((bf16[512,1024]{1,0:T(8,128)(2,1)}), bf16[2048,1024]{1,0:T(8,128)(2,1)}) %all-gather.17.cloned.1.call-update) | async-done | bytes 4194320 | tf_op jit(solution)/shard_map/all_gather | solution.py:52
  466.3 5.2 %fusion.7 = f32[512,1024]{1,0:T(8,128)S(1)} fusion(bf16[2048,1024]{1,0:T(8,128)(2,1)} %all-gather.17.cloned.1.call-done, bf16[512,2048]{1,0:T(8,128)(2,1)} %all-gather.15.cloned.1.call-done, f32[2048]{0:T(1024)S(1)} %copy-done.9, f32[512]{0:T(512)S(1)} %add_rsqrt_fusion.1), kind=kOutput, calls=%fused_computation.14 | convolution fusion | flops 2151677952 | bytes 8398848 | tf_op jit(solution)/shard_map/dot_general | solution.py:50
  474.3 0.7 copy-done.1
  475.0 1.8 fusion.11
  477.3 2.5 collective-permute-done
  479.9 2.0 gather_fusion
  481.8 0.9 broadcast_select_fusion.1
  482.8 1.4 pad_maximum_fusion
  484.2 2.1 gather_fusion.1
  486.2 1.1 broadcast_select_fusion
  (48 shorter events, 5.1 us)
Async XLA Ops:
  7.2 51.1 %all-gather.7.cloned.1.call-start = ((), (), s32[]{:S(2)}) async-start(), calls=%async_computation.1 | async-start | bytes 2621440 | tf_op jit(solution)/shard_map/all_gather | solution.py:26
  7.9 121.1 %copy-start.8 = (f32[2048]{0:T(1024)S(1)}, f32[2048]{0:T(1024)}, u32[]{:S(2)}) copy-start(f32[2048]{0:T(1024)} %param.11) | copy-start | bytes 24580
  7.9 121.1 %all-gather.9.cloned.1.call-start = ((), (), s32[]{:S(2)}) async-start(), calls=%async_computation.2 | async-start | bytes 7864320 | tf_op jit(solution)/shard_map/all_gather | solution.py:32
  8.7 192.4 %all-gather.11.cloned.1.call-start = ((), (), s32[]{:S(2)}) async-start(), calls=%async_computation.3 | async-start | bytes 7864320 | tf_op jit(solution)/shard_map/all_gather | solution.py:36
  9.4 263.4 %all-gather.13.cloned.1.call-start = ((), (), s32[]{:S(2)}) async-start(), calls=%async_computation.4 | async-start | bytes 7864320 | tf_op jit(solution)/shard_map/all_gather | solution.py:41
  10.0 354.0 %reduce-scatter.2.cloned.1.call-start = ((), (), s32[]{:S(2)}) async-start(), calls=%async_computation.5 | async-start | bytes 5242880 | tf_op jit(solution)/shard_map/reduce_scatter | solution.py:44
  60.3 212.4 %copy-start.3 = (bf16[512,2048]{1,0:T(8,128)(2,1)S(1)}, bf16[512,2048]{1,0:T(8,128)(2,1)}, u32[]{:S(2)}) copy-start(bf16[512,2048]{1,0:T(8,128)(2,1)} %all-gather.7.cloned.1.call-done) | copy-start | bytes 6291460
  287.1 77.0 %copy-start.4 = (bf16[512,512]{1,0:T(8,128)(2,1)S(1)}, bf16[512,512]{1,0:T(8,128)(2,1)}, u32[]{:S(2)}) copy-start(bf16[512,512]{1,0:T(8,128)(2,1)} %param.10) | copy-start | bytes 1572868
  287.1 80.0 %copy-start.6 = (f32[128]{0:T(128)S(1)}, f32[128]{0:T(128)}, u32[]{:S(2)}) copy-start(f32[128]{0:T(128)} %param.18) | copy-start | bytes 1540
  287.1 80.0 %copy-start.7 = (f32[128]{0:T(128)S(1)}, f32[128]{0:T(128)}, u32[]{:S(2)}) copy-start(f32[128]{0:T(128)} %param.17) | copy-start | bytes 1540
  287.1 179.2 %copy-start.9 = (f32[2048]{0:T(1024)S(1)}, f32[2048]{0:T(1024)}, u32[]{:S(2)}) copy-start(f32[2048]{0:T(1024)} %param.15) | copy-start | bytes 24580
  287.1 125.7 %all-gather.15.cloned.1.call-start = ((), (), s32[]{:S(2)}) async-start(), calls=%async_computation.6 | async-start | bytes 2621440 | tf_op jit(solution)/shard_map/all_gather | solution.py:46
  366.2 100.0 %all-gather.17.cloned.1.call-start = ((), (), s32[]{:S(2)}) async-start(), calls=%async_computation.7 | async-start | bytes 5242880 | tf_op jit(solution)/shard_map/all_gather | solution.py:52
  471.5 1.3 copy-start
  473.4 1.6 copy-start.1
  474.3 2.5 copy-start.2
  474.3 3.0 copy-start.5
  476.7 6.0 %collective-permute-start.1 = (bf16[512,1024]{1,0:T(8,128)(2,1)}, bf16[512,1024]{1,0:T(8,128)(2,1)S(1)}, u32[]{:S(2)}, u32[]{:S(2)}) collective-permute-start(bf16[512,1024]{1,0:T(8,128)(2,1)} %fusion.11), channel_id=1, source_target_pairs={{0,16},{16,0},{1,17},{17,1},{2,18},{18,2},{3,19},{19,3},{4,20},{20... | collective-permute-start | bytes 3145736 | tf_op jit(solution)/shard_map/ppermute | solution.py:15
  476.8 3.0 collective-permute-start
Sparse Core Ops, SparseCore 0:
  9.6 48.6 all-gather.6
  60.1 68.8 all-gather.8
  130.8 70.1 all-gather.10
  202.7 70.0 all-gather.12
  287.2 76.7 reduce-scatter.1
  366.3 46.4 all-gather.14
  414.8 51.4 all-gather.16
where the time goes:
time: 495 us; the launch traced here: 494 us
  waiting for transfers between devices  432 us (87%)
  matrix products  28.1 us (6%)
  between operations  14.3 us (3%)
  other arithmetic  12.6 us (3%)
  local copies, waits for them, and re-layouts  6.71 us (1%)
    reduce_scatter x1, waiting for transfers between devices, per_device(): lax.psum_scatter(partial_value, 'col', scatter_dimension=1, tiled=True)  76.9 us
    all_gather x1, waiting for transfers between devices, per_device(): lax.all_gather(w_down, 'row', axis=1, tiled=True)  71.7 us
    all_gather x1, waiting for transfers between devices, per_device(): lax.all_gather(w_gate, 'row', axis=0, tiled=True)  68.7 us
    all_gather x1, waiting for transfers between devices, per_device(): lax.all_gather(w_up, 'row', axis=0, tiled=True)  63.5 us
    all_gather x1, waiting for transfers between devices, per_device(): lax.all_gather(w_qkv, 'row', axis=0, tiled=True)  51.4 us
    all_gather x1, waiting for transfers between devices, per_device(): gathered = lax.all_gather(residual, 'col', axis=1, tiled=True)  48.2 us
    all_gather x1, waiting for transfers between devices, per_device(): resid_full = lax.all_gather(resid_own, 'col', axis=1, tiled=True)  45.7 us
    dot_general x1, matrix products, per_device(): jnp.dot(hidden, lax.all_gather(w_down, 'row', axis=1, tiled=True), prefer...  14.3 us
  transfers between devices with their start and end apart: 9, of which 8 were waited for; matrix products, arithmetic and copies ran while one was open for 3% of the time, Pallas kernels for 0%

commit v1 on v0

v1 whole, which is shorter than its diff:
```python
import jax
import jax.numpy as jnp
from jax import lax
from jax.sharding import PartitionSpec as P

HEADS = 16
KV_HEADS = 8
HD = 128
epsilon = 1e-06
bf16, f32 = jnp.bfloat16, jnp.float32


def swap_cores(x):
    return lax.ppermute(x, "rep", [(0, 1), (1, 0)])


def bits_of(n):
    return n.bit_length() - 1


def row_step(x, step):
    rows = lax.axis_size("row")
    last = bits_of(rows) - 1
    pairs = []
    for core in range(2):
        mask = 1 << (step if core == 0 else last - step)
        pairs += [(core * rows + i, core * rows + (i ^ mask)) for i in range(rows)]
    return lax.ppermute(x, ("rep", "row"), pairs)


def mirrored(mask, bits):
    return sum(1 << (bits - 1 - b) for b in range(bits) if mask >> b & 1)


def gather_halves(half):
    rows = lax.axis_size("row")
    bits = bits_of(rows)
    held = {0: half}
    for step in range(bits):
        for mask in list(held):
            held[mask | 1 << step] = row_step(held[mask], step)
    mine = held
    swapped = {mask: swap_cores(piece) for mask, piece in held.items() if mask}
    return mine, swapped


def placed_rows(own, mine, swapped, core):
    rows = lax.axis_size("row")
    bits = bits_of(rows)
    out = [own]
    for mask in range(1, rows):
        other = mirrored(mask, bits)
        first = jnp.where(core == 0, mine[mask], swapped[mask])
        second = jnp.where(core == 0, swapped[other], mine[other])
        out += [first, second]
    return jnp.concatenate(out, axis=0)


def gather_line(x, cols):
    up = [(i, i + 1) for i in range(cols - 1)]
    down = [(i + 1, i) for i in range(cols - 1)]
    below, above = [], []
    a = d = x
    for _ in range(cols - 1):
        a = lax.ppermute(a, "col", up)
        d = lax.ppermute(d, "col", down)
        below.append(a)
        above.append(d)
    return below[::-1] + [x] + above


def sum_line(own, cols):
    total = own
    carry = own.astype(bf16)
    for hop in range(cols - 1):
        got = lax.ppermute(carry, "col", [(hop, hop + 1), (cols - 1 - hop, cols - 2 - hop)])
        got = got.astype(f32)
        total = total + got
        carry = (own + got).astype(bf16)
    return total


def per_device(residual, post_gain, w_gate, w_up, w_down, next_gain, w_qkv, q_gain, k_gain, source):
    rows, cols = lax.axis_size("row"), lax.axis_size("col")
    me, core, col = lax.axis_index("row"), lax.axis_index("rep"), lax.axis_index("col")
    tok, width = residual.shape
    d_model = width * cols
    block = d_model // rows
    ff = w_gate.shape[1]

    my_block = core * rows + me
    from_peer = source // tok != my_block
    picked = source % tok + tok * from_peer.astype(jnp.int32)
    onehot = (picked[:, None] == jnp.arange(2 * tok, dtype=jnp.int32)[None, :]).astype(bf16)
    both = jnp.concatenate([residual, swap_cores(residual)], axis=0)
    placed = jnp.dot(onehot, both, preferred_element_type=f32).astype(bf16)

    line = jnp.concatenate(gather_line(placed, cols), axis=1)

    def rel(mask):
        at = (cols - 1 + (me ^ mask) - col) * block
        return lax.dynamic_slice_in_dim(line, at, block, 1)

    stream = jnp.concatenate([rel(m) for m in range(rows)], axis=1)

    def rel_gain(gain):
        g = gain.reshape(rows, block)
        return jnp.concatenate([lax.dynamic_index_in_dim(g, me ^ m, 0, False) for m in range(rows)])

    post_rel, next_rel = rel_gain(post_gain), rel_gain(next_gain)

    wide = stream.astype(f32)
    scale = lax.rsqrt(jnp.mean(wide * wide, axis=-1, keepdims=True) + epsilon)
    normed = (wide * scale * post_rel).astype(bf16)

    parts = 2 if ff % 512 == 0 else 1
    step = ff // parts
    half = block // 2
    hidden = []
    for n in range(parts):
        own = jnp.concatenate([w_gate[:, n * step:(n + 1) * step], w_up[:, n * step:(n + 1) * step]], axis=1)
        mine, swapped = gather_halves(lax.dynamic_slice_in_dim(own, core * half, half, 0))
        full = placed_rows(own, mine, swapped, core)
        both_proj = jnp.dot(normed, full, preferred_element_type=f32)
        hidden.append((jax.nn.silu(both_proj[:, :step]) * both_proj[:, step:]).astype(bf16))
    hidden = jnp.concatenate(hidden, axis=1) if parts > 1 else hidden[0]

    chunks = max(1, min(4, block // 128))
    w = block // chunks
    groups = [[0], [1], [2, 3]] if chunks == 4 else [[c] for c in range(chunks)]
    new_chunks = []
    ff_half = ff // 2
    for group in groups:
        own = w_down[:, group[0] * w:(group[-1] + 1) * w]
        mine, swapped = gather_halves(lax.dynamic_slice_in_dim(own, core * ff_half, ff_half, 0))
        bits = bits_of(rows)
        cols_full = [own]
        for mask in range(1, rows):
            other = mirrored(mask, bits)
            cols_full.append(jnp.concatenate([
                jnp.where(core == 0, mine[mask], swapped[mask]),
                jnp.where(core == 0, swapped[other], mine[other])], axis=0))
        for k, c in enumerate(group):
            rhs = jnp.concatenate([b[:, k * w:(k + 1) * w] for b in cols_full], axis=1)
            part = jnp.dot(hidden, rhs, preferred_element_type=f32)
            total = sum_line(part, cols)
            here = jnp.concatenate([stream[:, m * block + c * w:m * block + (c + 1) * w] for m in range(rows)], axis=1)
            new_chunks.append((here.astype(f32) + total).astype(bf16))

    mine, swapped = gather_halves(lax.dynamic_slice_in_dim(w_qkv, core * half, half, 0))
    full = placed_rows(w_qkv, mine, swapped, core)
    proj_width = w_qkv.shape[1]
    acc = jnp.zeros((tok, proj_width), f32)
    squares = jnp.zeros((tok, 1), f32)
    full_blocks = full.reshape(rows, chunks, w, proj_width)
    gain_blocks = next_rel.reshape(rows, chunks, w)
    for c in range(chunks):
        v = new_chunks[c].astype(f32)
        squares = squares + jnp.sum(v * v, axis=-1, keepdims=True)
        lhs = (v * gain_blocks[:, c].reshape(-1)).astype(bf16)
        acc = acc + jnp.dot(lhs, full_blocks[:, c].reshape(rows * w, proj_width), preferred_element_type=f32)
    projected = acc * lax.rsqrt(squares / d_model + epsilon)

    head_count = proj_width // HD
    per_head = projected.reshape(tok, head_count, HD)
    head_number = col * head_count + jnp.arange(head_count, dtype=jnp.int32)
    is_query = head_number < HEADS
    keep_norm = (head_number < HEADS + KV_HEADS)[None, :, None]
    head_gain = jnp.where(is_query[:, None], q_gain[None, :], k_gain[None, :])
    head_scale = lax.rsqrt(jnp.mean(per_head * per_head, axis=-1, keepdims=True) + epsilon)
    moved_qkv = jnp.where(keep_norm, per_head * head_scale * head_gain, per_head)
    moved_qkv = moved_qkv.reshape(tok, proj_width).astype(bf16)

    at = (me ^ col) * w
    moved_residual = jnp.concatenate(
        [lax.dynamic_slice_in_dim(chunk, at, w, 1) for chunk in new_chunks], axis=1)
    return (moved_residual, moved_qkv)


def solution(mesh):
    return jax.shard_map(
        per_device,
        mesh=mesh,
        in_specs=(
            P(("rep", "row"), "col"),
            P(),
            P("row", "col"),
            P("row", "col"),
            P("col", "row"),
            P(),
            P("row", "col"),
            P(),
            P(),
            P(("rep", "row")),
        ),
        out_specs=(P(("rep", "row"), "col"), P(("rep", "row"), "col")),
        check_vma=False,
    )
```

time: 495 us -> 265 us (0.54)
  waiting for transfers between devices: 432 us -> 158 us
  starting transfers between devices: 0.96 us -> 54.1 us
  matrix products: 28.1 us -> 15.5 us
  between operations: 14.3 us -> 1.77 us
  other arithmetic: 12.6 us -> 20.2 us
  local copies, waits for them, and re-layouts: 6.71 us -> 14.2 us
    all_gather x6 -> x0, waiting for transfers between devices: 349 us -> none  [the longest x1 71.7 us: per_device(): lax.all_gather(w_down, 'row', axis=1, tiled=True)]
    ppermute x2 -> x55, waiting for transfers between devices: 2.5 us -> 158 us  [the longest x12 72.8 us: sum_line(): lax.ppermute(carry, 'col', [(hop, hop + 1), (cols - 1 - hop, cols - 2 - h...]
    reduce_scatter x1 -> x0, waiting for transfers between devices: 76.9 us -> none  [per_device(): lax.psum_scatter(partial_value, 'col', scatter_dimension=1, tiled=True)]
    ppermute x2 -> x55, starting transfers between devices: 0.51 us -> 54.1 us  [the longest x18 21.7 us: row_step(): return lax.ppermute(x, ('rep', 'row'), pairs)]
    dot_general x3 -> x11, matrix products: 28.1 us -> 15.5 us  [the longest x2 7.15 us: per_device(): both_proj = jnp.dot(normed, full, preferred_element_type=f32)]
    slice x0 -> x8, local copies, waits for them, and re-layouts: none -> 4.99 us  [the longest x3 2.55 us: per_device(): own = w_down[:, group[0] * w:(group[-1] + 1) * w]]
  transfers between devices with their start and end apart: 9 -> 55, of which waited for: 8 -> 25; matrix products, arithmetic and copies ran while one was open for 3% -> 11% of each run, Pallas kernels for 0% -> 0%
where the time goes in v1:
time: 265 us; the launch traced here: 264 us
  waiting for transfers between devices  158 us (60%)
  starting transfers between devices  54.1 us (20%)
  other arithmetic  20.2 us (8%)
  matrix products  15.5 us (6%)
  local copies, waits for them, and re-layouts  14.2 us (5%)
    ppermute x12, waiting for transfers between devices, sum_line(): lax.ppermute(carry, 'col', [(hop, hop + 1), (cols - 1 - hop, cols - 2 - h...  72.8 us
    ppermute x18, waiting for transfers between devices, row_step(): return lax.ppermute(x, ('rep', 'row'), pairs)  52.3 us
    ppermute x18, starting transfers between devices, row_step(): return lax.ppermute(x, ('rep', 'row'), pairs)  21.7 us
    ppermute x3, waiting for transfers between devices, gather_line(): a = lax.ppermute(a, 'col', up)  17.5 us
    ppermute x12, starting transfers between devices, sum_line(): lax.ppermute(carry, 'col', [(hop, hop + 1), (cols - 1 - hop, cols - 2 - h...  14.6 us
    ppermute x3, waiting for transfers between devices, gather_line(): d = lax.ppermute(d, 'col', down)  13.9 us
    ppermute x3, starting transfers between devices, gather_line(): a = lax.ppermute(a, 'col', up)  10.5 us
    dot_general x2, matrix products, per_device(): both_proj = jnp.dot(normed, full, preferred_element_type=f32)  7.15 us
  transfers between devices with their start and end apart: 55, of which 25 were waited for; matrix products, arithmetic and copies ran while one was open for 11% of the time, Pallas kernels for 0%

profile of v1, /device:TPU:0, one launch (start us, length us, event | category | flops | bytes accessed | tf_op | source)
XLA Modules:
  0.0 263.9 jit_solution(13313934630009389851)
XLA Ops:
  29.0 6.1 %collective-permute-done.23 = bf16[768,128]{1,0:T(8,128)(2,1)S(1)} collective-permute-done((bf16[768,128]{1,0:T(8,128)(2,1)}, bf16[768,128]{1,0:T(8,128)(2,1)S(1)}, u32[]{:S(2)}, u32[]{:S(2)}) %collective-permute-start.23) | collective-permute-done | bytes 196640 | tf_op jit(solution)/shard_map/ppermute | solution.py:28
  37.0 4.0 %collective-permute-done.32 = bf16[768,128]{1,0:T(8,128)(2,1)S(1)} collective-permute-done((bf16[768,128]{1,0:T(8,128)(2,1)}, bf16[768,128]{1,0:T(8,128)(2,1)S(1)}, u32[]{:S(2)}, u32[]{:S(2)}) %collective-permute-start.32) | collective-permute-done | bytes 196640 | tf_op jit(solution)/shard_map/ppermute | solution.py:28
  46.1 8.9 %collective-permute-done.51 = bf16[256,1024]{1,0:T(8,128)(2,1)S(1)} collective-permute-done((bf16[256,1024]{1,0:T(8,128)(2,1)S(1)}, bf16[256,1024]{1,0:T(8,128)(2,1)S(1)}, u32[]{:S(2)}, u32[]{:S(2)}) %collective-permute-start.51) | collective-permute-done | bytes 524320 | tf_op jit(solution)/shard_map/ppermute | solution.py:28
  58.5 21.2 %collective-permute-done.41 = bf16[768,256]{1,0:T(8,128)(2,1)S(1)} collective-permute-done((bf16[768,256]{1,0:T(8,128)(2,1)}, bf16[768,256]{1,0:T(8,128)(2,1)S(1)}, u32[]{:S(2)}, u32[]{:S(2)}) %collective-permute-start.41) | collective-permute-done | bytes 393248 | tf_op jit(solution)/shard_map/ppermute | solution.py:28
  81.1 7.7 %collective-permute-done.53 = bf16[256,1024]{1,0:T(8,128)(2,1)S(1)} collective-permute-done((bf16[256,1024]{1,0:T(8,128)(2,1)S(1)}, bf16[256,1024]{1,0:T(8,128)(2,1)S(1)}, u32[]{:S(2)}, u32[]{:S(2)}) %collective-permute-start.53) | collective-permute-done | bytes 524320 | tf_op jit(solution)/shard_map/ppermute | solution.py:28
  90.2 3.5 %collective-permute-start.1 = (bf16[512,512]{0,1:T(8,128)(2,1)S(1)}, bf16[512,512]{0,1:T(8,128)(2,1)S(1)}, u32[]{:S(2)}, u32[]{:S(2)}) collective-permute-start(bf16[512,512]{0,1:T(8,128)(2,1)S(1)} %fusion.63), channel_id=1, source_target_pairs={{0,1},{1,2},{2,3},{4,5},{5,6},{6,7},{8,9},{9,10},{10,11},{12,13},{... | collective-permute-start | bytes 1572872 | tf_op jit(solution)/shard_map/ppermute | solution.py:65
  101.1 3.9 %collective-permute-done.1 = bf16[512,512]{0,1:T(8,128)(2,1)S(1)} collective-permute-done((bf16[512,512]{0,1:T(8,128)(2,1)S(1)}, bf16[512,512]{0,1:T(8,128)(2,1)S(1)}, u32[]{:S(2)}, u32[]{:S(2)}) %collective-permute-start.1) | collective-permute-done | bytes 524320 | tf_op jit(solution)/shard_map/ppermute | solution.py:65
  105.1 7.0 %collective-permute-done.4 = bf16[512,512]{0,1:T(8,128)(2,1)S(1)} collective-permute-done((bf16[512,512]{0,1:T(8,128)(2,1)S(1)}, bf16[512,512]{0,1:T(8,128)(2,1)S(1)}, u32[]{:S(2)}, u32[]{:S(2)}) %collective-permute-start.4) | collective-permute-done | bytes 524320 | tf_op jit(solution)/shard_map/ppermute | solution.py:66
  112.1 3.5 %collective-permute-start.2 = (bf16[512,512]{0,1:T(8,128)(2,1)S(1)}, bf16[512,512]{0,1:T(8,128)(2,1)S(1)}, u32[]{:S(2)}, u32[]{:S(2)}) collective-permute-start(bf16[512,512]{0,1:T(8,128)(2,1)S(1)} %collective-permute-done.1), channel_id=1, source_target_pairs={{0,1},{1,2},{2,3},{4,5},{5,6},{6,7},{8,9},{9,10},{10,11},{12,13},{... | collective-permute-start | bytes 1572872 | tf_op jit(solution)/shard_map/ppermute | solution.py:65
  117.5 8.7 %collective-permute-done.2 = bf16[512,512]{0,1:T(8,128)(2,1)S(1)} collective-permute-done((bf16[512,512]{0,1:T(8,128)(2,1)S(1)}, bf16[512,512]{0,1:T(8,128)(2,1)S(1)}, u32[]{:S(2)}, u32[]{:S(2)}) %collective-permute-start.2) | collective-permute-done | bytes 524320 | tf_op jit(solution)/shard_map/ppermute | solution.py:65
  127.4 3.0 %collective-permute-done.5 = bf16[512,512]{0,1:T(8,128)(2,1)S(1)} collective-permute-done((bf16[512,512]{0,1:T(8,128)(2,1)S(1)}, bf16[512,512]{0,1:T(8,128)(2,1)S(1)}, u32[]{:S(2)}, u32[]{:S(2)}) %collective-permute-start.5) | collective-permute-done | bytes 524320 | tf_op jit(solution)/shard_map/ppermute | solution.py:66
  130.3 3.5 %collective-permute-start.3 = (bf16[512,512]{0,1:T(8,128)(2,1)S(1)}, bf16[512,512]{0,1:T(8,128)(2,1)S(1)}, u32[]{:S(2)}, u32[]{:S(2)}) collective-permute-start(bf16[512,512]{0,1:T(8,128)(2,1)S(1)} %collective-permute-done.2), channel_id=1, source_target_pairs={{0,1},{1,2},{2,3},{4,5},{5,6},{6,7},{8,9},{9,10},{10,11},{12,13},{... | collective-permute-start | bytes 1572872 | tf_op jit(solution)/shard_map/ppermute | solution.py:65
  138.4 4.9 %collective-permute-done.3 = bf16[512,512]{0,1:T(8,128)(2,1)S(1)} collective-permute-done((bf16[512,512]{0,1:T(8,128)(2,1)S(1)}, bf16[512,512]{0,1:T(8,128)(2,1)S(1)}, u32[]{:S(2)}, u32[]{:S(2)}) %collective-permute-start.3) | collective-permute-done | bytes 524320 | tf_op jit(solution)/shard_map/ppermute | solution.py:65
  143.5 3.9 %collective-permute-done.6 = bf16[512,512]{0,1:T(8,128)(2,1)S(1)} collective-permute-done((bf16[512,512]{0,1:T(8,128)(2,1)S(1)}, bf16[512,512]{0,1:T(8,128)(2,1)S(1)}, u32[]{:S(2)}, u32[]{:S(2)}) %collective-permute-start.6) | collective-permute-done | bytes 524320 | tf_op jit(solution)/shard_map/ppermute | solution.py:66
  148.8 3.6 %fusion.101 = f32[512,1536]{1,0:T(8,128)S(1)} fusion(bf16[2048,1536]{1,0:T(8,128)(2,1)S(1)} %select_dynamic-update-slice_fusion.6, f32[2048]{0:T(1024)S(1)} %pad_maximum_fusion.5, f32[512]{0:T(512)S(1)} %add_rsqrt_fusion.2, bf16[512,512]{0,1:T(8,128)(2,1)S(1)} %get-tuple-element.39, bf16[512,512]{0,1:T(8,128)(2,1)S(1)} %get-tuple-element.40, ...), kind=kOutput, calls=%fused_computation.158 | convolution fusion | flops 3232759808 | bytes 11544576 | tf_op jit(solution)/shard_map/dot_general | solution.py:124
  153.2 3.6 %fusion.99 = f32[512,1536]{1,0:T(8,128)S(1)} fusion(bf16[2048,1536]{1,0:T(8,128)(2,1)S(1)} %select_dynamic-update-slice_fusion, f32[2048]{0:T(1024)S(1)} %pad_maximum_fusion.5, f32[512]{0:T(512)S(1)} %add_rsqrt_fusion.2, bf16[512,512]{0,1:T(8,128)(2,1)S(1)} %get-tuple-element.39, bf16[512,512]{0,1:T(8,128)(2,1)S(1)} %get-tuple-element.40, ...), kind=kOutput, calls=%fused_computation.157 | convolution fusion | flops 3232759808 | bytes 11544576 | tf_op jit(solution)/shard_map/dot_general | solution.py:124
  168.7 5.0 %collective-permute-done.25 = bf16[512,512]{0,1:T(8,128)(2,1)S(1)} collective-permute-done((bf16[512,512]{0,1:T(8,128)(2,1)S(1)}, bf16[512,512]{0,1:T(8,128)(2,1)S(1)}, u32[]{:S(2)}, u32[]{:S(2)}) %collective-permute-start.25) | collective-permute-done | bytes 524320 | tf_op jit(solution)/shard_map/ppermute | solution.py:76
  174.5 10.4 %collective-permute-done.34 = bf16[512,512]{0,1:T(8,128)(2,1)S(1)} collective-permute-done((bf16[512,512]{0,1:T(8,128)(2,1)S(1)}, bf16[512,512]{0,1:T(8,128)(2,1)S(1)}, u32[]{:S(2)}, u32[]{:S(2)}) %collective-permute-start.34) | collective-permute-done | bytes 524320 | tf_op jit(solution)/shard_map/ppermute | solution.py:76
  185.8 10.4 %collective-permute-done.43 = bf16[512,512]{0,1:T(8,128)(2,1)S(1)} collective-permute-done((bf16[512,512]{0,1:T(8,128)(2,1)S(1)}, bf16[512,512]{0,1:T(8,128)(2,1)S(1)}, u32[]{:S(2)}, u32[]{:S(2)}) %collective-permute-start.43) | collective-permute-done | bytes 524320 | tf_op jit(solution)/shard_map/ppermute | solution.py:76
  197.0 6.5 %collective-permute-done.46 = bf16[512,512]{0,1:T(8,128)(2,1)S(1)} collective-permute-done((bf16[512,512]{0,1:T(8,128)(2,1)S(1)}, bf16[512,512]{0,1:T(8,128)(2,1)S(1)}, u32[]{:S(2)}, u32[]{:S(2)}) %collective-permute-start.46) | collective-permute-done | bytes 524320 | tf_op jit(solution)/shard_map/ppermute | solution.py:76
  210.3 12.6 %collective-permute-done.27 = bf16[512,512]{0,1:T(8,128)(2,1)S(1)} collective-permute-done((bf16[512,512]{0,1:T(8,128)(2,1)S(1)}, bf16[512,512]{0,1:T(8,128)(2,1)S(1)}, u32[]{:S(2)}, u32[]{:S(2)}) %collective-permute-start.27) | collective-permute-done | bytes 524320 | tf_op jit(solution)/shard_map/ppermute | solution.py:76
  223.4 10.8 %collective-permute-done.36 = bf16[512,512]{0,1:T(8,128)(2,1)S(1)} collective-permute-done((bf16[512,512]{0,1:T(8,128)(2,1)S(1)}, bf16[512,512]{0,1:T(8,128)(2,1)S(1)}, u32[]{:S(2)}, u32[]{:S(2)}) %collective-permute-start.36) | collective-permute-done | bytes 524320 | tf_op jit(solution)/shard_map/ppermute | solution.py:76
  234.6 10.8 %collective-permute-done.45 = bf16[512,512]{0,1:T(8,128)(2,1)S(1)} collective-permute-done((bf16[512,512]{0,1:T(8,128)(2,1)S(1)}, bf16[512,512]{0,1:T(8,128)(2,1)S(1)}, u32[]{:S(2)}, u32[]{:S(2)}) %collective-permute-start.45) | collective-permute-done | bytes 524320 | tf_op jit(solution)/shard_map/ppermute | solution.py:76
  245.8 6.3 %collective-permute-done.48 = bf16[512,512]{0,1:T(8,128)(2,1)S(1)} collective-permute-done((bf16[512,512]{0,1:T(8,128)(2,1)S(1)}, bf16[512,512]{0,1:T(8,128)(2,1)S(1)}, u32[]{:S(2)}, u32[]{:S(2)}) %collective-permute-start.48) | collective-permute-done | bytes 524320 | tf_op jit(solution)/shard_map/ppermute | solution.py:76
  (232 shorter events, 92.4 us)
Async XLA Ops:
  3.9 15.7 %collective-permute-start.19 = (bf16[768,128]{1,0:T(8,128)(2,1)}, bf16[768,128]{1,0:T(8,128)(2,1)}, u32[]{:S(2)}, u32[]{:S(2)}) collective-permute-start(bf16[768,128]{1,0:T(8,128)(2,1)} %constant_dynamic-slice_fusion.25), channel_id=1, source_target_pairs={{0,4},{4,0},{8,12},{12,8},{16,24},{20,28},{24,16},{28,20},{1,5},{5... | collective-permute-start | bytes 589832 | tf_op jit(solution)/shard_map/ppermute | solution.py:28
  10.4 31.6 %collective-permute-start.37 = (bf16[768,256]{1,0:T(8,128)(2,1)}, bf16[768,256]{1,0:T(8,128)(2,1)}, u32[]{:S(2)}, u32[]{:S(2)}) collective-permute-start(bf16[768,256]{1,0:T(8,128)(2,1)} %constant_dynamic-slice_fusion.21), channel_id=1, source_target_pairs={{0,4},{4,0},{8,12},{12,8},{16,24},{20,28},{24,16},{28,20},{1,5},{5... | collective-permute-start | bytes 1179656 | tf_op jit(solution)/shard_map/ppermute | solution.py:28
  19.7 22.8 %collective-permute-start.39 = (bf16[768,256]{1,0:T(8,128)(2,1)}, bf16[768,256]{1,0:T(8,128)(2,1)S(1)}, u32[]{:S(2)}, u32[]{:S(2)}) collective-permute-start(bf16[768,256]{1,0:T(8,128)(2,1)} %constant_dynamic-slice_fusion.21), channel_id=1, source_target_pairs={{0,8},{4,12},{8,0},{12,4},{16,20},{20,16},{24,28},{28,24},{1,9},{5... | collective-permute-start | bytes 1179656 | tf_op jit(solution)/shard_map/ppermute | solution.py:28
  24.1 19.9 %collective-permute-start.49 = (bf16[256,1024]{1,0:T(8,128)(2,1)S(1)}, bf16[256,1024]{1,0:T(8,128)(2,1)S(1)}, u32[]{:S(2)}, u32[]{:S(2)}) collective-permute-start(bf16[256,1024]{1,0:T(8,128)(2,1)S(1)} %constant_dynamic-slice_fusion.14), channel_id=1, source_target_pairs={{0,4},{4,0},{8,12},{12,8},{16,24},{20,28},{24,16},{28,20},{1,5},{5... | collective-permute-start | bytes 1572872 | tf_op jit(solution)/shard_map/ppermute | solution.py:28
  42.6 47.6 %collective-permute-start.7 = (bf16[256,1536]{1,0:T(8,128)(2,1)S(1)}, bf16[256,1536]{1,0:T(8,128)(2,1)S(1)}, u32[]{:S(2)}, u32[]{:S(2)}) collective-permute-start(bf16[256,1536]{1,0:T(8,128)(2,1)S(1)} %copy-done.7), channel_id=1, source_target_pairs={{0,4},{4,0},{8,12},{12,8},{16,24},{20,28},{24,16},{28,20},{1,5},{5... | collective-permute-start | bytes 2359304 | tf_op jit(solution)/shard_map/ppermute | solution.py:28
  44.0 49.8 %collective-permute-start.9 = (bf16[256,1536]{1,0:T(8,128)(2,1)S(1)}, bf16[256,1536]{1,0:T(8,128)(2,1)S(1)}, u32[]{:S(2)}, u32[]{:S(2)}) collective-permute-start(bf16[256,1536]{1,0:T(8,128)(2,1)S(1)} %copy-done.7), channel_id=1, source_target_pairs={{0,8},{4,12},{8,0},{12,4},{16,20},{20,16},{24,28},{28,24},{1,9},{5... | collective-permute-start | bytes 2359304 | tf_op jit(solution)/shard_map/ppermute | solution.py:28
  55.0 24.6 %collective-permute-start.41 = (bf16[768,256]{1,0:T(8,128)(2,1)}, bf16[768,256]{1,0:T(8,128)(2,1)S(1)}, u32[]{:S(2)}, u32[]{:S(2)}) collective-permute-start(bf16[768,256]{1,0:T(8,128)(2,1)} %collective-permute-done.37), channel_id=1, source_target_pairs={{0,8},{4,12},{8,0},{12,4},{16,20},{20,16},{24,28},{28,24},{1,9},{5... | collective-permute-start | bytes 1179656 | tf_op jit(solution)/shard_map/ppermute | solution.py:28
  56.1 24.6 %collective-permute-start.52 = (bf16[256,1024]{1,0:T(8,128)(2,1)S(1)}, bf16[256,1024]{1,0:T(8,128)(2,1)S(1)}, u32[]{:S(2)}, u32[]{:S(2)}) collective-permute-start(bf16[256,1024]{1,0:T(8,128)(2,1)S(1)} %collective-permute-done.51), channel_id=1, source_target_pairs={{0,16},{16,0},{1,17},{17,1},{2,18},{18,2},{3,19},{19,3},{4,20},{20... | collective-permute-start | bytes 1572872 | tf_op jit(solution)/shard_map/ppermute | solution.py:14
  56.2 41.6 %collective-permute-start.13 = (bf16[256,1536]{1,0:T(8,128)(2,1)S(1)}, bf16[256,1536]{1,0:T(8,128)(2,1)S(1)}, u32[]{:S(2)}, u32[]{:S(2)}) collective-permute-start(bf16[256,1536]{1,0:T(8,128)(2,1)S(1)} %fusion.92), channel_id=1, source_target_pairs={{0,4},{4,0},{8,12},{12,8},{16,24},{20,28},{24,16},{28,20},{1,5},{5... | collective-permute-start | bytes 2359304 | tf_op jit(solution)/shard_map/ppermute | solution.py:28
  90.2 14.8 %collective-permute-start.1 = (bf16[512,512]{0,1:T(8,128)(2,1)S(1)}, bf16[512,512]{0,1:T(8,128)(2,1)S(1)}, u32[]{:S(2)}, u32[]{:S(2)}) collective-permute-start(bf16[512,512]{0,1:T(8,128)(2,1)S(1)} %fusion.63), channel_id=1, source_target_pairs={{0,1},{1,2},{2,3},{4,5},{5,6},{6,7},{8,9},{9,10},{10,11},{12,13},{... | collective-permute-start | bytes 1572872 | tf_op jit(solution)/shard_map/ppermute | solution.py:65
  93.9 21.7 %collective-permute-start.10 = (bf16[256,1536]{1,0:T(8,128)(2,1)S(1)}, bf16[256,1536]{1,0:T(8,128)(2,1)S(1)}, u32[]{:S(2)}, u32[]{:S(2)}) collective-permute-start(bf16[256,1536]{1,0:T(8,128)(2,1)S(1)} %collective-permute-done.9), channel_id=1, source_target_pairs={{0,16},{16,0},{1,17},{17,1},{2,18},{18,2},{3,19},{19,3},{4,20},{20... | collective-permute-start | bytes 2359304 | tf_op jit(solution)/shard_map/ppermute | solution.py:14
  96.1 16.0 %collective-permute-start.4 = (bf16[512,512]{0,1:T(8,128)(2,1)S(1)}, bf16[512,512]{0,1:T(8,128)(2,1)S(1)}, u32[]{:S(2)}, u32[]{:S(2)}) collective-permute-start(bf16[512,512]{0,1:T(8,128)(2,1)S(1)} %fusion.63), channel_id=1, source_target_pairs={{1,0},{2,1},{3,2},{5,4},{6,5},{7,6},{9,8},{10,9},{11,10},{13,12},{... | collective-permute-start | bytes 1572872 | tf_op jit(solution)/shard_map/ppermute | solution.py:66
  97.8 36.0 %collective-permute-start.11 = (bf16[256,1536]{1,0:T(8,128)(2,1)S(1)}, bf16[256,1536]{1,0:T(8,128)(2,1)S(1)}, u32[]{:S(2)}, u32[]{:S(2)}) collective-permute-start(bf16[256,1536]{1,0:T(8,128)(2,1)S(1)} %collective-permute-done.7), channel_id=1, source_target_pairs={{0,8},{4,12},{8,0},{12,4},{16,20},{20,16},{24,28},{28,24},{1,9},{5... | collective-permute-start | bytes 2359304 | tf_op jit(solution)/shard_map/ppermute | solution.py:28
  101.1 34.2 %collective-permute-start.14 = (bf16[256,1536]{1,0:T(8,128)(2,1)S(1)}, bf16[256,1536]{1,0:T(8,128)(2,1)S(1)}, u32[]{:S(2)}, u32[]{:S(2)}) collective-permute-start(bf16[256,1536]{1,0:T(8,128)(2,1)S(1)} %collective-permute-done.13), channel_id=1, source_target_pairs={{0,16},{16,0},{1,17},{17,1},{2,18},{18,2},{3,19},{19,3},{4,20},{20... | collective-permute-start | bytes 2359304 | tf_op jit(solution)/shard_map/ppermute | solution.py:14
  105.0 30.6 %collective-permute-start.16 = (bf16[256,1536]{1,0:T(8,128)(2,1)S(1)}, bf16[256,1536]{1,0:T(8,128)(2,1)S(1)}, u32[]{:S(2)}, u32[]{:S(2)}) collective-permute-start(bf16[256,1536]{1,0:T(8,128)(2,1)S(1)} %collective-permute-done.15), channel_id=1, source_target_pairs={{0,16},{16,0},{1,17},{17,1},{2,18},{18,2},{3,19},{19,3},{4,20},{20... | collective-permute-start | bytes 2359304 | tf_op jit(solution)/shard_map/ppermute | solution.py:14
  162.4 22.5 %collective-permute-start.34 = (bf16[512,512]{0,1:T(8,128)(2,1)S(1)}, bf16[512,512]{0,1:T(8,128)(2,1)S(1)}, u32[]{:S(2)}, u32[]{:S(2)}) collective-permute-start(bf16[512,512]{0,1:T(8,128)(2,1)S(1)} %get-tuple-element.84), channel_id=1, source_target_pairs={{0,1},{3,2},{4,5},{7,6},{8,9},{11,10},{12,13},{15,14},{16,17},{19,... | collective-permute-start | bytes 1572872 | tf_op jit(solution)/shard_map/ppermute | solution.py:76
  165.0 31.1 %collective-permute-start.43 = (bf16[512,512]{0,1:T(8,128)(2,1)S(1)}, bf16[512,512]{0,1:T(8,128)(2,1)S(1)}, u32[]{:S(2)}, u32[]{:S(2)}) collective-permute-start(bf16[512,512]{0,1:T(8,128)(2,1)S(1)} %get-tuple-element.82), channel_id=1, source_target_pairs={{0,1},{3,2},{4,5},{7,6},{8,9},{11,10},{12,13},{15,14},{16,17},{19,... | collective-permute-start | bytes 1572872 | tf_op jit(solution)/shard_map/ppermute | solution.py:76
  167.4 36.2 %collective-permute-start.46 = (bf16[512,512]{0,1:T(8,128)(2,1)S(1)}, bf16[512,512]{0,1:T(8,128)(2,1)S(1)}, u32[]{:S(2)}, u32[]{:S(2)}) collective-permute-start(bf16[512,512]{0,1:T(8,128)(2,1)S(1)} %get-tuple-element.80), channel_id=1, source_target_pairs={{0,1},{3,2},{4,5},{7,6},{8,9},{11,10},{12,13},{15,14},{16,17},{19,... | collective-permute-start | bytes 1572872 | tf_op jit(solution)/shard_map/ppermute | solution.py:76
  173.8 30.6 %collective-permute-start.26 = (bf16[512,512]{0,1:T(8,128)(2,1)S(1)}, bf16[512,512]{0,1:T(8,128)(2,1)S(1)}, u32[]{:S(2)}, u32[]{:S(2)}) collective-permute-start(bf16[512,512]{0,1:T(8,128)(2,1)S(1)} %fusion.95), channel_id=1, source_target_pairs={{1,2},{2,1},{5,6},{6,5},{9,10},{10,9},{13,14},{14,13},{17,18},{18,... | collective-permute-start | bytes 1572872 | tf_op jit(solution)/shard_map/ppermute | solution.py:76
  185.1 20.8 %collective-permute-start.35 = (bf16[512,512]{0,1:T(8,128)(2,1)S(1)}, bf16[512,512]{0,1:T(8,128)(2,1)S(1)}, u32[]{:S(2)}, u32[]{:S(2)}) collective-permute-start(bf16[512,512]{0,1:T(8,128)(2,1)S(1)} %fusion.96), channel_id=1, source_target_pairs={{1,2},{2,1},{5,6},{6,5},{9,10},{10,9},{13,14},{14,13},{17,18},{18,... | collective-permute-start | bytes 1572872 | tf_op jit(solution)/shard_map/ppermute | solution.py:76
  204.6 18.4 %collective-permute-start.27 = (bf16[512,512]{0,1:T(8,128)(2,1)S(1)}, bf16[512,512]{0,1:T(8,128)(2,1)S(1)}, u32[]{:S(2)}, u32[]{:S(2)}) collective-permute-start(bf16[512,512]{0,1:T(8,128)(2,1)S(1)} %fusion.67), channel_id=1, source_target_pairs={{2,3},{1,0},{6,7},{5,4},{10,11},{9,8},{14,15},{13,12},{18,19},{17,... | collective-permute-start | bytes 1572872 | tf_op jit(solution)/shard_map/ppermute | solution.py:76
  206.1 28.1 %collective-permute-start.36 = (bf16[512,512]{0,1:T(8,128)(2,1)S(1)}, bf16[512,512]{0,1:T(8,128)(2,1)S(1)}, u32[]{:S(2)}, u32[]{:S(2)}) collective-permute-start(bf16[512,512]{0,1:T(8,128)(2,1)S(1)} %fusion.71), channel_id=1, source_target_pairs={{2,3},{1,0},{6,7},{5,4},{10,11},{9,8},{14,15},{13,12},{18,19},{17,... | collective-permute-start | bytes 1572872 | tf_op jit(solution)/shard_map/ppermute | solution.py:76
  207.5 37.9 %collective-permute-start.45 = (bf16[512,512]{0,1:T(8,128)(2,1)S(1)}, bf16[512,512]{0,1:T(8,128)(2,1)S(1)}, u32[]{:S(2)}, u32[]{:S(2)}) collective-permute-start(bf16[512,512]{0,1:T(8,128)(2,1)S(1)} %fusion.75), channel_id=1, source_target_pairs={{2,3},{1,0},{6,7},{5,4},{10,11},{9,8},{14,15},{13,12},{18,19},{17,... | collective-permute-start | bytes 1572872 | tf_op jit(solution)/shard_map/ppermute | solution.py:76
  209.0 43.2 %collective-permute-start.48 = (bf16[512,512]{0,1:T(8,128)(2,1)S(1)}, bf16[512,512]{0,1:T(8,128)(2,1)S(1)}, u32[]{:S(2)}, u32[]{:S(2)}) collective-permute-start(bf16[512,512]{0,1:T(8,128)(2,1)S(1)} %fusion.79), channel_id=1, source_target_pairs={{2,3},{1,0},{6,7},{5,4},{10,11},{9,8},{14,15},{13,12},{18,19},{17,... | collective-permute-start | bytes 1572872 | tf_op jit(solution)/shard_map/ppermute | solution.py:76
  (52 other events, 487.3 us)

commit v2 on v0

v2 whole, which is shorter than its diff:
```python
import functools

import jax
import jax.numpy as jnp
from jax import lax
from jax.experimental import pallas as pl
from jax.experimental.pallas import tpu as pltpu
from jax.sharding import PartitionSpec as P

HEADS = 16
KV_HEADS = 8
HD = 128
epsilon = 1e-06
bf16, f32 = jnp.bfloat16, jnp.float32
VMEM_LIMIT = 48 * 1024 * 1024


def swap_cores(x):
    return lax.ppermute(x, "rep", [(0, 1), (1, 0)])


def bits_of(n):
    return n.bit_length() - 1


def after(x, *done):
    return lax.optimization_barrier((x,) + done)[0] if done else x


def mirrored(mask, bits):
    return sum(1 << (bits - 1 - b) for b in range(bits) if mask >> b & 1)


def row_step(x, step):
    rows = lax.axis_size("row")
    last = bits_of(rows) - 1
    pairs = []
    for core in range(2):
        mask = 1 << (step if core == 0 else last - step)
        pairs += [(core * rows + i, core * rows + (i ^ mask)) for i in range(rows)]
    return lax.ppermute(x, ("rep", "row"), pairs)


def transfers(rows):
    order = [(1 << step, 0, step) for step in range(bits_of(rows))]
    for step in range(bits_of(rows)):
        order += [(held | 1 << step, held, step) for held in range(1, 1 << step)]
    return order


def tile_of(n):
    return next(t for t in (256, 128, n) if n % t == 0)


def project_kernel(n, has_acc, d_model, at_ref, *refs):
    lhs, ws, rest = refs[:n], refs[n:2 * n], refs[2 * n:]
    out_ref = rest[-1]
    x = jnp.concatenate([r[...] for r in lhs], axis=1)
    w = jnp.concatenate([r[...] for r in ws], axis=0)
    v = jnp.dot(x, w, preferred_element_type=f32)
    if has_acc:
        v = v + rest[0][...]
    if d_model is None:
        out_ref[...] = v
        return
    squares_ref, q_gain_ref, k_gain_ref = rest[-4:-1]
    v = v * lax.rsqrt(squares_ref[...] / d_model + epsilon)
    heads = v.shape[1] // HD
    for h in range(heads):
        number = at_ref[0] + pl.program_id(0) * heads + h
        one = v[:, h * HD:(h + 1) * HD]
        gain = jnp.where(number < HEADS, q_gain_ref[...], k_gain_ref[...])
        normed = one * lax.rsqrt(jnp.mean(one * one, axis=-1, keepdims=True) + epsilon) * gain
        out_ref[:, h * HD:(h + 1) * HD] = jnp.where(number < HEADS + KV_HEADS, normed, one).astype(bf16)


def project(acc, terms, first_head=None, final=None, d_model=None):
    tok, depth = terms[0][0].shape
    width = terms[0][1].shape[1]
    tn = tile_of(width)
    n = len(terms)
    tile = pl.BlockSpec((tok, tn), lambda i: (0, i))
    in_specs = [pl.BlockSpec(memory_space=pltpu.SMEM)]
    in_specs += [pl.BlockSpec((tok, depth), lambda i: (0, 0))] * n
    in_specs += [pl.BlockSpec((depth, tn), functools.partial(lambda r, i: (r, i), r)) for _, _, r in terms]
    args = [t[0] for t in terms] + [t[1] for t in terms]
    if acc is not None:
        in_specs, args = in_specs + [tile], args + [acc]
    if final is not None:
        in_specs += [pl.BlockSpec((tok, 1), lambda i: (0, 0))] + [pl.BlockSpec((1, HD), lambda i: (0, 0))] * 2
        args += list(final)
    first_head = jnp.zeros((1,), jnp.int32) if first_head is None else first_head.astype(jnp.int32).reshape(1)
    return pl.pallas_call(
        functools.partial(project_kernel, n, acc is not None, d_model),
        grid=(width // tn,),
        in_specs=in_specs,
        out_specs=tile,
        out_shape=jax.ShapeDtypeStruct((tok, width), f32 if final is None else bf16),
        compiler_params=pltpu.CompilerParams(vmem_limit_bytes=VMEM_LIMIT),
        cost_estimate=pl.CostEstimate(flops=2 * n * tok * depth * width,
                                      bytes_accessed=2 * n * depth * (width + tok) + 8 * tok * width, transcendentals=0),
    )(first_head, *args)


def per_device(residual, post_gain, w_gate, w_up, w_down, next_gain, w_qkv, q_gain, k_gain, source):
    rows, cols = lax.axis_size("row"), lax.axis_size("col")
    me, core, col = lax.axis_index("row"), lax.axis_index("rep"), lax.axis_index("col")
    tok, width = residual.shape
    d_model = width * cols
    block = d_model // rows
    half = block // 2
    bits = bits_of(rows)
    order = transfers(rows)
    direct = [o[0] for o in order if o[1] == 0]
    relayed = [o[0] for o in order if o[1] != 0]
    frames = [0] + direct + relayed

    def row_of(mask):
        return me ^ jnp.where(core == 0, mask, mirrored(mask, bits))

    barrier = lax.optimization_barrier
    even = [(i, i ^ 1) for i in range(cols)]
    odd = [(i, (i - 1 ^ 1) + 1) for i in range(1, cols - 1)]
    ff = w_gate.shape[1]
    ff_half = ff // 2
    last_mask = frames[-1]

    own = {"gate": w_gate, "up": w_up}
    gu = {(n, 0): lax.dynamic_slice_in_dim(w, core * half, half, 0) for n, w in own.items()}

    my_block = core * rows + me
    from_peer = after(source, gu["gate", 0]) // tok != my_block
    picked = source % tok + tok * from_peer.astype(jnp.int32)
    onehot = (picked[:, None] == jnp.arange(2 * tok, dtype=jnp.int32)[None, :]).astype(bf16)
    both = jnp.concatenate([residual, swap_cores(residual)], axis=0)
    placed = jnp.dot(onehot, both, preferred_element_type=f32).astype(bf16)

    by_even, by_odd = {0: placed}, {0: placed}
    left_over = cols - 1
    step = 0

    def line_step():
        nonlocal step
        if step < left_over:
            step += 1
            by_even[step] = lax.ppermute(by_odd[step - 1], "col", even)
            if step < left_over:
                by_odd[step] = lax.ppermute(by_even[step - 1], "col", odd)

    for n in own:
        for m in direct:
            gu[n, m] = row_step(gu[n, 0], bits_of(m))
        line_step()
        keys = [(n, m) for m in direct]
        ready = barrier(tuple(gu[k] for k in keys) + (by_even[step], by_odd[step], gu["up", 0]))
        for key, value in zip(keys, ready):
            gu[key] = value
        by_even[step], by_odd[step], gu["up", 0] = ready[len(keys):]
    for n in own:
        for mask, held, bit in order:
            if held:
                gu[n, mask] = row_step(gu[n, held], bit)
    while step < left_over:
        line_step()
    gu_other = {key: swap_cores(gu[key]) for key in gu if key[1]}

    arrived = [placed] + [by_even[t] for t in range(1, cols)] + [by_odd[t] for t in range(1, cols - 1)]
    place = [[0 if j == c else (abs(j - c) if (c % 2 == 1) == (j < c) else cols - 1 + abs(j - c))
              for j in range(cols)] for c in range(cols)]
    where_is = jnp.asarray(place, jnp.int32)[col]
    line = jnp.stack(arrived)
    blocks = {m: lax.dynamic_index_in_dim(line, where_is[row_of(m)], 0, False) for m in frames}

    squares = sum(jnp.sum(jnp.square(blocks[m].astype(f32)), axis=-1, keepdims=True) for m in frames)
    scale = lax.rsqrt(squares / d_model + epsilon)
    gains = post_gain.reshape(rows, block)

    def turned_halves(x):
        width = x.shape[1] // 2
        low, high = x[:, :width], x[:, width:]
        return jnp.concatenate([jnp.where(core == 0, low, high), jnp.where(core == 0, high, low)], axis=1)

    def normed(m):
        out = (blocks[m].astype(f32) * scale * lax.dynamic_index_in_dim(gains, row_of(m), 0, False)).astype(bf16)
        return out if m == 0 else turned_halves(out)

    def dot(x, w):
        return jnp.dot(x, w, preferred_element_type=f32)

    early, late = [0] + direct, relayed
    columns = [jnp.concatenate([normed(m) for m in ms], axis=1) for ms in (early, late)]

    def weights(n, masks):
        pieces = []
        for m in masks:
            pieces += [gu[n, m], gu_other[n, mirrored(m, bits)]] if m else [own[n]]
        return jnp.concatenate(pieces, axis=0)

    w_down_half = lax.dynamic_slice_in_dim(w_down, core * ff_half, ff_half, 0)
    w_qkv_half = lax.dynamic_slice_in_dim(w_qkv, core * half, half, 0)
    dn, dn_other, partial = {0: w_down_half}, {}, {}
    wq, wq_other = {0: w_qkv_half}, {}
    gate_early, up_early = (dot(columns[0], weights(n, early)) for n in own)
    keys = [(n, m) for n in own for m in relayed]
    ready = barrier(tuple(gu[k] for k in keys) + (gate_early, up_early, w_down_half))
    for key, value in zip(keys, ready):
        gu[key] = value
        gu_other[key] = swap_cores(value)
    gate_early, up_early, dn[0] = ready[len(keys):]
    for m in direct:
        dn[m] = row_step(dn[0], bits_of(m))
    gate = gate_early + dot(columns[1], weights("gate", late))
    up_proj = up_early + dot(columns[1], weights("up", late))
    hidden = (gate / (1 + jnp.exp(-gate)) * up_proj).astype(bf16)
    partial[0] = dot(hidden, w_down)
    turned = turned_halves(hidden)
    first_sent = partial[0].astype(bf16)

    def down_product(m):
        return dot(turned, jnp.concatenate([dn[m], dn_other[mirrored(m, bits)]], axis=0))

    from_low = col % 2 == 1
    place_even = jnp.where(from_low, cols - 1 - col, col)
    place_odd = jnp.where(from_low, col, cols - 1 - col)
    by_even, by_odd = {}, {}

    def placed_at(t, place, places):
        value = None
        for c in places:
            if 0 <= t - c < rows:
                value = partial[t - c] if value is None else jnp.where(place == c, partial[t - c], value)
        return value

    def bases(t):
        return [placed_at(t, place_even, range(0, cols - 1, 2)), placed_at(t, place_odd, range(1, cols - 1, 2))]

    def terms(k):
        found = {}
        for c in range(cols):
            if c > 0:
                found.setdefault((c % 2, k + c - 1), []).append(c)
            if c < cols - 1:
                found.setdefault(((c + 1) % 2, k + cols - 2 - c), []).append(c)
        return found

    def summed(k):
        total = partial[k]
        for (is_even, t), where in terms(k).items():
            came = (by_even if is_even else by_odd)[t].astype(f32)
            counts = functools.reduce(jnp.logical_or, [col == c for c in where])
            total = total + jnp.where(counts, came, 0)
        return total

    next_gains = next_gain.reshape(rows, 1, block)
    squares, fresh, scaled = {}, {}, {}

    def finish(k):
        m = frames[k]
        fresh[k] = (blocks[m].astype(f32) + summed(k)).astype(bf16)
        v = fresh[k].astype(f32)
        squares[k] = jnp.sum(v * v, axis=-1, keepdims=True)
        out = (v * lax.dynamic_index_in_dim(next_gains, row_of(m), 0, False)).astype(bf16)
        scaled[k] = out if m == 0 else turned_halves(out)

    def terms_of(k):
        m = frames[k]
        low, high = scaled[k][:, :half], scaled[k][:, half:]
        if m == 0:
            return [(low, w_qkv, 0), (high, w_qkv, 1)]
        return [(low, wq[m], 0), (high, wq_other[mirrored(m, bits)], 0)]

    place_of = {m: k for k, m in enumerate(frames)}
    steps = rows + cols - 2
    ready = barrier(tuple(dn[m] for m in direct) + (first_sent,))
    for m, value in zip(direct, ready):
        dn[m] = value
        dn_other[m] = swap_cores(value)
    first_sent = ready[-1]
    for mask, held, bit in order:
        if held:
            dn[mask] = row_step(dn[held], bit)
    acc, last_step = None, ()

    def tie(store, masks, values):
        for m, value in zip(masks, values):
            store[m] = value

    for t in range(steps):
        base = bases(t)
        sends = []
        for i, came in enumerate((by_odd.get(t - 1), by_even.get(t - 1))):
            if base[i] is not None:
                send = base[i] if came is None else base[i] + came.astype(f32)
                sends.append((i, first_sent if t == 0 else send.astype(bf16)))
        held_now = {0: [(dn_other, direct)], 1: [(dn, relayed), (partial, [place_of[m] for m in direct])],
                    2: [(dn_other, relayed), (wq, direct)],
                    3: [(wq, relayed), (wq_other, direct), (partial, [place_of[m] for m in relayed])],
                    4: [(wq_other, relayed)]}.get(t, [])
        flat = [store[m] for store, masks in held_now for m in masks]
        extra = [acc] if t == steps - 1 else []
        ready = barrier(tuple(v for _, v in sends) + tuple(flat) + tuple(last_step) + tuple(extra))
        for (i, _), send in zip(sends, ready):
            (by_even, by_odd)[i][t] = lax.ppermute(send, "col", (even, odd)[i])
        at = len(sends)
        for store, masks in held_now:
            tie(store, masks, ready[at:at + len(masks)])
            at += len(masks)
        if extra:
            acc = ready[-1]
        last_step = [(by_even, by_odd)[i][t] for i, _ in sends]
        if t == 0:
            for m in direct:
                partial[place_of[m]] = down_product(m)
        elif t == 1:
            for m in relayed:
                dn_other[m] = swap_cores(dn[m])
            for m in direct:
                wq[m] = row_step(wq[0], bits_of(m))
        elif t == 2:
            for m in relayed:
                partial[place_of[m]] = down_product(m)
            for m in direct:
                wq_other[m] = swap_cores(wq[m])
            for mask, held, bit in order:
                if held:
                    wq[mask] = row_step(wq[held], bit)
        elif t == 3:
            for m in relayed:
                wq_other[m] = swap_cores(wq[m])
        k = t - (cols - 2)
        if k >= 0:
            finish(k)
        if k == rows - 3:
            acc = project(None, [x for j in range(rows - 2) for x in terms_of(j)])
    acc = project(acc, terms_of(rows - 2))

    moved_residual = fresh[0]
    for k in range(1, rows):
        moved_residual = jnp.where(row_of(frames[k]) == col, fresh[k], moved_residual)
    moved_qkv = project(acc, terms_of(rows - 1), (w_qkv.shape[1] // HD) * col,
                        (sum(squares.values()), q_gain.reshape(1, HD), k_gain.reshape(1, HD)), d_model)
    return (moved_residual, moved_qkv)


def solution(mesh):
    return jax.shard_map(
        per_device,
        mesh=mesh,
        in_specs=(
            P(("rep", "row"), "col"),
            P(),
            P("row", "col"),
            P("row", "col"),
            P("col", "row"),
            P(),
            P("row", "col"),
            P(),
            P(),
            P(("rep", "row")),
        ),
        out_specs=(P(("rep", "row"), "col"), P(("rep", "row"), "col")),
        check_vma=False,
    )
```

time: 495 us -> 214 us (0.43)
  waiting for transfers between devices: 432 us -> 83.2 us
  starting transfers between devices: 0.96 us -> 45.2 us
  local copies, waits for them, and re-layouts: 6.71 us -> 29.7 us
  matrix products: 28.1 us -> 17.5 us
  other arithmetic: 12.6 us -> 21 us
  Pallas kernels: 0 us -> 6.83 us
  between operations: 14.3 us -> 9.22 us
    all_gather x6 -> x0, waiting for transfers between devices: 349 us -> none  [the longest x1 71.7 us: per_device(): lax.all_gather(w_down, 'row', axis=1, tiled=True)]
    ppermute x2 -> x40, waiting for transfers between devices: 2.5 us -> 83.2 us  [the longest x10 52.7 us: per_device(): (by_even, by_odd)[i][t] = lax.ppermute(send, 'col', (even, odd)[i])]
    reduce_scatter x1 -> x0, waiting for transfers between devices: 76.9 us -> none  [per_device(): lax.psum_scatter(partial_value, 'col', scatter_dimension=1, tiled=True)]
    ppermute x2 -> x40, starting transfers between devices: 0.51 us -> 45.2 us  [the longest x10 17 us: per_device(): (by_even, by_odd)[i][t] = lax.ppermute(send, 'col', (even, odd)[i])]
    unnamed x21 -> x98, local copies, waits for them, and re-layouts: 1.78 us -> 22.7 us
    dot_general x3 -> x9, matrix products: 28.1 us -> 17.5 us  [the longest x8 14.8 us: dot(): return jnp.dot(x, w, preferred_element_type=f32)]
    pallas_call x0 -> x3, Pallas kernels: none -> 6.83 us  [project(): pl.pallas_call(functools.partial(project_kernel, n, acc is not None, d_mo...]
    convert_element_type x2 -> x12, other arithmetic: 3.93 us -> 10.5 us  [the longest x7 7.99 us: per_device(): sends.append((i, first_sent if t == 0 else send.astype(bf16)))]
  transfers between devices with their start and end apart: 9 -> 40, of which waited for: 8 -> 14; matrix products, arithmetic and copies ran while one was open for 3% -> 27% of each run, Pallas kernels for 0% -> 2%
where the time goes in v2:
time: 214 us; the launch traced here: 213 us
  waiting for transfers between devices  83.2 us (39%)
  starting transfers between devices  45.2 us (21%)
  local copies, waits for them, and re-layouts  29.7 us (14%)
  other arithmetic  21 us (10%)
  matrix products  17.5 us (8%)
  between operations  9.22 us (4%)
  Pallas kernels  6.83 us (3%)
    ppermute x10, waiting for transfers between devices, per_device(): (by_even, by_odd)[i][t] = lax.ppermute(send, 'col', (even, odd)[i])  52.7 us
    unnamed x98, local copies, waits for them, and re-layouts  22.7 us
    ppermute x12, waiting for transfers between devices, row_step(): return lax.ppermute(x, ('rep', 'row'), pairs)  22.7 us
    ppermute x10, starting transfers between devices, per_device(): (by_even, by_odd)[i][t] = lax.ppermute(send, 'col', (even, odd)[i])  17 us
    ppermute x12, starting transfers between devices, row_step(): return lax.ppermute(x, ('rep', 'row'), pairs)  16.4 us
    dot_general x8, matrix products, dot(): return jnp.dot(x, w, preferred_element_type=f32)  14.8 us
    convert_element_type x7, other arithmetic, per_device(): sends.append((i, first_sent if t == 0 else send.astype(bf16)))  7.99 us
    pallas_call x3, Pallas kernels, project(): pl.pallas_call(functools.partial(project_kernel, n, acc is not None, d_mo...  6.83 us
  transfers between devices with their start and end apart: 40, of which 14 were waited for; matrix products, arithmetic and copies ran while one was open for 27% of the time, Pallas kernels for 2%

profile of v2, /device:TPU:0, one launch (start us, length us, event | category | flops | bytes accessed | tf_op | source)
XLA Modules:
  0.0 212.7 jit_solution(9197012418323568098)
XLA Ops:
  1.2 2.2 %constant_dynamic-slice_fusion.11 = bf16[256,1536]{1,0:T(8,128)(2,1)} fusion(bf16[512,1536]{1,0:T(8,128)(2,1)} %param.13, s32[]{:T(128)S(6)} %select_n.249), kind=kLoop, calls=%fused_computation.153 | loop fusion | bytes 1572868 | tf_op jit(solution)/shard_map/dynamic_slice | solution.py:129
  3.4 2.6 %collective-permute-start.1 = (bf16[256,1536]{1,0:T(8,128)(2,1)}, bf16[256,1536]{1,0:T(8,128)(2,1)}, u32[]{:S(2)}, u32[]{:S(2)}) collective-permute-start(bf16[256,1536]{1,0:T(8,128)(2,1)} %constant_dynamic-slice_fusion.11), channel_id=1, source_target_pairs={{0,4},{4,0},{8,12},{12,8},{16,24},{20,28},{24,16},{28,20},{1,5},{5... | collective-permute-start | bytes 2359304 | tf_op jit(solution)/shard_map/ppermute | solution.py:41
  8.1 2.7 %bitcast_dynamic-update-slice_fusion.5 = (bf16[6,512,512]{2,1,0:T(8,128)(2,1)}, bf16[512,512]{1,0:T(8,128)(2,1)S(1)}) fusion(bf16[512,512]{1,0:T(8,128)(2,1)} %collective-permute-done, bf16[512,512]{1,0:T(8,128)(2,1)} %param.11, s32[512]{0:T(512)S(1)} %fusion.70), kind=kOutput, calls=%fused_computation.118 | convolution fusion | flops 539754496 | bytes 2099200 | tf_op jit(solution)/shard_map/dot_general | solution.py:136
  16.1 7.5 %collective-permute-done.1 = bf16[256,1536]{1,0:T(8,128)(2,1)} collective-permute-done((bf16[256,1536]{1,0:T(8,128)(2,1)}, bf16[256,1536]{1,0:T(8,128)(2,1)}, u32[]{:S(2)}, u32[]{:S(2)}) %collective-permute-start.1) | collective-permute-done | bytes 786464 | tf_op jit(solution)/shard_map/ppermute | solution.py:41
  43.5 2.2 %constant_dynamic-update-slice_fusion.3 = bf16[1536,1536]{1,0:T(8,128)(2,1)} fusion(bf16[1536,1536]{1,0:T(8,128)(2,1)} %constant_dynamic-update-slice_fusion.4, bf16[256,1536]{1,0:T(8,128)(2,1)} %collective-permute-done.1), kind=kLoop, calls=%fused_computation.135 | loop fusion | bytes 1572864
  49.9 2.9 %collective-permute-start.9 = (bf16[512,512]{1,0:T(8,128)(2,1)}, bf16[512,512]{1,0:T(8,128)(2,1)S(1)}, u32[]{:S(2)}, u32[]{:S(2)}) collective-permute-start(bf16[512,512]{1,0:T(8,128)(2,1)} %collective-permute-done.8), channel_id=1, source_target_pairs={{0,1},{1,0},{2,3},{3,2},{4,5},{5,4},{6,7},{7,6},{8,9},{9,8},{10,11... | collective-permute-start | bytes 1572872 | tf_op jit(solution)/shard_map/ppermute | solution.py:146
  52.8 2.1 constant_dynamic-update-slice_fusion.2
  59.1 5.8 %collective-permute-done.9 = bf16[512,512]{1,0:T(8,128)(2,1)S(1)} collective-permute-done((bf16[512,512]{1,0:T(8,128)(2,1)}, bf16[512,512]{1,0:T(8,128)(2,1)S(1)}, u32[]{:S(2)}, u32[]{:S(2)}) %collective-permute-start.9) | collective-permute-done | bytes 524320 | tf_op jit(solution)/shard_map/ppermute | solution.py:146
  70.6 2.6 %fusion.88 = f32[512,1536]{1,0:T(8,128)S(1)} fusion(bf16[512,1536]{1,0:T(8,128)(2,1)S(1)} %select_dynamic-update-slice_fusion, bf16[1536,1536]{1,0:T(8,128)(2,1)S(1)} %copy-done.36), kind=kOutput, calls=%fused_computation.179 | convolution fusion | flops 2415919104 | bytes 9437184 | tf_op jit(solution)/shard_map/dot_general | solution.py:188
  74.5 2.6 %fusion.89 = f32[512,1536]{1,0:T(8,128)S(1)} fusion(bf16[512,1536]{1,0:T(8,128)(2,1)S(1)} %select_dynamic-update-slice_fusion, bf16[1536,1536]{1,0:T(8,128)(2,1)S(1)} %constant_dynamic-update-slice_fusion.5), kind=kOutput, calls=%fused_computation.180 | convolution fusion | flops 2415919104 | bytes 9437184 | tf_op jit(solution)/shard_map/dot_general | solution.py:188
  84.8 13.1 %collective-permute-done.18 = bf16[768,512]{1,0:T(8,128)(2,1)S(1)} collective-permute-done((bf16[768,512]{1,0:T(8,128)(2,1)S(1)}, bf16[768,512]{1,0:T(8,128)(2,1)S(1)}, u32[]{:S(2)}, u32[]{:S(2)}) %collective-permute-start.18) | collective-permute-done | bytes 786464 | tf_op jit(solution)/shard_map/ppermute | solution.py:41
  105.2 2.1 fusion.87
  107.3 8.0 %collective-permute-done.22 = bf16[512,512]{1,0:T(8,128)(2,1)S(1)} collective-permute-done((bf16[512,512]{1,0:T(8,128)(2,1)S(1)}, bf16[512,512]{1,0:T(8,128)(2,1)S(1)}, u32[]{:S(2)}, u32[]{:S(2)}) %collective-permute-start.22) | collective-permute-done | bytes 524320 | tf_op jit(solution)/shard_map/ppermute | solution.py:303
  121.6 8.0 %collective-permute-done.25 = bf16[512,512]{1,0:T(8,128)(2,1)S(1)} collective-permute-done((bf16[512,512]{1,0:T(8,128)(2,1)}, bf16[512,512]{1,0:T(8,128)(2,1)S(1)}, u32[]{:S(2)}, u32[]{:S(2)}) %collective-permute-start.25) | collective-permute-done | bytes 524320 | tf_op jit(solution)/shard_map/ppermute | solution.py:303
  134.4 2.5 %collective-permute-start.30 = (bf16[512,512]{1,0:T(8,128)(2,1)S(1)}, bf16[512,512]{1,0:T(8,128)(2,1)S(1)}, u32[]{:S(2)}, u32[]{:S(2)}) collective-permute-start(bf16[512,512]{1,0:T(8,128)(2,1)S(1)} %fusion.25), channel_id=1, source_target_pairs={{0,1},{1,0},{2,3},{3,2},{4,5},{5,4},{6,7},{7,6},{8,9},{9,8},{10,11... | collective-permute-start | bytes 1572872 | tf_op jit(solution)/shard_map/ppermute | solution.py:303
  139.1 10.0 %collective-permute-done.30 = bf16[512,512]{1,0:T(8,128)(2,1)S(1)} collective-permute-done((bf16[512,512]{1,0:T(8,128)(2,1)S(1)}, bf16[512,512]{1,0:T(8,128)(2,1)S(1)}, u32[]{:S(2)}, u32[]{:S(2)}) %collective-permute-start.30) | collective-permute-done | bytes 524320 | tf_op jit(solution)/shard_map/ppermute | solution.py:303
  150.8 2.6 %fusion.29 = (bf16[512,512]{1,0:T(8,128)(2,1)S(1)}, f32[512,512]{1,0:T(8,128)S(1)}) fusion(bf16[512,512]{1,0:T(8,128)(2,1)S(1)} %collective-permute-done.29, f32[512,512]{1,0:T(8,128)S(1)} %copy-done.23, pred[]{:T(512)S(6)} %eq.35, bf16[768,512]{1,0:T(8,128)(2,1)} %collective-permute-done.26, bf16[768,512]{1,0:T(8,128)(2,1)} %collective-permute-done.23, ...), kind=kOutput, calls=%fused_computation.70 | convolution fusion | flops 812646400 | bytes 6291457 | tf_op jit(solution)/shard_map/dot_general | solution.py:188
  154.2 4.3 %collective-permute-start.35 = (bf16[512,512]{1,0:T(8,128)(2,1)S(1)}, bf16[512,512]{1,0:T(8,128)(2,1)S(1)}, u32[]{:S(2)}, u32[]{:S(2)}) collective-permute-start(bf16[512,512]{1,0:T(8,128)(2,1)S(1)} %get-tuple-element.77), channel_id=1, source_target_pairs={{0,1},{1,0},{2,3},{3,2},{4,5},{5,4},{6,7},{7,6},{8,9},{9,8},{10,11... | collective-permute-start | bytes 1572872 | tf_op jit(solution)/shard_map/ppermute | solution.py:303
  159.5 10.1 %collective-permute-done.35 = bf16[512,512]{1,0:T(8,128)(2,1)S(1)} collective-permute-done((bf16[512,512]{1,0:T(8,128)(2,1)S(1)}, bf16[512,512]{1,0:T(8,128)(2,1)S(1)}, u32[]{:S(2)}, u32[]{:S(2)}) %collective-permute-start.35) | collective-permute-done | bytes 524320 | tf_op jit(solution)/shard_map/ppermute | solution.py:303
  173.2 10.1 %collective-permute-done.38 = bf16[512,512]{1,0:T(8,128)(2,1)} collective-permute-done((bf16[512,512]{1,0:T(8,128)(2,1)}, bf16[512,512]{1,0:T(8,128)(2,1)}, u32[]{:S(2)}, u32[]{:S(2)}) %collective-permute-start.38) | collective-permute-done | bytes 524320 | tf_op jit(solution)/shard_map/ppermute | solution.py:303
  183.3 5.0 %fusion.41 = (f32[512]{0:T(512)S(1)}, bf16[512,512]{1,0:T(8,128)(2,1)S(1)}, f32[512]{0:T(512)S(1)}, bf16[512,512]{1,0:T(8,128)(2,1)S(1)}, f32[512]{0:T(512)S(1)}, /*index=5*/bf16[512,512]{1,0:T(8,128)(2,1)S(1)}) fusion(bf16[512,512]{1,0:T(8,128)(2,1)} %copy-done.30, bf16[512,512]{1,0:T(8,128)(2,1)} %copy-done.29, pred[]{:T(512)S(6)} %or.5, ...), kind=kLoop, calls=%fused_computation.82 | loop fusion | flops 11532800 | bytes 10491918 | tf_op jit(solution)/shard_map/reduce_sum | solution.py:261
  189.7 2.2 %shard_map.122.refs_4_ = f32[512,1024]{1,0:T(8,128)S(1)} custom-call(s32[1]{0:T(128)} %constant.155.clone.1.at_ref, bf16[512,256]{1,0:T(8,128)(2,1)S(1)} %get-tuple-element.114.refs_0_, bf16[512,256]{1,0:T(8,128)(2,1)S(1)} %get-tuple-element.113.refs_1_, bf16[512,256]{1,0:T(8,128)(2,1)S(1)} %get-tuple-element.112.refs_2_, ...), custom_call_target="tpu_custom_call" | custom-call | flops 1073741824 | bytes 7340032 | tf_op jit(solution)/shard_map/pallas_call | solution.py:93
  197.1 6.5 %collective-permute-done.39 = bf16[512,512]{1,0:T(8,128)(2,1)S(1)} collective-permute-done((bf16[512,512]{1,0:T(8,128)(2,1)S(1)}, bf16[512,512]{1,0:T(8,128)(2,1)S(1)}, u32[]{:S(2)}, u32[]{:S(2)}) %collective-permute-start.39) | collective-permute-done | bytes 524320 | tf_op jit(solution)/shard_map/ppermute | solution.py:303
  209.8 2.9 %shard_map.124 = bf16[512,1024]{1,0:T(8,128)(2,1)} custom-call(s32[1]{0:T(128)} %bitcast.25.at_ref, bf16[512,256]{1,0:T(8,128)(2,1)S(1)} %get-tuple-element.110.refs_0_, bf16[512,256]{1,0:T(8,128)(2,1)S(1)} %get-tuple-element.109.refs_1_, bf16[256,1024]{1,0:T(8,128)(2,1)S(1)} %collective-permute-done.31.refs_2_, ...), custom_call_target="tpu_custom_call" | custom-call | flops 536870912 | bytes 5767168 | tf_op jit(solution)/shard_map/pallas_call | solution.py:93
  (209 shorter events, 82.8 us)
Async XLA Ops:
  3.4 20.3 %collective-permute-start.1 = (bf16[256,1536]{1,0:T(8,128)(2,1)}, bf16[256,1536]{1,0:T(8,128)(2,1)}, u32[]{:S(2)}, u32[]{:S(2)}) collective-permute-start(bf16[256,1536]{1,0:T(8,128)(2,1)} %constant_dynamic-slice_fusion.11), channel_id=1, source_target_pairs={{0,4},{4,0},{8,12},{12,8},{16,24},{20,28},{24,16},{28,20},{1,5},{5... | collective-permute-start | bytes 2359304 | tf_op jit(solution)/shard_map/ppermute | solution.py:41
  5.9 18.4 %collective-permute-start.2 = (bf16[256,1536]{1,0:T(8,128)(2,1)}, bf16[256,1536]{1,0:T(8,128)(2,1)}, u32[]{:S(2)}, u32[]{:S(2)}) collective-permute-start(bf16[256,1536]{1,0:T(8,128)(2,1)} %constant_dynamic-slice_fusion.11), channel_id=1, source_target_pairs={{0,8},{4,12},{8,0},{12,4},{16,20},{20,16},{24,28},{28,24},{1,9},{5... | collective-permute-start | bytes 2359304 | tf_op jit(solution)/shard_map/ppermute | solution.py:41
  25.3 22.4 %collective-permute-start.5 = (bf16[256,1536]{1,0:T(8,128)(2,1)}, bf16[256,1536]{1,0:T(8,128)(2,1)S(1)}, u32[]{:S(2)}, u32[]{:S(2)}) collective-permute-start(bf16[256,1536]{1,0:T(8,128)(2,1)} %constant_dynamic-slice_fusion.10), channel_id=1, source_target_pairs={{0,4},{4,0},{8,12},{12,8},{16,24},{20,28},{24,16},{28,20},{1,5},{5... | collective-permute-start | bytes 2359304 | tf_op jit(solution)/shard_map/ppermute | solution.py:41
  26.9 20.8 %collective-permute-start.6 = (bf16[256,1536]{1,0:T(8,128)(2,1)}, bf16[256,1536]{1,0:T(8,128)(2,1)}, u32[]{:S(2)}, u32[]{:S(2)}) collective-permute-start(bf16[256,1536]{1,0:T(8,128)(2,1)} %constant_dynamic-slice_fusion.10), channel_id=1, source_target_pairs={{0,8},{4,12},{8,0},{12,4},{16,20},{20,16},{24,28},{28,24},{1,9},{5... | collective-permute-start | bytes 2359304 | tf_op jit(solution)/shard_map/ppermute | solution.py:41
  29.9 15.8 %collective-permute-start.7 = (bf16[512,512]{1,0:T(8,128)(2,1)}, bf16[512,512]{1,0:T(8,128)(2,1)}, u32[]{:S(2)}, u32[]{:S(2)}) collective-permute-start(bf16[512,512]{1,0:T(8,128)(2,1)} %collective-permute-done.4), channel_id=1, source_target_pairs={{0,1},{1,0},{2,3},{3,2},{4,5},{5,4},{6,7},{7,6},{8,9},{9,8},{10,11... | collective-permute-start | bytes 1572872 | tf_op jit(solution)/shard_map/ppermute | solution.py:146
  31.6 14.6 %collective-permute-start.8 = (bf16[512,512]{1,0:T(8,128)(2,1)}, bf16[512,512]{1,0:T(8,128)(2,1)}, u32[]{:S(2)}, u32[]{:S(2)}) collective-permute-start(bf16[512,512]{1,0:T(8,128)(2,1)} %copy-done.37), channel_id=1, source_target_pairs={{1,2},{2,1},{5,6},{6,5},{9,10},{10,9},{13,14},{14,13},{17,18},{18,... | collective-permute-start | bytes 1572872 | tf_op jit(solution)/shard_map/ppermute | solution.py:148
  33.1 16.8 %collective-permute-start.12 = (bf16[256,1536]{1,0:T(8,128)(2,1)}, bf16[256,1536]{1,0:T(8,128)(2,1)}, u32[]{:S(2)}, u32[]{:S(2)}) collective-permute-start(bf16[256,1536]{1,0:T(8,128)(2,1)} %collective-permute-done.2), channel_id=1, source_target_pairs={{0,16},{16,0},{1,17},{17,1},{2,18},{18,2},{3,19},{19,3},{4,20},{20... | collective-permute-start | bytes 2359304 | tf_op jit(solution)/shard_map/ppermute | solution.py:19
  46.2 30.9 %collective-permute-start.10 = (bf16[256,1536]{1,0:T(8,128)(2,1)}, bf16[256,1536]{1,0:T(8,128)(2,1)S(1)}, u32[]{:S(2)}, u32[]{:S(2)}) collective-permute-start(bf16[256,1536]{1,0:T(8,128)(2,1)} %collective-permute-done.1), channel_id=1, source_target_pairs={{0,8},{4,12},{8,0},{12,4},{16,20},{20,16},{24,28},{28,24},{1,9},{5... | collective-permute-start | bytes 2359304 | tf_op jit(solution)/shard_map/ppermute | solution.py:41
  47.7 26.7 %collective-permute-start.15 = (bf16[256,1536]{1,0:T(8,128)(2,1)S(1)}, bf16[256,1536]{1,0:T(8,128)(2,1)S(1)}, u32[]{:S(2)}, u32[]{:S(2)}) collective-permute-start(bf16[256,1536]{1,0:T(8,128)(2,1)S(1)} %collective-permute-done.5), channel_id=1, source_target_pairs={{0,16},{16,0},{1,17},{17,1},{2,18},{18,2},{3,19},{19,3},{4,20},{20... | collective-permute-start | bytes 2359304 | tf_op jit(solution)/shard_map/ppermute | solution.py:19
  47.7 29.4 %collective-permute-start.11 = (bf16[256,1536]{1,0:T(8,128)(2,1)S(1)}, bf16[256,1536]{1,0:T(8,128)(2,1)S(1)}, u32[]{:S(2)}, u32[]{:S(2)}) collective-permute-start(bf16[256,1536]{1,0:T(8,128)(2,1)S(1)} %collective-permute-done.5), channel_id=1, source_target_pairs={{0,8},{4,12},{8,0},{12,4},{16,20},{20,16},{24,28},{28,24},{1,9},{5... | collective-permute-start | bytes 2359304 | tf_op jit(solution)/shard_map/ppermute | solution.py:41
  49.9 15.0 %collective-permute-start.9 = (bf16[512,512]{1,0:T(8,128)(2,1)}, bf16[512,512]{1,0:T(8,128)(2,1)S(1)}, u32[]{:S(2)}, u32[]{:S(2)}) collective-permute-start(bf16[512,512]{1,0:T(8,128)(2,1)} %collective-permute-done.8), channel_id=1, source_target_pairs={{0,1},{1,0},{2,3},{3,2},{4,5},{5,4},{6,7},{7,6},{8,9},{9,8},{10,11... | collective-permute-start | bytes 1572872 | tf_op jit(solution)/shard_map/ppermute | solution.py:146
  58.1 15.1 %collective-permute-start.14 = (bf16[256,1536]{1,0:T(8,128)(2,1)}, bf16[256,1536]{1,0:T(8,128)(2,1)S(1)}, u32[]{:S(2)}, u32[]{:S(2)}) collective-permute-start(bf16[256,1536]{1,0:T(8,128)(2,1)} %collective-permute-done.6), channel_id=1, source_target_pairs={{0,16},{16,0},{1,17},{17,1},{2,18},{18,2},{3,19},{19,3},{4,20},{20... | collective-permute-start | bytes 2359304 | tf_op jit(solution)/shard_map/ppermute | solution.py:19
  77.8 20.2 %collective-permute-start.18 = (bf16[768,512]{1,0:T(8,128)(2,1)S(1)}, bf16[768,512]{1,0:T(8,128)(2,1)S(1)}, u32[]{:S(2)}, u32[]{:S(2)}) collective-permute-start(bf16[768,512]{1,0:T(8,128)(2,1)S(1)} %constant_dynamic-slice_fusion.6), channel_id=1, source_target_pairs={{0,4},{4,0},{8,12},{12,8},{16,24},{20,28},{24,16},{28,20},{1,5},{5... | collective-permute-start | bytes 2359304 | tf_op jit(solution)/shard_map/ppermute | solution.py:41
  78.6 19.4 %collective-permute-start.19 = (bf16[768,512]{1,0:T(8,128)(2,1)S(1)}, bf16[768,512]{1,0:T(8,128)(2,1)S(1)}, u32[]{:S(2)}, u32[]{:S(2)}) collective-permute-start(bf16[768,512]{1,0:T(8,128)(2,1)S(1)} %constant_dynamic-slice_fusion.6), channel_id=1, source_target_pairs={{0,8},{4,12},{8,0},{12,4},{16,20},{20,16},{24,28},{28,24},{1,9},{5... | collective-permute-start | bytes 2359304 | tf_op jit(solution)/shard_map/ppermute | solution.py:41
  98.5 17.9 %collective-permute-start.23 = (bf16[768,512]{1,0:T(8,128)(2,1)S(1)}, bf16[768,512]{1,0:T(8,128)(2,1)}, u32[]{:S(2)}, u32[]{:S(2)}) collective-permute-start(bf16[768,512]{1,0:T(8,128)(2,1)S(1)} %collective-permute-done.18), channel_id=1, source_target_pairs={{0,8},{4,12},{8,0},{12,4},{16,20},{20,16},{24,28},{28,24},{1,9},{5... | collective-permute-start | bytes 2359304 | tf_op jit(solution)/shard_map/ppermute | solution.py:41
  101.4 14.0 %collective-permute-start.22 = (bf16[512,512]{1,0:T(8,128)(2,1)S(1)}, bf16[512,512]{1,0:T(8,128)(2,1)S(1)}, u32[]{:S(2)}, u32[]{:S(2)}) collective-permute-start(bf16[512,512]{1,0:T(8,128)(2,1)S(1)} %get-tuple-element.63), channel_id=1, source_target_pairs={{0,1},{1,0},{2,3},{3,2},{4,5},{5,4},{6,7},{7,6},{8,9},{9,8},{10,11... | collective-permute-start | bytes 1572872 | tf_op jit(solution)/shard_map/ppermute | solution.py:303
  118.8 15.7 %collective-permute-start.26 = (bf16[768,512]{1,0:T(8,128)(2,1)}, bf16[768,512]{1,0:T(8,128)(2,1)}, u32[]{:S(2)}, u32[]{:S(2)}) collective-permute-start(bf16[768,512]{1,0:T(8,128)(2,1)} %collective-permute-done.23), channel_id=1, source_target_pairs={{0,16},{16,0},{1,17},{17,1},{2,18},{18,2},{3,19},{19,3},{4,20},{20... | collective-permute-start | bytes 2359304 | tf_op jit(solution)/shard_map/ppermute | solution.py:19
  119.7 14.7 %collective-permute-start.27 = (bf16[256,1024]{1,0:T(8,128)(2,1)}, bf16[256,1024]{1,0:T(8,128)(2,1)S(1)}, u32[]{:S(2)}, u32[]{:S(2)}) collective-permute-start(bf16[256,1024]{1,0:T(8,128)(2,1)} %constant_dynamic-slice_fusion.4), channel_id=1, source_target_pairs={{0,4},{4,0},{8,12},{12,8},{16,24},{20,28},{24,16},{28,20},{1,5},{5... | collective-permute-start | bytes 1572872 | tf_op jit(solution)/shard_map/ppermute | solution.py:41
  134.4 14.7 %collective-permute-start.30 = (bf16[512,512]{1,0:T(8,128)(2,1)S(1)}, bf16[512,512]{1,0:T(8,128)(2,1)S(1)}, u32[]{:S(2)}, u32[]{:S(2)}) collective-permute-start(bf16[512,512]{1,0:T(8,128)(2,1)S(1)} %fusion.25), channel_id=1, source_target_pairs={{0,1},{1,0},{2,3},{3,2},{4,5},{5,4},{6,7},{7,6},{8,9},{9,8},{10,11... | collective-permute-start | bytes 1572872 | tf_op jit(solution)/shard_map/ppermute | solution.py:303
  137.8 15.6 %collective-permute-start.31 = (bf16[256,1024]{1,0:T(8,128)(2,1)S(1)}, bf16[256,1024]{1,0:T(8,128)(2,1)S(1)}, u32[]{:S(2)}, u32[]{:S(2)}) collective-permute-start(bf16[256,1024]{1,0:T(8,128)(2,1)S(1)} %collective-permute-done.27.refs_6_), channel_id=1, source_target_pairs={{0,8},{4,12},{8,0},{12,4},{16,20},{20,16},{24,28},{28,24},{1,9},{5... | collective-permute-start | bytes 1572872 | tf_op jit(solution)/shard_map/ppermute | solution.py:41
  138.6 14.8 %collective-permute-start.32 = (bf16[256,1024]{1,0:T(8,128)(2,1)S(1)}, bf16[256,1024]{1,0:T(8,128)(2,1)S(1)}, u32[]{:S(2)}, u32[]{:S(2)}) collective-permute-start(bf16[256,1024]{1,0:T(8,128)(2,1)S(1)} %collective-permute-done.27.refs_6_), channel_id=1, source_target_pairs={{0,16},{16,0},{1,17},{17,1},{2,18},{18,2},{3,19},{19,3},{4,20},{20... | collective-permute-start | bytes 1572872 | tf_op jit(solution)/shard_map/ppermute | solution.py:19
  138.6 14.8 %collective-permute-start.33 = (bf16[256,1024]{1,0:T(8,128)(2,1)S(1)}, bf16[256,1024]{1,0:T(8,128)(2,1)S(1)}, u32[]{:S(2)}, u32[]{:S(2)}) collective-permute-start(bf16[256,1024]{1,0:T(8,128)(2,1)S(1)} %collective-permute-done.28.refs_2_), channel_id=1, source_target_pairs={{0,16},{16,0},{1,17},{17,1},{2,18},{18,2},{3,19},{19,3},{4,20},{20... | collective-permute-start | bytes 1572872 | tf_op jit(solution)/shard_map/ppermute | solution.py:19
  154.2 15.4 %collective-permute-start.35 = (bf16[512,512]{1,0:T(8,128)(2,1)S(1)}, bf16[512,512]{1,0:T(8,128)(2,1)S(1)}, u32[]{:S(2)}, u32[]{:S(2)}) collective-permute-start(bf16[512,512]{1,0:T(8,128)(2,1)S(1)} %get-tuple-element.77), channel_id=1, source_target_pairs={{0,1},{1,0},{2,3},{3,2},{4,5},{5,4},{6,7},{7,6},{8,9},{9,8},{10,11... | collective-permute-start | bytes 1572872 | tf_op jit(solution)/shard_map/ppermute | solution.py:303
  172.5 19.4 %collective-permute-start.37 = (bf16[512,512]{1,0:T(8,128)(2,1)}, bf16[512,512]{1,0:T(8,128)(2,1)S(1)}, u32[]{:S(2)}, u32[]{:S(2)}) collective-permute-start(bf16[512,512]{1,0:T(8,128)(2,1)} %fusion.45), channel_id=1, source_target_pairs={{1,2},{2,1},{5,6},{6,5},{9,10},{10,9},{13,14},{14,13},{17,18},{18,... | collective-permute-start | bytes 1572872 | tf_op jit(solution)/shard_map/ppermute | solution.py:303
  (59 other events, 547.0 us)

commit v3 on v2

--- a/solution.py
+++ b/solution.py
@@ -54,16 +54,16 @@
 
 def project_kernel(n, has_acc, d_model, at_ref, *refs):
     lhs, ws, rest = refs[:n], refs[n:2 * n], refs[2 * n:]
-    out_ref = rest[-1]
     x = jnp.concatenate([r[...] for r in lhs], axis=1)
     w = jnp.concatenate([r[...] for r in ws], axis=0)
     v = jnp.dot(x, w, preferred_element_type=f32)
     if has_acc:
         v = v + rest[0][...]
     if d_model is None:
-        out_ref[...] = v
+        rest[-1][...] = v
         return
-    squares_ref, q_gain_ref, k_gain_ref = rest[-4:-1]
+    squares_ref, q_gain_ref, k_gain_ref, fresh_ref, other_ref, out_ref, moved_ref = rest[-7:]
+    moved_ref[...] = jnp.where(at_ref[1] == 1, fresh_ref[...], other_ref[...])
     v = v * lax.rsqrt(squares_ref[...] / d_model + epsilon)
     heads = v.shape[1] // HD
     for h in range(heads):
@@ -74,7 +74,7 @@
         out_ref[:, h * HD:(h + 1) * HD] = jnp.where(number < HEADS + KV_HEADS, normed, one).astype(bf16)
 
 
-def project(acc, terms, first_head=None, final=None, d_model=None):
+def project(acc, terms, scalars, final=None, d_model=None):
     tok, depth = terms[0][0].shape
     width = terms[0][1].shape[1]
     tn = tile_of(width)
@@ -87,19 +87,25 @@
     if acc is not None:
         in_specs, args = in_specs + [tile], args + [acc]
     if final is not None:
+        block = final[-1].shape[1]
+        moved = pl.BlockSpec((tok, block // (width // tn)), lambda i: (0, i))
         in_specs += [pl.BlockSpec((tok, 1), lambda i: (0, 0))] + [pl.BlockSpec((1, HD), lambda i: (0, 0))] * 2
+        in_specs += [moved] * 2
         args += list(final)
-    first_head = jnp.zeros((1,), jnp.int32) if first_head is None else first_head.astype(jnp.int32).reshape(1)
+    out_specs, out_shape = tile, jax.ShapeDtypeStruct((tok, width), f32)
+    if final is not None:
+        out_specs = [tile, moved]
+        out_shape = [jax.ShapeDtypeStruct((tok, width), bf16), jax.ShapeDtypeStruct((tok, block), bf16)]
     return pl.pallas_call(
         functools.partial(project_kernel, n, acc is not None, d_model),
         grid=(width // tn,),
         in_specs=in_specs,
-        out_specs=tile,
-        out_shape=jax.ShapeDtypeStruct((tok, width), f32 if final is None else bf16),
+        out_specs=out_specs,
+        out_shape=out_shape,
         compiler_params=pltpu.CompilerParams(vmem_limit_bytes=VMEM_LIMIT),
         cost_estimate=pl.CostEstimate(flops=2 * n * tok * depth * width,
                                       bytes_accessed=2 * n * depth * (width + tok) + 8 * tok * width, transcendentals=0),
-    )(first_head, *args)
+    )(scalars, *args)
 
 
 def per_device(residual, post_gain, w_gate, w_up, w_down, next_gain, w_qkv, q_gain, k_gain, source):
@@ -126,10 +132,10 @@
     last_mask = frames[-1]
 
     own = {"gate": w_gate, "up": w_up}
-    gu = {(n, 0): lax.dynamic_slice_in_dim(w, core * half, half, 0) for n, w in own.items()}
+    gu = {0: jnp.concatenate([lax.dynamic_slice_in_dim(w, core * half, half, 0) for w in own.values()], axis=0)}
 
     my_block = core * rows + me
-    from_peer = after(source, gu["gate", 0]) // tok != my_block
+    from_peer = after(source, gu[0]) // tok != my_block
     picked = source % tok + tok * from_peer.astype(jnp.int32)
     onehot = (picked[:, None] == jnp.arange(2 * tok, dtype=jnp.int32)[None, :]).astype(bf16)
     both = jnp.concatenate([residual, swap_cores(residual)], axis=0)
@@ -147,23 +153,18 @@
             if step < left_over:
                 by_odd[step] = lax.ppermute(by_even[step - 1], "col", odd)
 
-    for n in own:
-        for m in direct:
-            gu[n, m] = row_step(gu[n, 0], bits_of(m))
+    for m in direct:
+        gu[m] = row_step(gu[0], bits_of(m))
+    for _ in range(left_over - 1):
         line_step()
-        keys = [(n, m) for m in direct]
-        ready = barrier(tuple(gu[k] for k in keys) + (by_even[step], by_odd[step], gu["up", 0]))
-        for key, value in zip(keys, ready):
-            gu[key] = value
-        by_even[step], by_odd[step], gu["up", 0] = ready[len(keys):]
-    for n in own:
-        for mask, held, bit in order:
-            if held:
-                gu[n, mask] = row_step(gu[n, held], bit)
-    while step < left_over:
-        line_step()
-    gu_other = {key: swap_cores(gu[key]) for key in gu if key[1]}
-
+    ready = barrier(tuple(gu[m] for m in direct) + (by_even[step], by_odd[step]))
+    for m, value in zip(direct, ready):
+        gu[m] = value
+    by_even[step], by_odd[step] = ready[len(direct):]
+    for mask, held, bit in order:
+        if held:
+            gu[mask] = row_step(gu[held], bit)
+    line_step()
     arrived = [placed] + [by_even[t] for t in range(1, cols)] + [by_odd[t] for t in range(1, cols - 1)]
     place = [[0 if j == c else (abs(j - c) if (c % 2 == 1) == (j < c) else cols - 1 + abs(j - c))
               for j in range(cols)] for c in range(cols)]
@@ -190,34 +191,34 @@
     early, late = [0] + direct, relayed
     columns = [jnp.concatenate([normed(m) for m in ms], axis=1) for ms in (early, late)]
 
+    w_down_half = lax.dynamic_slice_in_dim(w_down, core * ff_half, ff_half, 0)
+    ready = barrier(tuple(gu[m] for m in relayed) + tuple(columns) + (w_down_half,))
+    for m, value in zip(relayed, ready):
+        gu[m] = value
+    columns, w_down_half = ready[len(relayed):-1], ready[-1]
+    gu_other = {m: swap_cores(gu[m]) for m in frames[1:]}
+
     def weights(n, masks):
-        pieces = []
+        pieces, at = [], half * (n == "up")
         for m in masks:
-            pieces += [gu[n, m], gu_other[n, mirrored(m, bits)]] if m else [own[n]]
+            pieces += [x[at:at + half] for x in (gu[m], gu_other[mirrored(m, bits)])] if m else [own[n]]
         return jnp.concatenate(pieces, axis=0)
 
-    w_down_half = lax.dynamic_slice_in_dim(w_down, core * ff_half, ff_half, 0)
     w_qkv_half = lax.dynamic_slice_in_dim(w_qkv, core * half, half, 0)
     dn, dn_other, partial = {0: w_down_half}, {}, {}
     wq, wq_other = {0: w_qkv_half}, {}
-    gate_early, up_early = (dot(columns[0], weights(n, early)) for n in own)
-    keys = [(n, m) for n in own for m in relayed]
-    ready = barrier(tuple(gu[k] for k in keys) + (gate_early, up_early, w_down_half))
-    for key, value in zip(keys, ready):
-        gu[key] = value
-        gu_other[key] = swap_cores(value)
-    gate_early, up_early, dn[0] = ready[len(keys):]
     for m in direct:
         dn[m] = row_step(dn[0], bits_of(m))
+    gate_early, up_early = (dot(columns[0], weights(n, early)) for n in own)
     gate = gate_early + dot(columns[1], weights("gate", late))
     up_proj = up_early + dot(columns[1], weights("up", late))
     hidden = (gate / (1 + jnp.exp(-gate)) * up_proj).astype(bf16)
-    partial[0] = dot(hidden, w_down)
+    partial[0] = dot(hidden, w_down).astype(bf16)
     turned = turned_halves(hidden)
-    first_sent = partial[0].astype(bf16)
+    first_sent = partial[0]
 
     def down_product(m):
-        return dot(turned, jnp.concatenate([dn[m], dn_other[mirrored(m, bits)]], axis=0))
+        return dot(turned, jnp.concatenate([dn[m], dn_other[mirrored(m, bits)]], axis=0)).astype(bf16)
 
     from_low = col % 2 == 1
     place_even = jnp.where(from_low, cols - 1 - col, col)
@@ -244,7 +245,7 @@
         return found
 
     def summed(k):
-        total = partial[k]
+        total = partial[k].astype(f32)
         for (is_even, t), where in terms(k).items():
             came = (by_even if is_even else by_odd)[t].astype(f32)
             counts = functools.reduce(jnp.logical_or, [col == c for c in where])
@@ -280,6 +281,7 @@
         if held:
             dn[mask] = row_step(dn[held], bit)
     acc, last_step = None, ()
+    scalars = jnp.stack([(w_qkv.shape[1] // HD) * col, row_of(frames[-1]) == col]).astype(jnp.int32)
 
     def tie(store, masks, values):
         for m, value in zip(masks, values):
@@ -290,12 +292,14 @@
         sends = []
         for i, came in enumerate((by_odd.get(t - 1), by_even.get(t - 1))):
             if base[i] is not None:
-                send = base[i] if came is None else base[i] + came.astype(f32)
+                send = base[i] if came is None else base[i].astype(f32) + came.astype(f32)
                 sends.append((i, first_sent if t == 0 else send.astype(bf16)))
-        held_now = {0: [(dn_other, direct)], 1: [(dn, relayed), (partial, [place_of[m] for m in direct])],
-                    2: [(dn_other, relayed), (wq, direct)],
-                    3: [(wq, relayed), (wq_other, direct), (partial, [place_of[m] for m in relayed])],
-                    4: [(wq_other, relayed)]}.get(t, [])
+        held_now = {1: [(dn, relayed), (partial, [place_of[m] for m in direct])], 2: [(dn_other, relayed), (wq, direct[:1])],
+                    3: [(wq, direct[1:]), (wq_other, direct[:1]), (partial, [place_of[m] for m in relayed])],
+                    4: [(wq, relayed), (wq_other, direct[1:])]}.get(t, [])
+        done = t - cols
+        if done >= 0:
+            held_now = held_now + [(fresh, [done]), (scaled, [done])]
         flat = [store[m] for store, masks in held_now for m in masks]
         extra = [acc] if t == steps - 1 else []
         ready = barrier(tuple(v for _, v in sends) + tuple(flat) + tuple(last_step) + tuple(extra))
@@ -307,38 +311,49 @@
             at += len(masks)
         if extra:
             acc = ready[-1]
+        if t > 0:
+            for (i, _), value in zip(sent_before, ready[at:]):
+                (by_even, by_odd)[i][t - 1] = value
+        sent_before = sends
         last_step = [(by_even, by_odd)[i][t] for i, _ in sends]
         if t == 0:
             for m in direct:
-                partial[place_of[m]] = down_product(m)
+                partial[place_of[m]] = barrier(down_product(m))
         elif t == 1:
             for m in relayed:
                 dn_other[m] = swap_cores(dn[m])
-            for m in direct:
+            for m in direct[:1]:
                 wq[m] = row_step(wq[0], bits_of(m))
         elif t == 2:
+            for m in direct[1:]:
+                wq[m] = row_step(wq[0], bits_of(m))
+            for m in direct[:1]:
+                wq_other[m] = swap_cores(wq[m])
             for m in relayed:
-                partial[place_of[m]] = down_product(m)
-            for m in direct:
+                partial[place_of[m]] = barrier(down_product(m))
+        elif t == 3:
+            for m in direct[1:]:
                 wq_other[m] = swap_cores(wq[m])
             for mask, held, bit in order:
                 if held:
                     wq[mask] = row_step(wq[held], bit)
-        elif t == 3:
+        elif t == 4:
             for m in relayed:
                 wq_other[m] = swap_cores(wq[m])
-        k = t - (cols - 2)
+        k = t - (cols - 1)
         if k >= 0:
             finish(k)
         if k == rows - 3:
-            acc = project(None, [x for j in range(rows - 2) for x in terms_of(j)])
-    acc = project(acc, terms_of(rows - 2))
-
-    moved_residual = fresh[0]
-    for k in range(1, rows):
-        moved_residual = jnp.where(row_of(frames[k]) == col, fresh[k], moved_residual)
-    moved_qkv = project(acc, terms_of(rows - 1), (w_qkv.shape[1] // HD) * col,
-                        (sum(squares.values()), q_gain.reshape(1, HD), k_gain.reshape(1, HD)), d_model)
+            acc = project(None, [x for j in range(rows - 2) for x in terms_of(j)], scalars)
+    acc = project(acc, terms_of(rows - 2), scalars)
+    finish(rows - 1)
+
+    kept = fresh[0]
+    for k in range(1, rows - 1):
+        kept = jnp.where(row_of(frames[k]) == col, fresh[k], kept)
+    moved_qkv, moved_residual = project(
+        acc, terms_of(rows - 1), scalars,
+        (sum(squares.values()), q_gain.reshape(1, HD), k_gain.reshape(1, HD), fresh[rows - 1], kept), d_model)
     return (moved_residual, moved_qkv)
 
 

time: 214 us -> 183 us (0.86)
  waiting for transfers between devices: 83.2 us -> 63.8 us
  local copies, waits for them, and re-layouts: 29.7 us -> 14.7 us
  starting transfers between devices: 45.2 us -> 49.6 us
  other arithmetic: 21 us -> 17.1 us
  Pallas kernels: 6.83 us -> 9.11 us
    ppermute x10, waiting for transfers between devices: 52.7 us -> 35.6 us  [per_device(): (by_even, by_odd)[i][t] = lax.ppermute(send, 'col', (even, odd)[i])]
    ppermute x12 -> x9, waiting for transfers between devices: 22.7 us -> 7.9 us  [row_step(): return lax.ppermute(x, ('rep', 'row'), pairs)]
    ppermute x3, waiting for transfers between devices: 6.02 us -> 18.7 us  [line_step(): by_even[step] = lax.ppermute(by_odd[step - 1], 'col', even)]
    unnamed x98 -> x56, local copies, waits for them, and re-layouts: 22.7 us -> 10.2 us
    ppermute x10, starting transfers between devices: 17 us -> 22 us  [per_device(): (by_even, by_odd)[i][t] = lax.ppermute(send, 'col', (even, odd)[i])]
    ppermute x3, starting transfers between devices: 6.19 us -> 9.19 us  [line_step(): by_even[step] = lax.ppermute(by_odd[step - 1], 'col', even)]
    pallas_call x3, Pallas kernels: 6.83 us -> 9.11 us  [project(): pl.pallas_call(functools.partial(project_kernel, n, acc is not None, d_mo...]
    reduce_sum x2 -> x4, other arithmetic: 6.55 us -> 4.27 us  [finish(): squares[k] = jnp.sum(v * v, axis=-1, keepdims=True)]
  transfers between devices with their start and end apart: 40 -> 34, of which waited for: 14 -> 13; matrix products, arithmetic and copies ran while one was open for 27% -> 26% of each run, Pallas kernels for 2% -> 3%
where the time goes in v3:
time: 183 us; the launch traced here: 182 us
  waiting for transfers between devices  63.8 us (35%)
  starting transfers between devices  49.6 us (27%)
  matrix products  18.6 us (10%)
  other arithmetic  17.1 us (9%)
  local copies, waits for them, and re-layouts  14.7 us (8%)
  Pallas kernels  9.11 us (5%)
  between operations  8.92 us (5%)
    ppermute x10, waiting for transfers between devices, per_device(): (by_even, by_odd)[i][t] = lax.ppermute(send, 'col', (even, odd)[i])  35.6 us
    ppermute x10, starting transfers between devices, per_device(): (by_even, by_odd)[i][t] = lax.ppermute(send, 'col', (even, odd)[i])  22 us
    ppermute x3, waiting for transfers between devices, line_step(): by_even[step] = lax.ppermute(by_odd[step - 1], 'col', even)  18.7 us
    dot_general x8, matrix products, dot(): return jnp.dot(x, w, preferred_element_type=f32)  15.7 us
    ppermute x9, starting transfers between devices, row_step(): return lax.ppermute(x, ('rep', 'row'), pairs)  14.8 us
    unnamed x56, local copies, waits for them, and re-layouts  10.2 us
    ppermute x3, starting transfers between devices, line_step(): by_even[step] = lax.ppermute(by_odd[step - 1], 'col', even)  9.19 us
    pallas_call x3, Pallas kernels, project(): pl.pallas_call(functools.partial(project_kernel, n, acc is not None, d_mo...  9.11 us
  transfers between devices with their start and end apart: 34, of which 13 were waited for; matrix products, arithmetic and copies ran while one was open for 26% of the time, Pallas kernels for 3%

profile of v3, /device:TPU:0, one launch (start us, length us, event | category | flops | bytes accessed | tf_op | source)
XLA Modules:
  0.0 182.0 jit_solution(9880715353278834026)
XLA Ops:
  4.9 2.6 %collective-permute-start.2 = (bf16[512,1536]{1,0:T(8,128)(2,1)}, bf16[512,1536]{1,0:T(8,128)(2,1)}, u32[]{:S(2)}, u32[]{:S(2)}) collective-permute-start(bf16[512,1536]{1,0:T(8,128)(2,1)} %pad_maximum_fusion), channel_id=1, source_target_pairs={{0,4},{4,0},{8,12},{12,8},{16,24},{20,28},{24,16},{28,20},{1,5},{5... | collective-permute-start | bytes 4718600 | tf_op jit(solution)/shard_map/ppermute | solution.py:41
  9.1 2.9 %bitcast_dynamic-update-slice_fusion.5 = (bf16[6,512,512]{2,1,0:T(8,128)(2,1)}, bf16[512,512]{1,0:T(8,128)(2,1)}) fusion(bf16[512,512]{1,0:T(8,128)(2,1)} %collective-permute-done, bf16[512,512]{1,0:T(8,128)(2,1)} %param.11, s32[512]{0:T(512)S(1)} %fusion.75), kind=kOutput, calls=%fused_computation.127 | convolution fusion | flops 539754496 | bytes 2099200 | tf_op jit(solution)/shard_map/dot_general | solution.py:142
  13.6 3.6 %collective-permute-start.1 = (bf16[512,512]{1,0:T(8,128)(2,1)}, bf16[512,512]{1,0:T(8,128)(2,1)}, u32[]{:S(2)}, u32[]{:S(2)}) collective-permute-start(bf16[512,512]{1,0:T(8,128)(2,1)} %get-tuple-element.148), channel_id=1, source_target_pairs={{0,1},{1,0},{2,3},{3,2},{4,5},{5,4},{6,7},{7,6},{8,9},{9,8},{10,11... | collective-permute-start | bytes 1572872 | tf_op jit(solution)/shard_map/ppermute | solution.py:152
  25.6 3.9 %collective-permute-start.5 = (bf16[512,512]{1,0:T(8,128)(2,1)}, bf16[512,512]{1,0:T(8,128)(2,1)S(1)}, u32[]{:S(2)}, u32[]{:S(2)}) collective-permute-start(bf16[512,512]{1,0:T(8,128)(2,1)} %collective-permute-done.4), channel_id=1, source_target_pairs={{0,1},{1,0},{2,3},{3,2},{4,5},{5,4},{6,7},{7,6},{8,9},{9,8},{10,11... | collective-permute-start | bytes 1572872 | tf_op jit(solution)/shard_map/ppermute | solution.py:152
  32.9 7.8 %collective-permute-done.5 = bf16[512,512]{1,0:T(8,128)(2,1)S(1)} collective-permute-done((bf16[512,512]{1,0:T(8,128)(2,1)}, bf16[512,512]{1,0:T(8,128)(2,1)S(1)}, u32[]{:S(2)}, u32[]{:S(2)}) %collective-permute-start.5) | collective-permute-done | bytes 524320 | tf_op jit(solution)/shard_map/ppermute | solution.py:152
  48.1 10.8 %collective-permute-done.7 = bf16[512,512]{1,0:T(8,128)(2,1)S(1)} collective-permute-done((bf16[512,512]{1,0:T(8,128)(2,1)S(1)}, bf16[512,512]{1,0:T(8,128)(2,1)S(1)}, u32[]{:S(2)}, u32[]{:S(2)}) %collective-permute-start.7) | collective-permute-done | bytes 524320 | tf_op jit(solution)/shard_map/ppermute | solution.py:152
  72.4 2.6 %convolution_add_fusion.1 = f32[512,1536]{1,0:T(8,128)S(1)} fusion(f32[512,1536]{1,0:T(8,128)S(1)} %fusion.1, bf16[512,1536]{1,0:T(8,128)(2,1)S(1)} %select_dynamic-update-slice_fusion, bf16[1536,1536]{1,0:T(8,128)(2,1)S(1)} %get-tuple-element.111), kind=kOutput, calls=%fused_computation.1 | convolution fusion | flops 2416705536 | bytes 12582912 | tf_op jit(solution)/shard_map/dot_general | solution.py:189
  75.1 2.8 %multiply_convert_fusion = bf16[512,1536]{1,0:T(8,128)(2,1)S(1)} fusion(f32[512,1536]{1,0:T(8,128)S(1)} %convolution_add_fusion.1, f32[512,1536]{1,0:T(8,128)S(1)} %fusion.5, bf16[512,1536]{1,0:T(8,128)(2,1)S(1)} %select_dynamic-update-slice_fusion, bf16[1536,1536]{1,0:T(8,128)(2,1)S(1)} %get-tuple-element.112), kind=kOutput, calls=%fused_computation.2 | convolution fusion | flops 2420637696 | bytes 14155776 | tf_op jit(solution)/shard_map/dot_general | solution.py:189
  78.8 4.5 %collective-permute-done.12 = bf16[768,512]{1,0:T(8,128)(2,1)S(1)} collective-permute-done((bf16[768,512]{1,0:T(8,128)(2,1)S(1)}, bf16[768,512]{1,0:T(8,128)(2,1)S(1)}, u32[]{:S(2)}, u32[]{:S(2)}) %collective-permute-start.12) | collective-permute-done | bytes 786464 | tf_op jit(solution)/shard_map/ppermute | solution.py:41
  87.7 9.1 %collective-permute-done.15 = bf16[512,512]{1,0:T(8,128)(2,1)S(1)} collective-permute-done((bf16[512,512]{1,0:T(8,128)(2,1)S(1)}, bf16[512,512]{1,0:T(8,128)(2,1)S(1)}, u32[]{:S(2)}, u32[]{:S(2)}) %collective-permute-start.15) | collective-permute-done | bytes 524320 | tf_op jit(solution)/shard_map/ppermute | solution.py:307
  100.0 2.3 %fusion.28 = bf16[512,512]{1,0:T(8,128)(2,1)S(1)} fusion(bf16[768,512]{1,0:T(8,128)(2,1)S(1)} %collective-permute-done.14, bf16[768,512]{1,0:T(8,128)(2,1)S(1)} %collective-permute-done.12, bf16[512,768]{1,0:T(8,128)(2,1)} %get-tuple-element.110, bf16[512,768]{1,0:T(8,128)(2,1)S(1)} %get-tuple-element.109), kind=kOutput, calls=%fused_computation.65 | convolution fusion | flops 811859968 | bytes 3670016 | tf_op jit(solution)/shard_map/dot_general | solution.py:189
  105.7 2.4 %collective-permute-start.21 = (bf16[256,1024]{1,0:T(8,128)(2,1)}, bf16[256,1024]{1,0:T(8,128)(2,1)S(1)}, u32[]{:S(2)}, u32[]{:S(2)}) collective-permute-start(bf16[256,1024]{1,0:T(8,128)(2,1)} %constant_dynamic-slice_fusion.4), channel_id=1, source_target_pairs={{0,4},{4,0},{8,12},{12,8},{16,24},{20,28},{24,16},{28,20},{1,5},{5... | collective-permute-start | bytes 1572872 | tf_op jit(solution)/shard_map/ppermute | solution.py:41
  108.1 7.1 %collective-permute-done.19 = bf16[512,512]{1,0:T(8,128)(2,1)} collective-permute-done((bf16[512,512]{1,0:T(8,128)(2,1)S(1)}, bf16[512,512]{1,0:T(8,128)(2,1)}, u32[]{:S(2)}, u32[]{:S(2)}) %collective-permute-start.19) | collective-permute-done | bytes 524320 | tf_op jit(solution)/shard_map/ppermute | solution.py:307
  119.3 3.1 %collective-permute-start.23 = (bf16[512,512]{1,0:T(8,128)(2,1)}, bf16[512,512]{1,0:T(8,128)(2,1)}, u32[]{:S(2)}, u32[]{:S(2)}) collective-permute-start(bf16[512,512]{1,0:T(8,128)(2,1)} %add_convert_fusion.1), channel_id=1, source_target_pairs={{0,1},{1,0},{2,3},{3,2},{4,5},{5,4},{6,7},{7,6},{8,9},{9,8},{10,11... | collective-permute-start | bytes 1572872 | tf_op jit(solution)/shard_map/ppermute | solution.py:307
  125.3 2.9 %fusion.22 = bf16[512,512]{1,0:T(8,128)(2,1)S(1)} fusion(bf16[768,512]{1,0:T(8,128)(2,1)} %collective-permute-done.20, bf16[768,512]{1,0:T(8,128)(2,1)} %collective-permute-done.16, bf16[512,768]{1,0:T(8,128)(2,1)} %get-tuple-element.110, bf16[512,768]{1,0:T(8,128)(2,1)} %copy-done.19), kind=kOutput, calls=%fused_computation.63 | convolution fusion | flops 811859968 | bytes 3670016 | tf_op jit(solution)/shard_map/dot_general | solution.py:189
  128.2 4.5 %collective-permute-done.23 = bf16[512,512]{1,0:T(8,128)(2,1)} collective-permute-done((bf16[512,512]{1,0:T(8,128)(2,1)}, bf16[512,512]{1,0:T(8,128)(2,1)}, u32[]{:S(2)}, u32[]{:S(2)}) %collective-permute-start.23) | collective-permute-done | bytes 524320 | tf_op jit(solution)/shard_map/ppermute | solution.py:307
  134.2 3.7 %collective-permute-start.27 = (bf16[512,512]{1,0:T(8,128)(2,1)S(1)}, bf16[512,512]{1,0:T(8,128)(2,1)S(1)}, u32[]{:S(2)}, u32[]{:S(2)}) collective-permute-start(bf16[512,512]{1,0:T(8,128)(2,1)S(1)} %add_convert_fusion), channel_id=1, source_target_pairs={{0,1},{1,0},{2,3},{3,2},{4,5},{5,4},{6,7},{7,6},{8,9},{9,8},{10,11... | collective-permute-start | bytes 1572872 | tf_op jit(solution)/shard_map/ppermute | solution.py:307
  140.7 7.4 %collective-permute-done.27 = bf16[512,512]{1,0:T(8,128)(2,1)S(1)} collective-permute-done((bf16[512,512]{1,0:T(8,128)(2,1)S(1)}, bf16[512,512]{1,0:T(8,128)(2,1)S(1)}, u32[]{:S(2)}, u32[]{:S(2)}) %collective-permute-start.27) | collective-permute-done | bytes 524320 | tf_op jit(solution)/shard_map/ppermute | solution.py:307
  149.0 6.4 %collective-permute-start.31 = (bf16[512,512]{1,0:T(8,128)(2,1)S(1)}, bf16[512,512]{1,0:T(8,128)(2,1)S(1)}, u32[]{:S(2)}, u32[]{:S(2)}) collective-permute-start(bf16[512,512]{1,0:T(8,128)(2,1)S(1)} %fusion.50), channel_id=1, source_target_pairs={{0,1},{1,0},{2,3},{3,2},{4,5},{5,4},{6,7},{7,6},{8,9},{9,8},{10,11... | collective-permute-start | bytes 1572872 | tf_op jit(solution)/shard_map/ppermute | solution.py:307
  157.2 2.7 %shard_map.122.refs_4_ = f32[512,1024]{1,0:T(8,128)S(1)} custom-call(s32[2]{0:T(128)S(1)} %pad_add_fusion.at_ref, bf16[512,256]{1,0:T(8,128)(2,1)S(1)} %get-tuple-element.132.refs_0_, bf16[512,256]{1,0:T(8,128)(2,1)S(1)} %get-tuple-element.131.refs_1_, bf16[512,256]{1,0:T(8,128)(2,1)S(1)} %get-tuple-element.130.refs_2_, ...), custom_call_target="tpu_custom_call" | custom-call | flops 1073741824 | bytes 7340032 | tf_op jit(solution)/shard_map/pallas_call | solution.py:99
  160.1 4.9 %collective-permute-done.31 = bf16[512,512]{1,0:T(8,128)(2,1)S(1)} collective-permute-done((bf16[512,512]{1,0:T(8,128)(2,1)S(1)}, bf16[512,512]{1,0:T(8,128)(2,1)S(1)}, u32[]{:S(2)}, u32[]{:S(2)}) %collective-permute-start.31) | collective-permute-done | bytes 524320 | tf_op jit(solution)/shard_map/ppermute | solution.py:307
  165.0 2.4 %collective-permute-start.32 = (bf16[512,512]{1,0:T(8,128)(2,1)S(1)}, bf16[512,512]{1,0:T(8,128)(2,1)S(1)}, u32[]{:S(2)}, u32[]{:S(2)}) collective-permute-start(bf16[512,512]{1,0:T(8,128)(2,1)S(1)} %fusion.52), channel_id=1, source_target_pairs={{0,1},{1,0},{2,3},{3,2},{4,5},{5,4},{6,7},{7,6},{8,9},{9,8},{10,11... | collective-permute-start | bytes 1572872 | tf_op jit(solution)/shard_map/ppermute | solution.py:307
  172.9 2.5 %collective-permute-done.32 = bf16[512,512]{1,0:T(8,128)(2,1)S(1)} collective-permute-done((bf16[512,512]{1,0:T(8,128)(2,1)S(1)}, bf16[512,512]{1,0:T(8,128)(2,1)S(1)}, u32[]{:S(2)}, u32[]{:S(2)}) %collective-permute-start.32) | collective-permute-done | bytes 524320 | tf_op jit(solution)/shard_map/ppermute | solution.py:307
  177.8 4.2 %shard_map.124 = (bf16[512,1024]{1,0:T(8,128)(2,1)}, bf16[512,512]{1,0:T(8,128)(2,1)}) custom-call(s32[2]{0:T(128)S(1)} %pad_add_fusion.at_ref, bf16[512,256]{1,0:T(8,128)(2,1)S(1)} %get-tuple-element.128.refs_0_, bf16[512,256]{1,0:T(8,128)(2,1)S(1)} %get-tuple-element.127.refs_1_, bf16[256,1024]{1,0:T(8,128)(2,1)S(1)} %collective-permute-done.28.refs_2_, ...), custom_call_target="tpu_custom_call" | custom-call | flops 536870912 | bytes 5767168 | tf_op jit(solution)/shard_map/pallas_call | solution.py:99
  (159 shorter events, 65.7 us)
Async XLA Ops:
  4.9 37.1 %collective-permute-start.2 = (bf16[512,1536]{1,0:T(8,128)(2,1)}, bf16[512,1536]{1,0:T(8,128)(2,1)}, u32[]{:S(2)}, u32[]{:S(2)}) collective-permute-start(bf16[512,1536]{1,0:T(8,128)(2,1)} %pad_maximum_fusion), channel_id=1, source_target_pairs={{0,4},{4,0},{8,12},{12,8},{16,24},{20,28},{24,16},{28,20},{1,5},{5... | collective-permute-start | bytes 4718600 | tf_op jit(solution)/shard_map/ppermute | solution.py:41
  7.5 35.3 %collective-permute-start.3 = (bf16[512,1536]{1,0:T(8,128)(2,1)}, bf16[512,1536]{1,0:T(8,128)(2,1)}, u32[]{:S(2)}, u32[]{:S(2)}) collective-permute-start(bf16[512,1536]{1,0:T(8,128)(2,1)} %pad_maximum_fusion), channel_id=1, source_target_pairs={{0,8},{4,12},{8,0},{12,4},{16,20},{20,16},{24,28},{28,24},{1,9},{5... | collective-permute-start | bytes 4718600 | tf_op jit(solution)/shard_map/ppermute | solution.py:41
  12.0 13.5 %collective-permute-start.4 = (bf16[512,512]{1,0:T(8,128)(2,1)}, bf16[512,512]{1,0:T(8,128)(2,1)}, u32[]{:S(2)}, u32[]{:S(2)}) collective-permute-start(bf16[512,512]{1,0:T(8,128)(2,1)} %get-tuple-element.148), channel_id=1, source_target_pairs={{1,2},{2,1},{5,6},{6,5},{9,10},{10,9},{13,14},{14,13},{17,18},{18,... | collective-permute-start | bytes 1572872 | tf_op jit(solution)/shard_map/ppermute | solution.py:154
  13.6 15.9 %collective-permute-start.1 = (bf16[512,512]{1,0:T(8,128)(2,1)}, bf16[512,512]{1,0:T(8,128)(2,1)}, u32[]{:S(2)}, u32[]{:S(2)}) collective-permute-start(bf16[512,512]{1,0:T(8,128)(2,1)} %get-tuple-element.148), channel_id=1, source_target_pairs={{0,1},{1,0},{2,3},{3,2},{4,5},{5,4},{6,7},{7,6},{8,9},{9,8},{10,11... | collective-permute-start | bytes 1572872 | tf_op jit(solution)/shard_map/ppermute | solution.py:152
  25.6 15.1 %collective-permute-start.5 = (bf16[512,512]{1,0:T(8,128)(2,1)}, bf16[512,512]{1,0:T(8,128)(2,1)S(1)}, u32[]{:S(2)}, u32[]{:S(2)}) collective-permute-start(bf16[512,512]{1,0:T(8,128)(2,1)} %collective-permute-done.4), channel_id=1, source_target_pairs={{0,1},{1,0},{2,3},{3,2},{4,5},{5,4},{6,7},{7,6},{8,9},{9,8},{10,11... | collective-permute-start | bytes 1572872 | tf_op jit(solution)/shard_map/ppermute | solution.py:152
  42.8 20.6 %collective-permute-start.8 = (bf16[512,1536]{1,0:T(8,128)(2,1)}, bf16[512,1536]{1,0:T(8,128)(2,1)S(1)}, u32[]{:S(2)}, u32[]{:S(2)}) collective-permute-start(bf16[512,1536]{1,0:T(8,128)(2,1)} %collective-permute-done.2), channel_id=1, source_target_pairs={{0,8},{4,12},{8,0},{12,4},{16,20},{20,16},{24,28},{28,24},{1,9},{5... | collective-permute-start | bytes 4718600 | tf_op jit(solution)/shard_map/ppermute | solution.py:41
  44.6 24.1 %collective-permute-start.10 = (bf16[512,1536]{1,0:T(8,128)(2,1)}, bf16[512,1536]{1,0:T(8,128)(2,1)S(1)}, u32[]{:S(2)}, u32[]{:S(2)}) collective-permute-start(bf16[512,1536]{1,0:T(8,128)(2,1)} %collective-permute-done.2), channel_id=1, source_target_pairs={{0,16},{16,0},{1,17},{17,1},{2,18},{18,2},{3,19},{19,3},{4,20},{20... | collective-permute-start | bytes 4718600 | tf_op jit(solution)/shard_map/ppermute | solution.py:19
  44.7 14.3 %collective-permute-start.7 = (bf16[512,512]{1,0:T(8,128)(2,1)S(1)}, bf16[512,512]{1,0:T(8,128)(2,1)S(1)}, u32[]{:S(2)}, u32[]{:S(2)}) collective-permute-start(bf16[512,512]{1,0:T(8,128)(2,1)S(1)} %collective-permute-done.6), channel_id=1, source_target_pairs={{0,1},{1,0},{2,3},{3,2},{4,5},{5,4},{6,7},{7,6},{8,9},{9,8},{10,11... | collective-permute-start | bytes 1572872 | tf_op jit(solution)/shard_map/ppermute | solution.py:152
  46.4 20.7 %collective-permute-start.9 = (bf16[512,1536]{1,0:T(8,128)(2,1)}, bf16[512,1536]{1,0:T(8,128)(2,1)S(1)}, u32[]{:S(2)}, u32[]{:S(2)}) collective-permute-start(bf16[512,1536]{1,0:T(8,128)(2,1)} %collective-permute-done.3), channel_id=1, source_target_pairs={{0,16},{16,0},{1,17},{17,1},{2,18},{18,2},{3,19},{19,3},{4,20},{20... | collective-permute-start | bytes 4718600 | tf_op jit(solution)/shard_map/ppermute | solution.py:19
  63.5 19.9 %collective-permute-start.12 = (bf16[768,512]{1,0:T(8,128)(2,1)S(1)}, bf16[768,512]{1,0:T(8,128)(2,1)S(1)}, u32[]{:S(2)}, u32[]{:S(2)}) collective-permute-start(bf16[768,512]{1,0:T(8,128)(2,1)S(1)} %constant_dynamic-slice_fusion.5), channel_id=1, source_target_pairs={{0,4},{4,0},{8,12},{12,8},{16,24},{20,28},{24,16},{28,20},{1,5},{5... | collective-permute-start | bytes 2359304 | tf_op jit(solution)/shard_map/ppermute | solution.py:41
  65.2 18.2 %collective-permute-start.13 = (bf16[768,512]{1,0:T(8,128)(2,1)S(1)}, bf16[768,512]{1,0:T(8,128)(2,1)S(1)}, u32[]{:S(2)}, u32[]{:S(2)}) collective-permute-start(bf16[768,512]{1,0:T(8,128)(2,1)S(1)} %constant_dynamic-slice_fusion.5), channel_id=1, source_target_pairs={{0,8},{4,12},{8,0},{12,4},{16,20},{20,16},{24,28},{28,24},{1,9},{5... | collective-permute-start | bytes 2359304 | tf_op jit(solution)/shard_map/ppermute | solution.py:41
  83.3 13.5 %collective-permute-start.15 = (bf16[512,512]{1,0:T(8,128)(2,1)S(1)}, bf16[512,512]{1,0:T(8,128)(2,1)S(1)}, u32[]{:S(2)}, u32[]{:S(2)}) collective-permute-start(bf16[512,512]{1,0:T(8,128)(2,1)S(1)} %convolution_convert_fusion), channel_id=1, source_target_pairs={{0,1},{1,0},{2,3},{3,2},{4,5},{5,4},{6,7},{7,6},{8,9},{9,8},{10,11... | collective-permute-start | bytes 1572872 | tf_op jit(solution)/shard_map/ppermute | solution.py:307
  85.2 12.7 %collective-permute-start.17 = (bf16[768,512]{1,0:T(8,128)(2,1)S(1)}, bf16[768,512]{1,0:T(8,128)(2,1)S(1)}, u32[]{:S(2)}, u32[]{:S(2)}) collective-permute-start(bf16[768,512]{1,0:T(8,128)(2,1)S(1)} %collective-permute-done.12), channel_id=1, source_target_pairs={{0,16},{16,0},{1,17},{17,1},{2,18},{18,2},{3,19},{19,3},{4,20},{20... | collective-permute-start | bytes 2359304 | tf_op jit(solution)/shard_map/ppermute | solution.py:19
  85.2 14.9 %collective-permute-start.14 = (bf16[768,512]{1,0:T(8,128)(2,1)S(1)}, bf16[768,512]{1,0:T(8,128)(2,1)S(1)}, u32[]{:S(2)}, u32[]{:S(2)}) collective-permute-start(bf16[768,512]{1,0:T(8,128)(2,1)S(1)} %collective-permute-done.13), channel_id=1, source_target_pairs={{0,16},{16,0},{1,17},{17,1},{2,18},{18,2},{3,19},{19,3},{4,20},{20... | collective-permute-start | bytes 2359304 | tf_op jit(solution)/shard_map/ppermute | solution.py:19
  85.7 16.7 %collective-permute-start.16 = (bf16[768,512]{1,0:T(8,128)(2,1)S(1)}, bf16[768,512]{1,0:T(8,128)(2,1)}, u32[]{:S(2)}, u32[]{:S(2)}) collective-permute-start(bf16[768,512]{1,0:T(8,128)(2,1)S(1)} %collective-permute-done.12), channel_id=1, source_target_pairs={{0,8},{4,12},{8,0},{12,4},{16,20},{20,16},{24,28},{28,24},{1,9},{5... | collective-permute-start | bytes 2359304 | tf_op jit(solution)/shard_map/ppermute | solution.py:41
  102.4 12.9 %collective-permute-start.19 = (bf16[512,512]{1,0:T(8,128)(2,1)S(1)}, bf16[512,512]{1,0:T(8,128)(2,1)}, u32[]{:S(2)}, u32[]{:S(2)}) collective-permute-start(bf16[512,512]{1,0:T(8,128)(2,1)S(1)} %fusion.28), channel_id=1, source_target_pairs={{0,1},{1,0},{2,3},{3,2},{4,5},{5,4},{6,7},{7,6},{8,9},{9,8},{10,11... | collective-permute-start | bytes 1572872 | tf_op jit(solution)/shard_map/ppermute | solution.py:307
  103.4 13.8 %collective-permute-start.18 = (bf16[512,512]{1,0:T(8,128)(2,1)}, bf16[512,512]{1,0:T(8,128)(2,1)}, u32[]{:S(2)}, u32[]{:S(2)}) collective-permute-start(bf16[512,512]{1,0:T(8,128)(2,1)} %fusion.31), channel_id=1, source_target_pairs={{1,2},{2,1},{5,6},{6,5},{9,10},{10,9},{13,14},{14,13},{17,18},{18,... | collective-permute-start | bytes 1572872 | tf_op jit(solution)/shard_map/ppermute | solution.py:307
  104.9 14.4 %collective-permute-start.20 = (bf16[768,512]{1,0:T(8,128)(2,1)}, bf16[768,512]{1,0:T(8,128)(2,1)}, u32[]{:S(2)}, u32[]{:S(2)}) collective-permute-start(bf16[768,512]{1,0:T(8,128)(2,1)} %collective-permute-done.16), channel_id=1, source_target_pairs={{0,16},{16,0},{1,17},{17,1},{2,18},{18,2},{3,19},{19,3},{4,20},{20... | collective-permute-start | bytes 2359304 | tf_op jit(solution)/shard_map/ppermute | solution.py:19
  105.7 13.5 %collective-permute-start.21 = (bf16[256,1024]{1,0:T(8,128)(2,1)}, bf16[256,1024]{1,0:T(8,128)(2,1)S(1)}, u32[]{:S(2)}, u32[]{:S(2)}) collective-permute-start(bf16[256,1024]{1,0:T(8,128)(2,1)} %constant_dynamic-slice_fusion.4), channel_id=1, source_target_pairs={{0,4},{4,0},{8,12},{12,8},{16,24},{20,28},{24,16},{28,20},{1,5},{5... | collective-permute-start | bytes 1572872 | tf_op jit(solution)/shard_map/ppermute | solution.py:41
  119.3 13.5 %collective-permute-start.23 = (bf16[512,512]{1,0:T(8,128)(2,1)}, bf16[512,512]{1,0:T(8,128)(2,1)}, u32[]{:S(2)}, u32[]{:S(2)}) collective-permute-start(bf16[512,512]{1,0:T(8,128)(2,1)} %add_convert_fusion.1), channel_id=1, source_target_pairs={{0,1},{1,0},{2,3},{3,2},{4,5},{5,4},{6,7},{7,6},{8,9},{9,8},{10,11... | collective-permute-start | bytes 1572872 | tf_op jit(solution)/shard_map/ppermute | solution.py:307
  123.2 25.0 %collective-permute-start.28 = (bf16[256,1024]{1,0:T(8,128)(2,1)S(1)}, bf16[256,1024]{1,0:T(8,128)(2,1)S(1)}, u32[]{:S(2)}, u32[]{:S(2)}) collective-permute-start(bf16[256,1024]{1,0:T(8,128)(2,1)S(1)} %collective-permute-done.21.refs_6_), channel_id=1, source_target_pairs={{0,8},{4,12},{8,0},{12,4},{16,20},{20,16},{24,28},{28,24},{1,9},{5... | collective-permute-start | bytes 1572872 | tf_op jit(solution)/shard_map/ppermute | solution.py:41
  134.2 13.9 %collective-permute-start.27 = (bf16[512,512]{1,0:T(8,128)(2,1)S(1)}, bf16[512,512]{1,0:T(8,128)(2,1)S(1)}, u32[]{:S(2)}, u32[]{:S(2)}) collective-permute-start(bf16[512,512]{1,0:T(8,128)(2,1)S(1)} %add_convert_fusion), channel_id=1, source_target_pairs={{0,1},{1,0},{2,3},{3,2},{4,5},{5,4},{6,7},{7,6},{8,9},{9,8},{10,11... | collective-permute-start | bytes 1572872 | tf_op jit(solution)/shard_map/ppermute | solution.py:307
  149.0 16.1 %collective-permute-start.31 = (bf16[512,512]{1,0:T(8,128)(2,1)S(1)}, bf16[512,512]{1,0:T(8,128)(2,1)S(1)}, u32[]{:S(2)}, u32[]{:S(2)}) collective-permute-start(bf16[512,512]{1,0:T(8,128)(2,1)S(1)} %fusion.50), channel_id=1, source_target_pairs={{0,1},{1,0},{2,3},{3,2},{4,5},{5,4},{6,7},{7,6},{8,9},{9,8},{10,11... | collective-permute-start | bytes 1572872 | tf_op jit(solution)/shard_map/ppermute | solution.py:307
  155.4 21.0 %collective-permute-start.33 = (bf16[256,1024]{1,0:T(8,128)(2,1)S(1)}, bf16[256,1024]{1,0:T(8,128)(2,1)}, u32[]{:S(2)}, u32[]{:S(2)}) collective-permute-start(bf16[256,1024]{1,0:T(8,128)(2,1)S(1)} %collective-permute-done.28.refs_2_), channel_id=1, source_target_pairs={{0,16},{16,0},{1,17},{17,1},{2,18},{18,2},{3,19},{19,3},{4,20},{20... | collective-permute-start | bytes 1572872 | tf_op jit(solution)/shard_map/ppermute | solution.py:19
  (34 other events, 404.4 us)

commit v4 on v3

--- a/solution.py
+++ b/solution.py
@@ -49,7 +49,28 @@
 
 
 def tile_of(n):
-    return next(t for t in (256, 128, n) if n % t == 0)
+    return next(t for t in (512, 256, 128, n) if n % t == 0)
+
+
+def halves_kernel(core_ref, top_ref, bottom_ref, out_ref):
+    half = top_ref.shape[0]
+    out_ref[:half] = top_ref[...]
+    out_ref[half:] = bottom_ref[...]
+
+
+def core_halves(core, top, bottom):
+    half, width = top.shape[0] // 2, top.shape[1]
+    tn = next(t for t in (512, 384, 128, width) if width % t == 0)
+    piece = pl.BlockSpec((half, tn), lambda i, c: (c[0], i))
+    return pl.pallas_call(
+        halves_kernel,
+        grid_spec=pltpu.PrefetchScalarGridSpec(
+            num_scalar_prefetch=1, grid=(width // tn,), in_specs=[piece, piece],
+            out_specs=pl.BlockSpec((2 * half, tn), lambda i, c: (0, i))),
+        out_shape=jax.ShapeDtypeStruct((2 * half, width), bf16),
+        compiler_params=pltpu.CompilerParams(vmem_limit_bytes=VMEM_LIMIT),
+        cost_estimate=pl.CostEstimate(flops=0, bytes_accessed=8 * half * width, transcendentals=0),
+    )(core, top, bottom)
 
 
 def project_kernel(n, has_acc, d_model, at_ref, *refs):
@@ -126,13 +147,16 @@
 
     barrier = lax.optimization_barrier
     even = [(i, i ^ 1) for i in range(cols)]
-    odd = [(i, (i - 1 ^ 1) + 1) for i in range(1, cols - 1)]
+    odd = [(cols * r + i, cols * r + (i - 1 ^ 1) + 1) for r in range(2) for i in range(1, cols - 1)]
+    odd += [(cols * r + i, cols * (1 - r) + i) for r in range(2) for i in (0, cols - 1)]
+    line_axes = ("col", ("rep", "col"))
+    at_end = (col == 0) | (col == cols - 1)
     ff = w_gate.shape[1]
     ff_half = ff // 2
     last_mask = frames[-1]
 
     own = {"gate": w_gate, "up": w_up}
-    gu = {0: jnp.concatenate([lax.dynamic_slice_in_dim(w, core * half, half, 0) for w in own.values()], axis=0)}
+    gu = {0: core_halves(core.astype(jnp.int32).reshape(1), w_gate, w_up)}
 
     my_block = core * rows + me
     from_peer = after(source, gu[0]) // tok != my_block
@@ -151,20 +175,21 @@
             step += 1
             by_even[step] = lax.ppermute(by_odd[step - 1], "col", even)
             if step < left_over:
-                by_odd[step] = lax.ppermute(by_even[step - 1], "col", odd)
+                by_odd[step] = lax.ppermute(by_even[step - 1], line_axes[1], odd)
 
     for m in direct:
         gu[m] = row_step(gu[0], bits_of(m))
-    for _ in range(left_over - 1):
+    for _ in range(left_over):
         line_step()
-    ready = barrier(tuple(gu[m] for m in direct) + (by_even[step], by_odd[step]))
+    before = max(left_over - 1, 0)
+    ready = barrier(tuple(gu[m] for m in direct) + (by_even[before], by_odd[before]))
     for m, value in zip(direct, ready):
         gu[m] = value
-    by_even[step], by_odd[step] = ready[len(direct):]
+    by_even[before], by_odd[before] = ready[len(direct):]
     for mask, held, bit in order:
         if held:
             gu[mask] = row_step(gu[held], bit)
-    line_step()
+
     arrived = [placed] + [by_even[t] for t in range(1, cols)] + [by_odd[t] for t in range(1, cols - 1)]
     place = [[0 if j == c else (abs(j - c) if (c % 2 == 1) == (j < c) else cols - 1 + abs(j - c))
               for j in range(cols)] for c in range(cols)]
@@ -276,7 +301,6 @@
     for m, value in zip(direct, ready):
         dn[m] = value
         dn_other[m] = swap_cores(value)
-    first_sent = ready[-1]
     for mask, held, bit in order:
         if held:
             dn[mask] = row_step(dn[held], bit)
@@ -292,7 +316,10 @@
         sends = []
         for i, came in enumerate((by_odd.get(t - 1), by_even.get(t - 1))):
             if base[i] is not None:
-                send = base[i] if came is None else base[i].astype(f32) + came.astype(f32)
+                send = base[i]
+                if came is not None:
+                    came = came.astype(f32)
+                    send = send.astype(f32) + (jnp.where(at_end, 0, came) if i == 0 else came)
                 sends.append((i, first_sent if t == 0 else send.astype(bf16)))
         held_now = {1: [(dn, relayed), (partial, [place_of[m] for m in direct])], 2: [(dn_other, relayed), (wq, direct[:1])],
                     3: [(wq, direct[1:]), (wq_other, direct[:1]), (partial, [place_of[m] for m in relayed])],
@@ -304,7 +331,7 @@
         extra = [acc] if t == steps - 1 else []
         ready = barrier(tuple(v for _, v in sends) + tuple(flat) + tuple(last_step) + tuple(extra))
         for (i, _), send in zip(sends, ready):
-            (by_even, by_odd)[i][t] = lax.ppermute(send, "col", (even, odd)[i])
+            (by_even, by_odd)[i][t] = lax.ppermute(send, line_axes[i], (even, odd)[i])
         at = len(sends)
         for store, masks in held_now:
             tie(store, masks, ready[at:at + len(masks)])

time: 183 us -> 173 us (0.945)
  starting transfers between devices: 49.6 us -> 42.7 us
  matrix products: 18.6 us -> 16.1 us
  other arithmetic: 17.1 us -> 14.8 us
    ppermute x12, starting transfers between devices: 24.2 us -> 12.2 us  [the longest x10 12.2 us: per_device(): (by_even, by_odd)[i][t] = lax.ppermute(send, line_axes[i], (even, odd)[i])]
    ppermute x3, waiting for transfers between devices: 18.7 us -> 10.2 us  [line_step(): by_even[step] = lax.ppermute(by_odd[step - 1], 'col', even)]
    ppermute x12, waiting for transfers between devices: 35.6 us -> 40.9 us  [the longest x10 40.9 us: per_device(): (by_even, by_odd)[i][t] = lax.ppermute(send, line_axes[i], (even, odd)[i])]
    ppermute x9, waiting for transfers between devices: 7.9 us -> 12.7 us  [row_step(): return lax.ppermute(x, ('rep', 'row'), pairs)]
    ppermute x3, starting transfers between devices: 9.19 us -> 13.4 us  [line_step(): by_even[step] = lax.ppermute(by_odd[step - 1], 'col', even)]
    unnamed x56 -> x66, local copies, waits for them, and re-layouts: 10.2 us -> 13 us
    dot_general x8, matrix products: 15.7 us -> 13.2 us  [dot(): return jnp.dot(x, w, preferred_element_type=f32)]
    dynamic_slice x2 -> x0, local copies, waits for them, and re-layouts: 2.39 us -> none  [per_device(): lax.dynamic_slice_in_dim(w, core * half, half, 0)]
  transfers between devices with their start and end apart: 34 -> 34, of which waited for: 13 -> 14; matrix products, arithmetic and copies ran while one was open for 26% -> 23% of each run, Pallas kernels for 3% -> 3%
where the time goes in v4:
time: 173 us; the launch traced here: 172 us
  waiting for transfers between devices  65.4 us (38%)
  starting transfers between devices  42.7 us (25%)
  matrix products  16.1 us (9%)
  local copies, waits for them, and re-layouts  15.2 us (9%)
  other arithmetic  14.8 us (9%)
  Pallas kernels  9.19 us (5%)
  between operations  8.74 us (5%)
    ppermute x10, waiting for transfers between devices, per_device(): (by_even, by_odd)[i][t] = lax.ppermute(send, line_axes[i], (even, odd)[i])  40.9 us
    ppermute x9, starting transfers between devices, row_step(): return lax.ppermute(x, ('rep', 'row'), pairs)  13.9 us
    ppermute x3, starting transfers between devices, line_step(): by_even[step] = lax.ppermute(by_odd[step - 1], 'col', even)  13.4 us
    dot_general x8, matrix products, dot(): return jnp.dot(x, w, preferred_element_type=f32)  13.2 us
    unnamed x66, local copies, waits for them, and re-layouts  13 us
    ppermute x9, waiting for transfers between devices, row_step(): return lax.ppermute(x, ('rep', 'row'), pairs)  12.7 us
    ppermute x10, starting transfers between devices, per_device(): (by_even, by_odd)[i][t] = lax.ppermute(send, line_axes[i], (even, odd)[i])  12.2 us
    ppermute x3, waiting for transfers between devices, line_step(): by_even[step] = lax.ppermute(by_odd[step - 1], 'col', even)  10.2 us
  transfers between devices with their start and end apart: 34, of which 14 were waited for; matrix products, arithmetic and copies ran while one was open for 23% of the time, Pallas kernels for 3%

profile of v4, /device:TPU:0, one launch (start us, length us, event | category | flops | bytes accessed | tf_op | source)
XLA Modules:
  0.0 172.1 jit_solution(1035132873269082482)
XLA Ops:
  4.0 1.9 %shard_map.122 = bf16[512,1536]{1,0:T(8,128)(2,1)} custom-call(s32[1]{0:T(128)} %bitcast.2.core_ref, bf16[512,1536]{1,0:T(8,128)(2,1)S(1)} %copy-done.5, bf16[512,1536]{1,0:T(8,128)(2,1)S(1)} %copy-done.7), custom_call_target="tpu_custom_call" | custom-call | bytes 3145728 | tf_op jit(solution)/shard_map/pallas_call | solution.py:65
  5.9 2.6 %collective-permute-start.2 = (bf16[512,1536]{1,0:T(8,128)(2,1)}, bf16[512,1536]{1,0:T(8,128)(2,1)}, u32[]{:S(2)}, u32[]{:S(2)}) collective-permute-start(bf16[512,1536]{1,0:T(8,128)(2,1)} %shard_map.122), channel_id=1, source_target_pairs={{0,4},{4,0},{8,12},{12,8},{16,24},{20,28},{24,16},{28,20},{1,5},{5... | collective-permute-start | bytes 4718600 | tf_op jit(solution)/shard_map/ppermute | solution.py:41
  10.1 2.9 %bitcast_dynamic-update-slice_fusion.5 = (bf16[6,512,512]{2,1,0:T(8,128)(2,1)}, bf16[512,512]{1,0:T(8,128)(2,1)}) fusion(bf16[512,512]{1,0:T(8,128)(2,1)} %collective-permute-done, bf16[512,512]{1,0:T(8,128)(2,1)} %param.11, s32[512]{0:T(512)S(1)} %fusion.75), kind=kOutput, calls=%fused_computation.126 | convolution fusion | flops 539754496 | bytes 2099200 | tf_op jit(solution)/shard_map/dot_general | solution.py:166
  22.9 4.2 %collective-permute-done.1 = bf16[512,512]{1,0:T(8,128)(2,1)} collective-permute-done((bf16[512,512]{1,0:T(8,128)(2,1)}, bf16[512,512]{1,0:T(8,128)(2,1)}, u32[]{:S(2)}, u32[]{:S(2)}) %collective-permute-start.1) | collective-permute-done | bytes 524320 | tf_op jit(solution)/shard_map/ppermute | solution.py:176
  27.0 3.2 %collective-permute-start.5 = (bf16[512,512]{1,0:T(8,128)(2,1)}, bf16[512,512]{1,0:T(8,128)(2,1)S(1)}, u32[]{:S(2)}, u32[]{:S(2)}) collective-permute-start(bf16[512,512]{1,0:T(8,128)(2,1)} %collective-permute-done.4), channel_id=1, source_target_pairs={{0,1},{1,0},{2,3},{3,2},{4,5},{5,4},{6,7},{7,6},{8,9},{9,8},{10,11... | collective-permute-start | bytes 1572872 | tf_op jit(solution)/shard_map/ppermute | solution.py:176
  32.9 8.7 %collective-permute-start.7 = (bf16[512,512]{1,0:T(8,128)(2,1)S(1)}, bf16[512,512]{1,0:T(8,128)(2,1)S(1)}, u32[]{:S(2)}, u32[]{:S(2)}) collective-permute-start(bf16[512,512]{1,0:T(8,128)(2,1)S(1)} %collective-permute-done.6), channel_id=1, source_target_pairs={{0,1},{1,0},{2,3},{3,2},{4,5},{5,4},{6,7},{7,6},{8,9},{9,8},{10,11... | collective-permute-start | bytes 1572872 | tf_op jit(solution)/shard_map/ppermute | solution.py:176
  47.7 5.1 %collective-permute-done.7 = bf16[512,512]{1,0:T(8,128)(2,1)S(1)} collective-permute-done((bf16[512,512]{1,0:T(8,128)(2,1)S(1)}, bf16[512,512]{1,0:T(8,128)(2,1)S(1)}, u32[]{:S(2)}, u32[]{:S(2)}) %collective-permute-start.7) | collective-permute-done | bytes 524320 | tf_op jit(solution)/shard_map/ppermute | solution.py:176
  56.0 8.5 %collective-permute-done.8 = bf16[512,1536]{1,0:T(8,128)(2,1)S(1)} collective-permute-done((bf16[512,1536]{1,0:T(8,128)(2,1)}, bf16[512,1536]{1,0:T(8,128)(2,1)S(1)}, u32[]{:S(2)}, u32[]{:S(2)}) %collective-permute-start.8) | collective-permute-done | bytes 1572896 | tf_op jit(solution)/shard_map/ppermute | solution.py:41
  73.4 2.6 %convolution_add_fusion.1 = f32[512,1536]{1,0:T(8,128)S(1)} fusion(f32[512,1536]{1,0:T(8,128)S(1)} %fusion.1, bf16[512,1536]{1,0:T(8,128)(2,1)S(1)} %select_dynamic-update-slice_fusion, bf16[1536,1536]{1,0:T(8,128)(2,1)S(1)} %get-tuple-element.109), kind=kOutput, calls=%fused_computation.1 | convolution fusion | flops 2416705536 | bytes 12582912 | tf_op jit(solution)/shard_map/dot_general | solution.py:214
  76.1 2.8 %multiply_convert_fusion = bf16[512,1536]{1,0:T(8,128)(2,1)S(1)} fusion(f32[512,1536]{1,0:T(8,128)S(1)} %convolution_add_fusion.1, f32[512,1536]{1,0:T(8,128)S(1)} %fusion.5, bf16[512,1536]{1,0:T(8,128)(2,1)S(1)} %select_dynamic-update-slice_fusion, bf16[1536,1536]{1,0:T(8,128)(2,1)S(1)} %get-tuple-element.110), kind=kOutput, calls=%fused_computation.2 | convolution fusion | flops 2420637696 | bytes 14155776 | tf_op jit(solution)/shard_map/dot_general | solution.py:214
  81.5 2.8 %collective-permute-done.12 = bf16[768,512]{1,0:T(8,128)(2,1)S(1)} collective-permute-done((bf16[768,512]{1,0:T(8,128)(2,1)S(1)}, bf16[768,512]{1,0:T(8,128)(2,1)S(1)}, u32[]{:S(2)}, u32[]{:S(2)}) %collective-permute-start.12) | collective-permute-done | bytes 786464 | tf_op jit(solution)/shard_map/ppermute | solution.py:41
  86.0 7.9 %collective-permute-done.15 = bf16[512,512]{1,0:T(8,128)(2,1)S(1)} collective-permute-done((bf16[512,512]{1,0:T(8,128)(2,1)S(1)}, bf16[512,512]{1,0:T(8,128)(2,1)S(1)}, u32[]{:S(2)}, u32[]{:S(2)}) %collective-permute-start.15) | collective-permute-done | bytes 524320 | tf_op jit(solution)/shard_map/ppermute | solution.py:334
  101.7 8.7 %collective-permute-done.19 = bf16[512,512]{1,0:T(8,128)(2,1)} collective-permute-done((bf16[512,512]{1,0:T(8,128)(2,1)S(1)}, bf16[512,512]{1,0:T(8,128)(2,1)}, u32[]{:S(2)}, u32[]{:S(2)}) %collective-permute-start.19) | collective-permute-done | bytes 524320 | tf_op jit(solution)/shard_map/ppermute | solution.py:334
  110.4 2.0 %fusion.34 = bf16[512,512]{1,0:T(8,128)(2,1)} fusion(bf16[512,512]{1,0:T(8,128)(2,1)S(1)} %fusion.28, bf16[512,512]{1,0:T(8,128)(2,1)} %collective-permute-done.19), kind=kLoop, calls=%fused_computation.68 | loop fusion | flops 1048576 | bytes 1572864 | tf_op jit(solution)/shard_map/convert_element_type | solution.py:323
  112.4 2.1 %add_convert_fusion.1 = bf16[512,512]{1,0:T(8,128)(2,1)} fusion(bf16[512,512]{1,0:T(8,128)(2,1)} %collective-permute-done.18, bf16[512,512]{1,0:T(8,128)(2,1)S(1)} %convolution_convert_fusion, bf16[512,512]{1,0:T(8,128)(2,1)S(1)} %fusion.25, pred[]{:T(512)S(6)} %or.4, pred[]{:T(512)S(6)} %eq.36), kind=kLoop, calls=%fused_computation.107 | loop fusion | flops 1572864 | bytes 2097154 | tf_op jit(solution)/shard_map/convert_element_type | solution.py:323
  118.7 2.9 %fusion.22 = bf16[512,512]{1,0:T(8,128)(2,1)S(1)} fusion(bf16[768,512]{1,0:T(8,128)(2,1)} %collective-permute-done.20, bf16[768,512]{1,0:T(8,128)(2,1)} %collective-permute-done.16, bf16[512,768]{1,0:T(8,128)(2,1)} %copy-done.24, bf16[512,768]{1,0:T(8,128)(2,1)} %copy-done.23), kind=kOutput, calls=%fused_computation.62 | convolution fusion | flops 811859968 | bytes 3670016 | tf_op jit(solution)/shard_map/dot_general | solution.py:214
  121.6 5.5 %collective-permute-done.23 = bf16[512,512]{1,0:T(8,128)(2,1)} collective-permute-done((bf16[512,512]{1,0:T(8,128)(2,1)}, bf16[512,512]{1,0:T(8,128)(2,1)}, u32[]{:S(2)}, u32[]{:S(2)}) %collective-permute-start.23) | collective-permute-done | bytes 524320 | tf_op jit(solution)/shard_map/ppermute | solution.py:334
  128.6 2.3 %collective-permute-start.27 = (bf16[512,512]{1,0:T(8,128)(2,1)S(1)}, bf16[512,512]{1,0:T(8,128)(2,1)S(1)}, u32[]{:S(2)}, u32[]{:S(2)}) collective-permute-start(bf16[512,512]{1,0:T(8,128)(2,1)S(1)} %add_convert_fusion), channel_id=1, source_target_pairs={{0,1},{1,0},{2,3},{3,2},{4,5},{5,4},{6,7},{7,6},{8,9},{9,8},{10,11... | collective-permute-start | bytes 1572872 | tf_op jit(solution)/shard_map/ppermute | solution.py:334
  133.5 7.1 %collective-permute-done.27 = bf16[512,512]{1,0:T(8,128)(2,1)S(1)} collective-permute-done((bf16[512,512]{1,0:T(8,128)(2,1)S(1)}, bf16[512,512]{1,0:T(8,128)(2,1)S(1)}, u32[]{:S(2)}, u32[]{:S(2)}) %collective-permute-start.27) | collective-permute-done | bytes 524320 | tf_op jit(solution)/shard_map/ppermute | solution.py:334
  140.9 4.5 %collective-permute-start.31 = (bf16[512,512]{1,0:T(8,128)(2,1)S(1)}, bf16[512,512]{1,0:T(8,128)(2,1)S(1)}, u32[]{:S(2)}, u32[]{:S(2)}) collective-permute-start(bf16[512,512]{1,0:T(8,128)(2,1)S(1)} %fusion.50), channel_id=1, source_target_pairs={{0,1},{1,0},{2,3},{3,2},{4,5},{5,4},{6,7},{7,6},{8,9},{9,8},{10,11... | collective-permute-start | bytes 1572872 | tf_op jit(solution)/shard_map/ppermute | solution.py:334
  147.1 2.2 %shard_map.123.refs_4_ = f32[512,1024]{1,0:T(8,128)S(1)} custom-call(s32[2]{0:T(128)S(1)} %pad_add_fusion.at_ref, bf16[512,256]{1,0:T(8,128)(2,1)S(1)} %get-tuple-element.130.refs_0_, bf16[512,256]{1,0:T(8,128)(2,1)S(1)} %get-tuple-element.129.refs_1_, bf16[512,256]{1,0:T(8,128)(2,1)S(1)} %get-tuple-element.128.refs_2_, ...), custom_call_target="tpu_custom_call" | custom-call | flops 1073741824 | bytes 7340032 | tf_op jit(solution)/shard_map/pallas_call | solution.py:120
  149.5 5.9 %collective-permute-done.31 = bf16[512,512]{1,0:T(8,128)(2,1)S(1)} collective-permute-done((bf16[512,512]{1,0:T(8,128)(2,1)S(1)}, bf16[512,512]{1,0:T(8,128)(2,1)S(1)}, u32[]{:S(2)}, u32[]{:S(2)}) %collective-permute-start.31) | collective-permute-done | bytes 524320 | tf_op jit(solution)/shard_map/ppermute | solution.py:334
  160.6 5.8 %collective-permute-done.32 = bf16[512,512]{1,0:T(8,128)(2,1)S(1)} collective-permute-done((bf16[512,512]{1,0:T(8,128)(2,1)S(1)}, bf16[512,512]{1,0:T(8,128)(2,1)S(1)}, u32[]{:S(2)}, u32[]{:S(2)}) %collective-permute-start.32) | collective-permute-done | bytes 524320 | tf_op jit(solution)/shard_map/ppermute | solution.py:334
  168.8 3.3 %shard_map.125 = (bf16[512,1024]{1,0:T(8,128)(2,1)}, bf16[512,512]{1,0:T(8,128)(2,1)}) custom-call(s32[2]{0:T(128)S(1)} %pad_add_fusion.at_ref, bf16[512,256]{1,0:T(8,128)(2,1)S(1)} %get-tuple-element.126.refs_0_, bf16[512,256]{1,0:T(8,128)(2,1)S(1)} %get-tuple-element.125.refs_1_, bf16[256,1024]{1,0:T(8,128)(2,1)S(1)} %collective-permute-done.28.refs_2_, ...), custom_call_target="tpu_custom_call" | custom-call | flops 536870912 | bytes 5767168 | tf_op jit(solution)/shard_map/pallas_call | solution.py:120
  (167 shorter events, 57.9 us)
Async XLA Ops:
  5.9 37.1 %collective-permute-start.2 = (bf16[512,1536]{1,0:T(8,128)(2,1)}, bf16[512,1536]{1,0:T(8,128)(2,1)}, u32[]{:S(2)}, u32[]{:S(2)}) collective-permute-start(bf16[512,1536]{1,0:T(8,128)(2,1)} %shard_map.122), channel_id=1, source_target_pairs={{0,4},{4,0},{8,12},{12,8},{16,24},{20,28},{24,16},{28,20},{1,5},{5... | collective-permute-start | bytes 4718600 | tf_op jit(solution)/shard_map/ppermute | solution.py:41
  8.6 35.3 %collective-permute-start.3 = (bf16[512,1536]{1,0:T(8,128)(2,1)}, bf16[512,1536]{1,0:T(8,128)(2,1)}, u32[]{:S(2)}, u32[]{:S(2)}) collective-permute-start(bf16[512,1536]{1,0:T(8,128)(2,1)} %shard_map.122), channel_id=1, source_target_pairs={{0,8},{4,12},{8,0},{12,4},{16,20},{20,16},{24,28},{28,24},{1,9},{5... | collective-permute-start | bytes 4718600 | tf_op jit(solution)/shard_map/ppermute | solution.py:41
  13.0 14.0 %collective-permute-start.1 = (bf16[512,512]{1,0:T(8,128)(2,1)}, bf16[512,512]{1,0:T(8,128)(2,1)}, u32[]{:S(2)}, u32[]{:S(2)}) collective-permute-start(bf16[512,512]{1,0:T(8,128)(2,1)} %get-tuple-element.146), channel_id=1, source_target_pairs={{0,1},{1,0},{2,3},{3,2},{4,5},{5,4},{6,7},{7,6},{8,9},{9,8},{10,11... | collective-permute-start | bytes 1572872 | tf_op jit(solution)/shard_map/ppermute | solution.py:176
  14.6 12.4 %collective-permute-start.4 = (bf16[512,512]{1,0:T(8,128)(2,1)}, bf16[512,512]{1,0:T(8,128)(2,1)}, u32[]{:S(2)}, u32[]{:S(2)}) collective-permute-start(bf16[512,512]{1,0:T(8,128)(2,1)} %get-tuple-element.146), channel_id=1, source_target_pairs={{1,2},{2,1},{17,18},{18,17},{0,16},{3,19},{16,0},{19,3},{5,6},{6,5... | collective-permute-start | bytes 1572872 | tf_op jit(solution)/shard_map/ppermute | solution.py:178
  27.0 15.5 %collective-permute-start.5 = (bf16[512,512]{1,0:T(8,128)(2,1)}, bf16[512,512]{1,0:T(8,128)(2,1)S(1)}, u32[]{:S(2)}, u32[]{:S(2)}) collective-permute-start(bf16[512,512]{1,0:T(8,128)(2,1)} %collective-permute-done.4), channel_id=1, source_target_pairs={{0,1},{1,0},{2,3},{3,2},{4,5},{5,4},{6,7},{7,6},{8,9},{9,8},{10,11... | collective-permute-start | bytes 1572872 | tf_op jit(solution)/shard_map/ppermute | solution.py:176
  32.9 19.9 %collective-permute-start.7 = (bf16[512,512]{1,0:T(8,128)(2,1)S(1)}, bf16[512,512]{1,0:T(8,128)(2,1)S(1)}, u32[]{:S(2)}, u32[]{:S(2)}) collective-permute-start(bf16[512,512]{1,0:T(8,128)(2,1)S(1)} %collective-permute-done.6), channel_id=1, source_target_pairs={{0,1},{1,0},{2,3},{3,2},{4,5},{5,4},{6,7},{7,6},{8,9},{9,8},{10,11... | collective-permute-start | bytes 1572872 | tf_op jit(solution)/shard_map/ppermute | solution.py:176
  43.8 20.6 %collective-permute-start.8 = (bf16[512,1536]{1,0:T(8,128)(2,1)}, bf16[512,1536]{1,0:T(8,128)(2,1)S(1)}, u32[]{:S(2)}, u32[]{:S(2)}) collective-permute-start(bf16[512,1536]{1,0:T(8,128)(2,1)} %collective-permute-done.2), channel_id=1, source_target_pairs={{0,8},{4,12},{8,0},{12,4},{16,20},{20,16},{24,28},{28,24},{1,9},{5... | collective-permute-start | bytes 4718600 | tf_op jit(solution)/shard_map/ppermute | solution.py:41
  45.7 24.0 %collective-permute-start.10 = (bf16[512,1536]{1,0:T(8,128)(2,1)}, bf16[512,1536]{1,0:T(8,128)(2,1)S(1)}, u32[]{:S(2)}, u32[]{:S(2)}) collective-permute-start(bf16[512,1536]{1,0:T(8,128)(2,1)} %collective-permute-done.2), channel_id=1, source_target_pairs={{0,16},{16,0},{1,17},{17,1},{2,18},{18,2},{3,19},{19,3},{4,20},{20... | collective-permute-start | bytes 4718600 | tf_op jit(solution)/shard_map/ppermute | solution.py:19
  45.9 22.2 %collective-permute-start.9 = (bf16[512,1536]{1,0:T(8,128)(2,1)}, bf16[512,1536]{1,0:T(8,128)(2,1)S(1)}, u32[]{:S(2)}, u32[]{:S(2)}) collective-permute-start(bf16[512,1536]{1,0:T(8,128)(2,1)} %collective-permute-done.3), channel_id=1, source_target_pairs={{0,16},{16,0},{1,17},{17,1},{2,18},{18,2},{3,19},{19,3},{4,20},{20... | collective-permute-start | bytes 4718600 | tf_op jit(solution)/shard_map/ppermute | solution.py:19
  64.5 19.9 %collective-permute-start.12 = (bf16[768,512]{1,0:T(8,128)(2,1)S(1)}, bf16[768,512]{1,0:T(8,128)(2,1)S(1)}, u32[]{:S(2)}, u32[]{:S(2)}) collective-permute-start(bf16[768,512]{1,0:T(8,128)(2,1)S(1)} %constant_dynamic-slice_fusion.5), channel_id=1, source_target_pairs={{0,4},{4,0},{8,12},{12,8},{16,24},{20,28},{24,16},{28,20},{1,5},{5... | collective-permute-start | bytes 2359304 | tf_op jit(solution)/shard_map/ppermute | solution.py:41
  66.2 18.2 %collective-permute-start.13 = (bf16[768,512]{1,0:T(8,128)(2,1)S(1)}, bf16[768,512]{1,0:T(8,128)(2,1)S(1)}, u32[]{:S(2)}, u32[]{:S(2)}) collective-permute-start(bf16[768,512]{1,0:T(8,128)(2,1)S(1)} %constant_dynamic-slice_fusion.5), channel_id=1, source_target_pairs={{0,8},{4,12},{8,0},{12,4},{16,20},{20,16},{24,28},{28,24},{1,9},{5... | collective-permute-start | bytes 2359304 | tf_op jit(solution)/shard_map/ppermute | solution.py:41
  79.9 14.0 %collective-permute-start.15 = (bf16[512,512]{1,0:T(8,128)(2,1)S(1)}, bf16[512,512]{1,0:T(8,128)(2,1)S(1)}, u32[]{:S(2)}, u32[]{:S(2)}) collective-permute-start(bf16[512,512]{1,0:T(8,128)(2,1)S(1)} %convolution_convert_fusion), channel_id=1, source_target_pairs={{0,1},{1,0},{2,3},{3,2},{4,5},{5,4},{6,7},{7,6},{8,9},{9,8},{10,11... | collective-permute-start | bytes 1572872 | tf_op jit(solution)/shard_map/ppermute | solution.py:334
  84.4 11.6 %collective-permute-start.14 = (bf16[768,512]{1,0:T(8,128)(2,1)S(1)}, bf16[768,512]{1,0:T(8,128)(2,1)S(1)}, u32[]{:S(2)}, u32[]{:S(2)}) collective-permute-start(bf16[768,512]{1,0:T(8,128)(2,1)S(1)} %collective-permute-done.13), channel_id=1, source_target_pairs={{0,16},{16,0},{1,17},{17,1},{2,18},{18,2},{3,19},{19,3},{4,20},{20... | collective-permute-start | bytes 2359304 | tf_op jit(solution)/shard_map/ppermute | solution.py:19
  84.9 12.1 %collective-permute-start.16 = (bf16[768,512]{1,0:T(8,128)(2,1)S(1)}, bf16[768,512]{1,0:T(8,128)(2,1)}, u32[]{:S(2)}, u32[]{:S(2)}) collective-permute-start(bf16[768,512]{1,0:T(8,128)(2,1)S(1)} %collective-permute-done.12), channel_id=1, source_target_pairs={{0,8},{4,12},{8,0},{12,4},{16,20},{20,16},{24,28},{28,24},{1,9},{5... | collective-permute-start | bytes 2359304 | tf_op jit(solution)/shard_map/ppermute | solution.py:41
  97.0 13.4 %collective-permute-start.19 = (bf16[512,512]{1,0:T(8,128)(2,1)S(1)}, bf16[512,512]{1,0:T(8,128)(2,1)}, u32[]{:S(2)}, u32[]{:S(2)}) collective-permute-start(bf16[512,512]{1,0:T(8,128)(2,1)S(1)} %fusion.28), channel_id=1, source_target_pairs={{0,1},{1,0},{2,3},{3,2},{4,5},{5,4},{6,7},{7,6},{8,9},{9,8},{10,11... | collective-permute-start | bytes 1572872 | tf_op jit(solution)/shard_map/ppermute | solution.py:334
  98.8 13.6 %collective-permute-start.18 = (bf16[512,512]{1,0:T(8,128)(2,1)}, bf16[512,512]{1,0:T(8,128)(2,1)}, u32[]{:S(2)}, u32[]{:S(2)}) collective-permute-start(bf16[512,512]{1,0:T(8,128)(2,1)} %fusion.31), channel_id=1, source_target_pairs={{1,2},{2,1},{17,18},{18,17},{0,16},{3,19},{16,0},{19,3},{5,6},{6,5... | collective-permute-start | bytes 1572872 | tf_op jit(solution)/shard_map/ppermute | solution.py:334
  98.8 15.6 %collective-permute-start.20 = (bf16[768,512]{1,0:T(8,128)(2,1)}, bf16[768,512]{1,0:T(8,128)(2,1)}, u32[]{:S(2)}, u32[]{:S(2)}) collective-permute-start(bf16[768,512]{1,0:T(8,128)(2,1)} %collective-permute-done.16), channel_id=1, source_target_pairs={{0,16},{16,0},{1,17},{17,1},{2,18},{18,2},{3,19},{19,3},{4,20},{20... | collective-permute-start | bytes 2359304 | tf_op jit(solution)/shard_map/ppermute | solution.py:19
  100.2 14.3 %collective-permute-start.21 = (bf16[256,1024]{1,0:T(8,128)(2,1)}, bf16[256,1024]{1,0:T(8,128)(2,1)S(1)}, u32[]{:S(2)}, u32[]{:S(2)}) collective-permute-start(bf16[256,1024]{1,0:T(8,128)(2,1)} %constant_dynamic-slice_fusion.4), channel_id=1, source_target_pairs={{0,4},{4,0},{8,12},{12,8},{16,24},{20,28},{24,16},{28,20},{1,5},{5... | collective-permute-start | bytes 1572872 | tf_op jit(solution)/shard_map/ppermute | solution.py:41
  114.4 12.7 %collective-permute-start.23 = (bf16[512,512]{1,0:T(8,128)(2,1)}, bf16[512,512]{1,0:T(8,128)(2,1)}, u32[]{:S(2)}, u32[]{:S(2)}) collective-permute-start(bf16[512,512]{1,0:T(8,128)(2,1)} %add_convert_fusion.1), channel_id=1, source_target_pairs={{0,1},{1,0},{2,3},{3,2},{4,5},{5,4},{6,7},{7,6},{8,9},{9,8},{10,11... | collective-permute-start | bytes 1572872 | tf_op jit(solution)/shard_map/ppermute | solution.py:334
  116.1 12.5 %collective-permute-start.24 = (bf16[256,1024]{1,0:T(8,128)(2,1)}, bf16[256,1024]{1,0:T(8,128)(2,1)S(1)}, u32[]{:S(2)}, u32[]{:S(2)}) collective-permute-start(bf16[256,1024]{1,0:T(8,128)(2,1)} %constant_dynamic-slice_fusion.4), channel_id=1, source_target_pairs={{0,8},{4,12},{8,0},{12,4},{16,20},{20,16},{24,28},{28,24},{1,9},{5... | collective-permute-start | bytes 1572872 | tf_op jit(solution)/shard_map/ppermute | solution.py:41
  117.6 23.1 %collective-permute-start.28 = (bf16[256,1024]{1,0:T(8,128)(2,1)S(1)}, bf16[256,1024]{1,0:T(8,128)(2,1)S(1)}, u32[]{:S(2)}, u32[]{:S(2)}) collective-permute-start(bf16[256,1024]{1,0:T(8,128)(2,1)S(1)} %collective-permute-done.21.refs_6_), channel_id=1, source_target_pairs={{0,8},{4,12},{8,0},{12,4},{16,20},{20,16},{24,28},{28,24},{1,9},{5... | collective-permute-start | bytes 1572872 | tf_op jit(solution)/shard_map/ppermute | solution.py:41
  128.6 12.0 %collective-permute-start.27 = (bf16[512,512]{1,0:T(8,128)(2,1)S(1)}, bf16[512,512]{1,0:T(8,128)(2,1)S(1)}, u32[]{:S(2)}, u32[]{:S(2)}) collective-permute-start(bf16[512,512]{1,0:T(8,128)(2,1)S(1)} %add_convert_fusion), channel_id=1, source_target_pairs={{0,1},{1,0},{2,3},{3,2},{4,5},{5,4},{6,7},{7,6},{8,9},{9,8},{10,11... | collective-permute-start | bytes 1572872 | tf_op jit(solution)/shard_map/ppermute | solution.py:334
  140.9 14.5 %collective-permute-start.31 = (bf16[512,512]{1,0:T(8,128)(2,1)S(1)}, bf16[512,512]{1,0:T(8,128)(2,1)S(1)}, u32[]{:S(2)}, u32[]{:S(2)}) collective-permute-start(bf16[512,512]{1,0:T(8,128)(2,1)S(1)} %fusion.50), channel_id=1, source_target_pairs={{0,1},{1,0},{2,3},{3,2},{4,5},{5,4},{6,7},{7,6},{8,9},{9,8},{10,11... | collective-permute-start | bytes 1572872 | tf_op jit(solution)/shard_map/ppermute | solution.py:334
  145.3 22.0 %collective-permute-start.33 = (bf16[256,1024]{1,0:T(8,128)(2,1)S(1)}, bf16[256,1024]{1,0:T(8,128)(2,1)}, u32[]{:S(2)}, u32[]{:S(2)}) collective-permute-start(bf16[256,1024]{1,0:T(8,128)(2,1)S(1)} %collective-permute-done.28.refs_2_), channel_id=1, source_target_pairs={{0,16},{16,0},{1,17},{17,1},{2,18},{18,2},{3,19},{19,3},{4,20},{20... | collective-permute-start | bytes 1572872 | tf_op jit(solution)/shard_map/ppermute | solution.py:19
  (39 other events, 402.5 us)

commit v5 on v4

--- a/solution.py
+++ b/solution.py
@@ -52,24 +52,26 @@
     return next(t for t in (512, 256, 128, n) if n % t == 0)
 
 
-def halves_kernel(core_ref, top_ref, bottom_ref, out_ref):
-    half = top_ref.shape[0]
-    out_ref[:half] = top_ref[...]
-    out_ref[half:] = bottom_ref[...]
+def halves_kernel(core_ref, top_ref, bottom_ref, out_ref, sems):
+    half = top_ref.shape[0] // 2
+    rows = pl.ds(pl.multiple_of(core_ref[0] * half, half), half)
+    first = pltpu.make_async_copy(top_ref.at[rows], out_ref.at[pl.ds(0, half)], sems.at[0])
+    second = pltpu.make_async_copy(bottom_ref.at[rows], out_ref.at[pl.ds(half, half)], sems.at[1])
+    first.start()
+    second.start()
+    first.wait()
+    second.wait()
 
 
 def core_halves(core, top, bottom):
-    half, width = top.shape[0] // 2, top.shape[1]
-    tn = next(t for t in (512, 384, 128, width) if width % t == 0)
-    piece = pl.BlockSpec((half, tn), lambda i, c: (c[0], i))
+    anywhere = pl.BlockSpec(memory_space=pl.ANY)
     return pl.pallas_call(
         halves_kernel,
-        grid_spec=pltpu.PrefetchScalarGridSpec(
-            num_scalar_prefetch=1, grid=(width // tn,), in_specs=[piece, piece],
-            out_specs=pl.BlockSpec((2 * half, tn), lambda i, c: (0, i))),
-        out_shape=jax.ShapeDtypeStruct((2 * half, width), bf16),
-        compiler_params=pltpu.CompilerParams(vmem_limit_bytes=VMEM_LIMIT),
-        cost_estimate=pl.CostEstimate(flops=0, bytes_accessed=8 * half * width, transcendentals=0),
+        in_specs=[pl.BlockSpec(memory_space=pltpu.SMEM), anywhere, anywhere],
+        out_specs=pl.BlockSpec(memory_space=pltpu.VMEM),
+        out_shape=jax.ShapeDtypeStruct(top.shape, bf16),
+        scratch_shapes=[pltpu.SemaphoreType.DMA((2,))],
+        cost_estimate=pl.CostEstimate(flops=0, bytes_accessed=4 * top.size, transcendentals=0),
     )(core, top, bottom)
 
 
@@ -217,11 +219,7 @@
     columns = [jnp.concatenate([normed(m) for m in ms], axis=1) for ms in (early, late)]
 
     w_down_half = lax.dynamic_slice_in_dim(w_down, core * ff_half, ff_half, 0)
-    ready = barrier(tuple(gu[m] for m in relayed) + tuple(columns) + (w_down_half,))
-    for m, value in zip(relayed, ready):
-        gu[m] = value
-    columns, w_down_half = ready[len(relayed):-1], ready[-1]
-    gu_other = {m: swap_cores(gu[m]) for m in frames[1:]}
+    gu_other = {m: swap_cores(gu[m]) for m in direct}
 
     def weights(n, masks):
         pieces, at = [], half * (n == "up")
@@ -230,11 +228,17 @@
         return jnp.concatenate(pieces, axis=0)
 
     w_qkv_half = lax.dynamic_slice_in_dim(w_qkv, core * half, half, 0)
+    gate_early, up_early = (dot(columns[0], weights(n, early)) for n in own)
+    ready = barrier(tuple(gu[m] for m in relayed) + (gate_early, up_early, columns[1], w_down_half))
+    for m, value in zip(relayed, ready):
+        gu[m] = value
+        gu_other[m] = swap_cores(value)
+    gate_early, up_early, late_columns, w_down_half = ready[len(relayed):]
+    columns = (columns[0], late_columns)
     dn, dn_other, partial = {0: w_down_half}, {}, {}
     wq, wq_other = {0: w_qkv_half}, {}
     for m in direct:
         dn[m] = row_step(dn[0], bits_of(m))
-    gate_early, up_early = (dot(columns[0], weights(n, early)) for n in own)
     gate = gate_early + dot(columns[1], weights("gate", late))
     up_proj = up_early + dot(columns[1], weights("up", late))
     hidden = (gate / (1 + jnp.exp(-gate)) * up_proj).astype(bf16)
@@ -321,7 +325,7 @@
                     came = came.astype(f32)
                     send = send.astype(f32) + (jnp.where(at_end, 0, came) if i == 0 else came)
                 sends.append((i, first_sent if t == 0 else send.astype(bf16)))
-        held_now = {1: [(dn, relayed), (partial, [place_of[m] for m in direct])], 2: [(dn_other, relayed), (wq, direct[:1])],
+        held_now = {1: [(partial, [place_of[m] for m in direct])], 2: [(dn_other, relayed), (wq, direct[:1])],
                     3: [(wq, direct[1:]), (wq_other, direct[:1]), (partial, [place_of[m] for m in relayed])],
                     4: [(wq, relayed), (wq_other, direct[1:])]}.get(t, [])
         done = t - cols

time: 173 us -> 170 us (0.983)
  waiting for transfers between devices: 65.4 us -> 60.1 us
  local copies, waits for them, and re-layouts: 15.2 us -> 12.3 us
  other arithmetic: 14.8 us -> 17 us
    ppermute x10, waiting for transfers between devices: 40.9 us -> 33.4 us  [per_device(): (by_even, by_odd)[i][t] = lax.ppermute(send, line_axes[i], (even, odd)[i])]
    ppermute x9, waiting for transfers between devices: 12.7 us -> 16.3 us  [row_step(): return lax.ppermute(x, ('rep', 'row'), pairs)]
    unnamed x66 -> x50, local copies, waits for them, and re-layouts: 13 us -> 10.2 us
  transfers between devices with their start and end apart: 34 -> 34, of which waited for: 14 -> 16; matrix products, arithmetic and copies ran while one was open for 23% -> 26% of each run, Pallas kernels for 3% -> 4%
where the time goes in v5:
time: 170 us; the launch traced here: 169 us
  waiting for transfers between devices  60.1 us (35%)
  starting transfers between devices  43 us (25%)
  matrix products  17.7 us (10%)
  other arithmetic  17 us (10%)
  local copies, waits for them, and re-layouts  12.3 us (7%)
  Pallas kernels  10.2 us (6%)
  between operations  8.85 us (5%)
    ppermute x10, waiting for transfers between devices, per_device(): (by_even, by_odd)[i][t] = lax.ppermute(send, line_axes[i], (even, odd)[i])  33.4 us
    ppermute x9, waiting for transfers between devices, row_step(): return lax.ppermute(x, ('rep', 'row'), pairs)  16.3 us
    ppermute x9, starting transfers between devices, row_step(): return lax.ppermute(x, ('rep', 'row'), pairs)  14.9 us
    dot_general x8, matrix products, dot(): return jnp.dot(x, w, preferred_element_type=f32)  14.8 us
    ppermute x3, starting transfers between devices, line_step(): by_even[step] = lax.ppermute(by_odd[step - 1], 'col', even)  13.4 us
    ppermute x10, starting transfers between devices, per_device(): (by_even, by_odd)[i][t] = lax.ppermute(send, line_axes[i], (even, odd)[i])  12.1 us
    ppermute x3, waiting for transfers between devices, line_step(): by_even[step] = lax.ppermute(by_odd[step - 1], 'col', even)  10.3 us
    unnamed x50, local copies, waits for them, and re-layouts  10.2 us
  transfers between devices with their start and end apart: 34, of which 16 were waited for; matrix products, arithmetic and copies ran while one was open for 26% of the time, Pallas kernels for 4%

profile of v5, /device:TPU:0, one launch (start us, length us, event | category | flops | bytes accessed | tf_op | source)
XLA Modules:
  0.0 169.3 jit_solution(10766398695519460841)
XLA Ops:
  1.2 2.6 %shard_map.122 = bf16[512,1536]{1,0:T(8,128)(2,1)} custom-call(s32[1]{0:T(128)} %bitcast.2.core_ref, bf16[512,1536]{1,0:T(8,128)(2,1)} %top_ref.1, bf16[512,1536]{1,0:T(8,128)(2,1)} %bottom_ref.1), custom_call_target="tpu_custom_call" | custom-call | bytes 3145728 | tf_op jit(solution)/shard_map/pallas_call | solution.py:68
  3.8 2.7 %collective-permute-start.2 = (bf16[512,1536]{1,0:T(8,128)(2,1)}, bf16[512,1536]{1,0:T(8,128)(2,1)}, u32[]{:S(2)}, u32[]{:S(2)}) collective-permute-start(bf16[512,1536]{1,0:T(8,128)(2,1)} %shard_map.122), channel_id=1, source_target_pairs={{0,4},{4,0},{8,12},{12,8},{16,24},{20,28},{24,16},{28,20},{1,5},{5... | collective-permute-start | bytes 4718600 | tf_op jit(solution)/shard_map/ppermute | solution.py:41
  8.0 2.9 %bitcast_dynamic-update-slice_fusion.5 = (bf16[6,512,512]{2,1,0:T(8,128)(2,1)}, bf16[512,512]{1,0:T(8,128)(2,1)}) fusion(bf16[512,512]{1,0:T(8,128)(2,1)} %collective-permute-done, bf16[512,512]{1,0:T(8,128)(2,1)} %param.11, s32[512]{0:T(512)S(1)} %fusion.75), kind=kOutput, calls=%fused_computation.124 | convolution fusion | flops 539754496 | bytes 2099200 | tf_op jit(solution)/shard_map/dot_general | solution.py:168
  21.0 4.0 %collective-permute-done.1 = bf16[512,512]{1,0:T(8,128)(2,1)} collective-permute-done((bf16[512,512]{1,0:T(8,128)(2,1)}, bf16[512,512]{1,0:T(8,128)(2,1)}, u32[]{:S(2)}, u32[]{:S(2)}) %collective-permute-start.1) | collective-permute-done | bytes 524320 | tf_op jit(solution)/shard_map/ppermute | solution.py:178
  25.0 3.2 %collective-permute-start.5 = (bf16[512,512]{1,0:T(8,128)(2,1)}, bf16[512,512]{1,0:T(8,128)(2,1)S(1)}, u32[]{:S(2)}, u32[]{:S(2)}) collective-permute-start(bf16[512,512]{1,0:T(8,128)(2,1)} %collective-permute-done.4), channel_id=1, source_target_pairs={{0,1},{1,0},{2,3},{3,2},{4,5},{5,4},{6,7},{7,6},{8,9},{9,8},{10,11... | collective-permute-start | bytes 1572872 | tf_op jit(solution)/shard_map/ppermute | solution.py:178
  30.8 8.7 %collective-permute-start.7 = (bf16[512,512]{1,0:T(8,128)(2,1)S(1)}, bf16[512,512]{1,0:T(8,128)(2,1)S(1)}, u32[]{:S(2)}, u32[]{:S(2)}) collective-permute-start(bf16[512,512]{1,0:T(8,128)(2,1)S(1)} %collective-permute-done.6), channel_id=1, source_target_pairs={{0,1},{1,0},{2,3},{3,2},{4,5},{5,4},{6,7},{7,6},{8,9},{9,8},{10,11... | collective-permute-start | bytes 1572872 | tf_op jit(solution)/shard_map/ppermute | solution.py:178
  45.3 5.4 %collective-permute-done.7 = bf16[512,512]{1,0:T(8,128)(2,1)S(1)} collective-permute-done((bf16[512,512]{1,0:T(8,128)(2,1)S(1)}, bf16[512,512]{1,0:T(8,128)(2,1)S(1)}, u32[]{:S(2)}, u32[]{:S(2)}) %collective-permute-start.7) | collective-permute-done | bytes 524320 | tf_op jit(solution)/shard_map/ppermute | solution.py:178
  55.7 2.6 %fusion.94 = f32[512,1536]{1,0:T(8,128)S(1)} fusion(bf16[512,1536]{1,0:T(8,128)(2,1)S(1)} %select_dynamic-update-slice_fusion, bf16[1536,1536]{1,0:T(8,128)(2,1)S(1)} %get-tuple-element.113), kind=kOutput, calls=%fused_computation.177 | convolution fusion | flops 2415919104 | bytes 9437184 | tf_op jit(solution)/shard_map/dot_general | solution.py:216
  58.3 2.6 %fusion.93 = f32[512,1536]{1,0:T(8,128)S(1)} fusion(bf16[512,1536]{1,0:T(8,128)(2,1)S(1)} %select_dynamic-update-slice_fusion, bf16[1536,1536]{1,0:T(8,128)(2,1)S(1)} %get-tuple-element.114), kind=kOutput, calls=%fused_computation.176 | convolution fusion | flops 2415919104 | bytes 9437184 | tf_op jit(solution)/shard_map/dot_general | solution.py:216
  70.8 2.2 %collective-permute-start.15 = (bf16[512,512]{1,0:T(8,128)(2,1)S(1)}, bf16[512,512]{1,0:T(8,128)(2,1)S(1)}, u32[]{:S(2)}, u32[]{:S(2)}) collective-permute-start(bf16[512,512]{1,0:T(8,128)(2,1)S(1)} %convolution_convert_fusion), channel_id=1, source_target_pairs={{0,1},{1,0},{2,3},{3,2},{4,5},{5,4},{6,7},{7,6},{8,9},{9,8},{10,11... | collective-permute-start | bytes 1572872 | tf_op jit(solution)/shard_map/ppermute | solution.py:338
  73.0 9.4 %collective-permute-done.12 = bf16[768,512]{1,0:T(8,128)(2,1)S(1)} collective-permute-done((bf16[768,512]{1,0:T(8,128)(2,1)S(1)}, bf16[768,512]{1,0:T(8,128)(2,1)S(1)}, u32[]{:S(2)}, u32[]{:S(2)}) %collective-permute-start.12) | collective-permute-done | bytes 786464 | tf_op jit(solution)/shard_map/ppermute | solution.py:41
  91.9 3.4 %collective-permute-done.17 = bf16[768,512]{1,0:T(8,128)(2,1)} collective-permute-done((bf16[768,512]{1,0:T(8,128)(2,1)S(1)}, bf16[768,512]{1,0:T(8,128)(2,1)}, u32[]{:S(2)}, u32[]{:S(2)}) %collective-permute-start.17) | collective-permute-done | bytes 786464 | tf_op jit(solution)/shard_map/ppermute | solution.py:41
  98.3 6.4 %collective-permute-done.19 = bf16[512,512]{1,0:T(8,128)(2,1)} collective-permute-done((bf16[512,512]{1,0:T(8,128)(2,1)}, bf16[512,512]{1,0:T(8,128)(2,1)}, u32[]{:S(2)}, u32[]{:S(2)}) %collective-permute-start.19) | collective-permute-done | bytes 524320 | tf_op jit(solution)/shard_map/ppermute | solution.py:338
  104.7 2.1 %fusion.34 = bf16[512,512]{1,0:T(8,128)(2,1)} fusion(bf16[512,512]{1,0:T(8,128)(2,1)} %fusion.28, bf16[512,512]{1,0:T(8,128)(2,1)} %collective-permute-done.19), kind=kLoop, calls=%fused_computation.66 | loop fusion | flops 1048576 | bytes 1572864 | tf_op jit(solution)/shard_map/convert_element_type | solution.py:327
  106.8 2.2 %add_convert_fusion.1 = bf16[512,512]{1,0:T(8,128)(2,1)} fusion(bf16[512,512]{1,0:T(8,128)(2,1)} %collective-permute-done.18, bf16[512,512]{1,0:T(8,128)(2,1)} %copy-done.11, bf16[512,512]{1,0:T(8,128)(2,1)} %fusion.25, pred[]{:T(512)S(6)} %or.4, pred[]{:T(512)S(6)} %eq.36), kind=kLoop, calls=%fused_computation.105 | loop fusion | flops 1572864 | bytes 2097154 | tf_op jit(solution)/shard_map/convert_element_type | solution.py:327
  113.2 2.9 %fusion.22 = bf16[512,512]{1,0:T(8,128)(2,1)S(1)} fusion(bf16[768,512]{1,0:T(8,128)(2,1)} %collective-permute-done.20, bf16[768,512]{1,0:T(8,128)(2,1)} %collective-permute-done.17, bf16[512,768]{1,0:T(8,128)(2,1)} %copy-done.16, bf16[512,768]{1,0:T(8,128)(2,1)} %copy-done.15), kind=kOutput, calls=%fused_computation.60 | convolution fusion | flops 811859968 | bytes 3670016 | tf_op jit(solution)/shard_map/dot_general | solution.py:216
  116.1 6.6 %collective-permute-done.23 = bf16[512,512]{1,0:T(8,128)(2,1)} collective-permute-done((bf16[512,512]{1,0:T(8,128)(2,1)}, bf16[512,512]{1,0:T(8,128)(2,1)}, u32[]{:S(2)}, u32[]{:S(2)}) %collective-permute-start.23) | collective-permute-done | bytes 524320 | tf_op jit(solution)/shard_map/ppermute | solution.py:338
  124.2 2.5 %collective-permute-start.27 = (bf16[512,512]{1,0:T(8,128)(2,1)S(1)}, bf16[512,512]{1,0:T(8,128)(2,1)S(1)}, u32[]{:S(2)}, u32[]{:S(2)}) collective-permute-start(bf16[512,512]{1,0:T(8,128)(2,1)S(1)} %add_convert_fusion), channel_id=1, source_target_pairs={{0,1},{1,0},{2,3},{3,2},{4,5},{5,4},{6,7},{7,6},{8,9},{9,8},{10,11... | collective-permute-start | bytes 1572872 | tf_op jit(solution)/shard_map/ppermute | solution.py:338
  129.5 7.8 %collective-permute-done.27 = bf16[512,512]{1,0:T(8,128)(2,1)S(1)} collective-permute-done((bf16[512,512]{1,0:T(8,128)(2,1)S(1)}, bf16[512,512]{1,0:T(8,128)(2,1)S(1)}, u32[]{:S(2)}, u32[]{:S(2)}) %collective-permute-start.27) | collective-permute-done | bytes 524320 | tf_op jit(solution)/shard_map/ppermute | solution.py:338
  137.5 3.7 %collective-permute-start.31 = (bf16[512,512]{1,0:T(8,128)(2,1)S(1)}, bf16[512,512]{1,0:T(8,128)(2,1)S(1)}, u32[]{:S(2)}, u32[]{:S(2)}) collective-permute-start(bf16[512,512]{1,0:T(8,128)(2,1)S(1)} %fusion.50), channel_id=1, source_target_pairs={{0,1},{1,0},{2,3},{3,2},{4,5},{5,4},{6,7},{7,6},{8,9},{9,8},{10,11... | collective-permute-start | bytes 1572872 | tf_op jit(solution)/shard_map/ppermute | solution.py:338
  143.2 2.2 %shard_map.123.refs_4_ = f32[512,1024]{1,0:T(8,128)S(1)} custom-call(s32[2]{0:T(128)S(1)} %pad_add_fusion.at_ref, bf16[512,256]{1,0:T(8,128)(2,1)S(1)} %get-tuple-element.130.refs_0_, bf16[512,256]{1,0:T(8,128)(2,1)S(1)} %get-tuple-element.129.refs_1_, bf16[512,256]{1,0:T(8,128)(2,1)S(1)} %get-tuple-element.128.refs_2_, ...), custom_call_target="tpu_custom_call" | custom-call | flops 1073741824 | bytes 7340032 | tf_op jit(solution)/shard_map/pallas_call | solution.py:122
  145.6 6.3 %collective-permute-done.31 = bf16[512,512]{1,0:T(8,128)(2,1)S(1)} collective-permute-done((bf16[512,512]{1,0:T(8,128)(2,1)S(1)}, bf16[512,512]{1,0:T(8,128)(2,1)S(1)}, u32[]{:S(2)}, u32[]{:S(2)}) %collective-permute-start.31) | collective-permute-done | bytes 524320 | tf_op jit(solution)/shard_map/ppermute | solution.py:338
  157.4 6.2 %collective-permute-done.32 = bf16[512,512]{1,0:T(8,128)(2,1)S(1)} collective-permute-done((bf16[512,512]{1,0:T(8,128)(2,1)S(1)}, bf16[512,512]{1,0:T(8,128)(2,1)S(1)}, u32[]{:S(2)}, u32[]{:S(2)}) %collective-permute-start.32) | collective-permute-done | bytes 524320 | tf_op jit(solution)/shard_map/ppermute | solution.py:338
  165.9 3.4 %shard_map.125 = (bf16[512,1024]{1,0:T(8,128)(2,1)}, bf16[512,512]{1,0:T(8,128)(2,1)}) custom-call(s32[2]{0:T(128)S(1)} %pad_add_fusion.at_ref, bf16[512,256]{1,0:T(8,128)(2,1)S(1)} %get-tuple-element.126.refs_0_, bf16[512,256]{1,0:T(8,128)(2,1)S(1)} %get-tuple-element.125.refs_1_, bf16[256,1024]{1,0:T(8,128)(2,1)} %collective-permute-done.28.refs_2_, ...), custom_call_target="tpu_custom_call" | custom-call | flops 536870912 | bytes 5767168 | tf_op jit(solution)/shard_map/pallas_call | solution.py:122
  (152 shorter events, 58.6 us)
Async XLA Ops:
  3.8 37.2 %collective-permute-start.2 = (bf16[512,1536]{1,0:T(8,128)(2,1)}, bf16[512,1536]{1,0:T(8,128)(2,1)}, u32[]{:S(2)}, u32[]{:S(2)}) collective-permute-start(bf16[512,1536]{1,0:T(8,128)(2,1)} %shard_map.122), channel_id=1, source_target_pairs={{0,4},{4,0},{8,12},{12,8},{16,24},{20,28},{24,16},{28,20},{1,5},{5... | collective-permute-start | bytes 4718600 | tf_op jit(solution)/shard_map/ppermute | solution.py:41
  6.5 35.3 %collective-permute-start.3 = (bf16[512,1536]{1,0:T(8,128)(2,1)}, bf16[512,1536]{1,0:T(8,128)(2,1)}, u32[]{:S(2)}, u32[]{:S(2)}) collective-permute-start(bf16[512,1536]{1,0:T(8,128)(2,1)} %shard_map.122), channel_id=1, source_target_pairs={{0,8},{4,12},{8,0},{12,4},{16,20},{20,16},{24,28},{28,24},{1,9},{5... | collective-permute-start | bytes 4718600 | tf_op jit(solution)/shard_map/ppermute | solution.py:41
  11.0 14.0 %collective-permute-start.1 = (bf16[512,512]{1,0:T(8,128)(2,1)}, bf16[512,512]{1,0:T(8,128)(2,1)}, u32[]{:S(2)}, u32[]{:S(2)}) collective-permute-start(bf16[512,512]{1,0:T(8,128)(2,1)} %get-tuple-element.146), channel_id=1, source_target_pairs={{0,1},{1,0},{2,3},{3,2},{4,5},{5,4},{6,7},{7,6},{8,9},{9,8},{10,11... | collective-permute-start | bytes 1572872 | tf_op jit(solution)/shard_map/ppermute | solution.py:178
  12.6 12.4 %collective-permute-start.4 = (bf16[512,512]{1,0:T(8,128)(2,1)}, bf16[512,512]{1,0:T(8,128)(2,1)}, u32[]{:S(2)}, u32[]{:S(2)}) collective-permute-start(bf16[512,512]{1,0:T(8,128)(2,1)} %get-tuple-element.146), channel_id=1, source_target_pairs={{1,2},{2,1},{17,18},{18,17},{0,16},{3,19},{16,0},{19,3},{5,6},{6,5... | collective-permute-start | bytes 1572872 | tf_op jit(solution)/shard_map/ppermute | solution.py:180
  25.0 15.5 %collective-permute-start.5 = (bf16[512,512]{1,0:T(8,128)(2,1)}, bf16[512,512]{1,0:T(8,128)(2,1)S(1)}, u32[]{:S(2)}, u32[]{:S(2)}) collective-permute-start(bf16[512,512]{1,0:T(8,128)(2,1)} %collective-permute-done.4), channel_id=1, source_target_pairs={{0,1},{1,0},{2,3},{3,2},{4,5},{5,4},{6,7},{7,6},{8,9},{9,8},{10,11... | collective-permute-start | bytes 1572872 | tf_op jit(solution)/shard_map/ppermute | solution.py:178
  30.8 19.9 %collective-permute-start.7 = (bf16[512,512]{1,0:T(8,128)(2,1)S(1)}, bf16[512,512]{1,0:T(8,128)(2,1)S(1)}, u32[]{:S(2)}, u32[]{:S(2)}) collective-permute-start(bf16[512,512]{1,0:T(8,128)(2,1)S(1)} %collective-permute-done.6), channel_id=1, source_target_pairs={{0,1},{1,0},{2,3},{3,2},{4,5},{5,4},{6,7},{7,6},{8,9},{9,8},{10,11... | collective-permute-start | bytes 1572872 | tf_op jit(solution)/shard_map/ppermute | solution.py:178
  41.8 13.8 %collective-permute-start.10 = (bf16[512,1536]{1,0:T(8,128)(2,1)}, bf16[512,1536]{1,0:T(8,128)(2,1)S(1)}, u32[]{:S(2)}, u32[]{:S(2)}) collective-permute-start(bf16[512,1536]{1,0:T(8,128)(2,1)} %collective-permute-done.2), channel_id=1, source_target_pairs={{0,16},{16,0},{1,17},{17,1},{2,18},{18,2},{3,19},{19,3},{4,20},{20... | collective-permute-start | bytes 4718600 | tf_op jit(solution)/shard_map/ppermute | solution.py:19
  42.1 20.6 %collective-permute-start.8 = (bf16[512,1536]{1,0:T(8,128)(2,1)}, bf16[512,1536]{1,0:T(8,128)(2,1)S(1)}, u32[]{:S(2)}, u32[]{:S(2)}) collective-permute-start(bf16[512,1536]{1,0:T(8,128)(2,1)} %collective-permute-done.2), channel_id=1, source_target_pairs={{0,8},{4,12},{8,0},{12,4},{16,20},{20,16},{24,28},{28,24},{1,9},{5... | collective-permute-start | bytes 4718600 | tf_op jit(solution)/shard_map/ppermute | solution.py:41
  62.7 19.6 %collective-permute-start.12 = (bf16[768,512]{1,0:T(8,128)(2,1)S(1)}, bf16[768,512]{1,0:T(8,128)(2,1)S(1)}, u32[]{:S(2)}, u32[]{:S(2)}) collective-permute-start(bf16[768,512]{1,0:T(8,128)(2,1)S(1)} %constant_dynamic-slice_fusion.5), channel_id=1, source_target_pairs={{0,4},{4,0},{8,12},{12,8},{16,24},{20,28},{24,16},{28,20},{1,5},{5... | collective-permute-start | bytes 2359304 | tf_op jit(solution)/shard_map/ppermute | solution.py:41
  64.7 17.9 %collective-permute-start.13 = (bf16[768,512]{1,0:T(8,128)(2,1)S(1)}, bf16[768,512]{1,0:T(8,128)(2,1)S(1)}, u32[]{:S(2)}, u32[]{:S(2)}) collective-permute-start(bf16[768,512]{1,0:T(8,128)(2,1)S(1)} %constant_dynamic-slice_fusion.5), channel_id=1, source_target_pairs={{0,8},{4,12},{8,0},{12,4},{16,20},{20,16},{24,28},{28,24},{1,9},{5... | collective-permute-start | bytes 2359304 | tf_op jit(solution)/shard_map/ppermute | solution.py:41
  70.8 14.5 %collective-permute-start.15 = (bf16[512,512]{1,0:T(8,128)(2,1)S(1)}, bf16[512,512]{1,0:T(8,128)(2,1)S(1)}, u32[]{:S(2)}, u32[]{:S(2)}) collective-permute-start(bf16[512,512]{1,0:T(8,128)(2,1)S(1)} %convolution_convert_fusion), channel_id=1, source_target_pairs={{0,1},{1,0},{2,3},{3,2},{4,5},{5,4},{6,7},{7,6},{8,9},{9,8},{10,11... | collective-permute-start | bytes 1572872 | tf_op jit(solution)/shard_map/ppermute | solution.py:338
  83.2 12.1 %collective-permute-start.17 = (bf16[768,512]{1,0:T(8,128)(2,1)S(1)}, bf16[768,512]{1,0:T(8,128)(2,1)}, u32[]{:S(2)}, u32[]{:S(2)}) collective-permute-start(bf16[768,512]{1,0:T(8,128)(2,1)S(1)} %collective-permute-done.12), channel_id=1, source_target_pairs={{0,8},{4,12},{8,0},{12,4},{16,20},{20,16},{24,28},{28,24},{1,9},{5... | collective-permute-start | bytes 2359304 | tf_op jit(solution)/shard_map/ppermute | solution.py:41
  90.2 14.5 %collective-permute-start.19 = (bf16[512,512]{1,0:T(8,128)(2,1)}, bf16[512,512]{1,0:T(8,128)(2,1)}, u32[]{:S(2)}, u32[]{:S(2)}) collective-permute-start(bf16[512,512]{1,0:T(8,128)(2,1)} %fusion.28), channel_id=1, source_target_pairs={{0,1},{1,0},{2,3},{3,2},{4,5},{5,4},{6,7},{7,6},{8,9},{9,8},{10,11... | collective-permute-start | bytes 1572872 | tf_op jit(solution)/shard_map/ppermute | solution.py:338
  91.9 14.9 %collective-permute-start.18 = (bf16[512,512]{1,0:T(8,128)(2,1)}, bf16[512,512]{1,0:T(8,128)(2,1)}, u32[]{:S(2)}, u32[]{:S(2)}) collective-permute-start(bf16[512,512]{1,0:T(8,128)(2,1)} %fusion.31), channel_id=1, source_target_pairs={{1,2},{2,1},{17,18},{18,17},{0,16},{3,19},{16,0},{19,3},{5,6},{6,5... | collective-permute-start | bytes 1572872 | tf_op jit(solution)/shard_map/ppermute | solution.py:338
  95.3 13.7 %collective-permute-start.20 = (bf16[768,512]{1,0:T(8,128)(2,1)}, bf16[768,512]{1,0:T(8,128)(2,1)}, u32[]{:S(2)}, u32[]{:S(2)}) collective-permute-start(bf16[768,512]{1,0:T(8,128)(2,1)} %collective-permute-done.17), channel_id=1, source_target_pairs={{0,16},{16,0},{1,17},{17,1},{2,18},{18,2},{3,19},{19,3},{4,20},{20... | collective-permute-start | bytes 2359304 | tf_op jit(solution)/shard_map/ppermute | solution.py:19
  96.2 12.8 %collective-permute-start.21 = (bf16[256,1024]{1,0:T(8,128)(2,1)}, bf16[256,1024]{1,0:T(8,128)(2,1)S(1)}, u32[]{:S(2)}, u32[]{:S(2)}) collective-permute-start(bf16[256,1024]{1,0:T(8,128)(2,1)} %constant_dynamic-slice_fusion.4), channel_id=1, source_target_pairs={{0,4},{4,0},{8,12},{12,8},{16,24},{20,28},{24,16},{28,20},{1,5},{5... | collective-permute-start | bytes 1572872 | tf_op jit(solution)/shard_map/ppermute | solution.py:41
  109.0 13.7 %collective-permute-start.23 = (bf16[512,512]{1,0:T(8,128)(2,1)}, bf16[512,512]{1,0:T(8,128)(2,1)}, u32[]{:S(2)}, u32[]{:S(2)}) collective-permute-start(bf16[512,512]{1,0:T(8,128)(2,1)} %add_convert_fusion.1), channel_id=1, source_target_pairs={{0,1},{1,0},{2,3},{3,2},{4,5},{5,4},{6,7},{7,6},{8,9},{9,8},{10,11... | collective-permute-start | bytes 1572872 | tf_op jit(solution)/shard_map/ppermute | solution.py:338
  110.6 13.5 %collective-permute-start.24 = (bf16[256,1024]{1,0:T(8,128)(2,1)}, bf16[256,1024]{1,0:T(8,128)(2,1)}, u32[]{:S(2)}, u32[]{:S(2)}) collective-permute-start(bf16[256,1024]{1,0:T(8,128)(2,1)} %constant_dynamic-slice_fusion.4), channel_id=1, source_target_pairs={{0,8},{4,12},{8,0},{12,4},{16,20},{20,16},{24,28},{28,24},{1,9},{5... | collective-permute-start | bytes 1572872 | tf_op jit(solution)/shard_map/ppermute | solution.py:41
  111.8 12.1 %collective-permute-start.22 = (bf16[512,512]{1,0:T(8,128)(2,1)}, bf16[512,512]{1,0:T(8,128)(2,1)S(1)}, u32[]{:S(2)}, u32[]{:S(2)}) collective-permute-start(bf16[512,512]{1,0:T(8,128)(2,1)} %fusion.34), channel_id=1, source_target_pairs={{1,2},{2,1},{17,18},{18,17},{0,16},{3,19},{16,0},{19,3},{5,6},{6,5... | collective-permute-start | bytes 1572872 | tf_op jit(solution)/shard_map/ppermute | solution.py:338
  111.9 12.3 %collective-permute-start.25 = (bf16[256,1024]{1,0:T(8,128)(2,1)S(1)}, bf16[256,1024]{1,0:T(8,128)(2,1)S(1)}, u32[]{:S(2)}, u32[]{:S(2)}) collective-permute-start(bf16[256,1024]{1,0:T(8,128)(2,1)S(1)} %collective-permute-done.21.refs_6_), channel_id=1, source_target_pairs={{0,16},{16,0},{1,17},{17,1},{2,18},{18,2},{3,19},{19,3},{4,20},{20... | collective-permute-start | bytes 1572872 | tf_op jit(solution)/shard_map/ppermute | solution.py:19
  112.4 25.1 %collective-permute-start.28 = (bf16[256,1024]{1,0:T(8,128)(2,1)S(1)}, bf16[256,1024]{1,0:T(8,128)(2,1)}, u32[]{:S(2)}, u32[]{:S(2)}) collective-permute-start(bf16[256,1024]{1,0:T(8,128)(2,1)S(1)} %collective-permute-done.21.refs_6_), channel_id=1, source_target_pairs={{0,8},{4,12},{8,0},{12,4},{16,20},{20,16},{24,28},{28,24},{1,9},{5... | collective-permute-start | bytes 1572872 | tf_op jit(solution)/shard_map/ppermute | solution.py:41
  124.2 13.1 %collective-permute-start.27 = (bf16[512,512]{1,0:T(8,128)(2,1)S(1)}, bf16[512,512]{1,0:T(8,128)(2,1)S(1)}, u32[]{:S(2)}, u32[]{:S(2)}) collective-permute-start(bf16[512,512]{1,0:T(8,128)(2,1)S(1)} %add_convert_fusion), channel_id=1, source_target_pairs={{0,1},{1,0},{2,3},{3,2},{4,5},{5,4},{6,7},{7,6},{8,9},{9,8},{10,11... | collective-permute-start | bytes 1572872 | tf_op jit(solution)/shard_map/ppermute | solution.py:338
  137.5 14.3 %collective-permute-start.31 = (bf16[512,512]{1,0:T(8,128)(2,1)S(1)}, bf16[512,512]{1,0:T(8,128)(2,1)S(1)}, u32[]{:S(2)}, u32[]{:S(2)}) collective-permute-start(bf16[512,512]{1,0:T(8,128)(2,1)S(1)} %fusion.50), channel_id=1, source_target_pairs={{0,1},{1,0},{2,3},{3,2},{4,5},{5,4},{6,7},{7,6},{8,9},{9,8},{10,11... | collective-permute-start | bytes 1572872 | tf_op jit(solution)/shard_map/ppermute | solution.py:338
  141.3 23.2 %collective-permute-start.33 = (bf16[256,1024]{1,0:T(8,128)(2,1)}, bf16[256,1024]{1,0:T(8,128)(2,1)}, u32[]{:S(2)}, u32[]{:S(2)}) collective-permute-start(bf16[256,1024]{1,0:T(8,128)(2,1)} %collective-permute-done.28.refs_2_), channel_id=1, source_target_pairs={{0,16},{16,0},{1,17},{17,1},{2,18},{18,2},{3,19},{19,3},{4,20},{20... | collective-permute-start | bytes 1572872 | tf_op jit(solution)/shard_map/ppermute | solution.py:19
  (31 other events, 270.8 us)

commit v6 on v5

--- a/solution.py
+++ b/solution.py
@@ -375,8 +375,8 @@
         if k >= 0:
             finish(k)
         if k == rows - 3:
-            acc = project(None, [x for j in range(rows - 2) for x in terms_of(j)], scalars)
-    acc = project(acc, terms_of(rows - 2), scalars)
+            acc = project(None, [x for j in range(rows - 3) for x in terms_of(j)], scalars)
+    acc = project(acc, [x for j in (rows - 3, rows - 2) for x in terms_of(j)], scalars)
     finish(rows - 1)
 
     kept = fresh[0]

time: 170 us -> 169 us (level)
  waiting for transfers between devices: 60.1 us -> 56.3 us
  starting transfers between devices: 43 us -> 45.2 us
    ppermute x10, waiting for transfers between devices: 33.4 us -> 28.9 us  [per_device(): (by_even, by_odd)[i][t] = lax.ppermute(send, line_axes[i], (even, odd)[i])]
    ppermute x10, starting transfers between devices: 12.1 us -> 14.2 us  [per_device(): (by_even, by_odd)[i][t] = lax.ppermute(send, line_axes[i], (even, odd)[i])]
    unnamed x50 -> x54, local copies, waits for them, and re-layouts: 10.2 us -> 10.2 us
where the time goes in v6:
time: 169 us; the launch traced here: 168 us
  waiting for transfers between devices  56.3 us (33%)
  starting transfers between devices  45.2 us (27%)
  other arithmetic  17.9 us (11%)
  matrix products  16.9 us (10%)
  local copies, waits for them, and re-layouts  12.4 us (7%)
  Pallas kernels  10.6 us (6%)
  between operations  9.05 us (5%)
    ppermute x10, waiting for transfers between devices, per_device(): (by_even, by_odd)[i][t] = lax.ppermute(send, line_axes[i], (even, odd)[i])  28.9 us
    ppermute x9, waiting for transfers between devices, row_step(): return lax.ppermute(x, ('rep', 'row'), pairs)  17 us
    ppermute x9, starting transfers between devices, row_step(): return lax.ppermute(x, ('rep', 'row'), pairs)  14.9 us
    ppermute x10, starting transfers between devices, per_device(): (by_even, by_odd)[i][t] = lax.ppermute(send, line_axes[i], (even, odd)[i])  14.2 us
    dot_general x8, matrix products, dot(): return jnp.dot(x, w, preferred_element_type=f32)  13.9 us
    ppermute x3, starting transfers between devices, line_step(): by_even[step] = lax.ppermute(by_odd[step - 1], 'col', even)  13.4 us
    unnamed x54, local copies, waits for them, and re-layouts  10.2 us
    ppermute x3, waiting for transfers between devices, line_step(): by_even[step] = lax.ppermute(by_odd[step - 1], 'col', even)  10.2 us
  transfers between devices with their start and end apart: 34, of which 16 were waited for; matrix products, arithmetic and copies ran while one was open for 26% of the time, Pallas kernels for 4%

profile of v6, /device:TPU:0, one launch (start us, length us, event | category | flops | bytes accessed | tf_op | source)
XLA Modules:
  0.0 168.3 jit_solution(10104685855734447591)
XLA Ops:
  1.2 2.6 %shard_map.122 = bf16[512,1536]{1,0:T(8,128)(2,1)} custom-call(s32[1]{0:T(128)} %bitcast.2.core_ref, bf16[512,1536]{1,0:T(8,128)(2,1)} %top_ref.1, bf16[512,1536]{1,0:T(8,128)(2,1)} %bottom_ref.1), custom_call_target="tpu_custom_call" | custom-call | bytes 3145728 | tf_op jit(solution)/shard_map/pallas_call | solution.py:68
  3.8 2.7 %collective-permute-start.2 = (bf16[512,1536]{1,0:T(8,128)(2,1)}, bf16[512,1536]{1,0:T(8,128)(2,1)}, u32[]{:S(2)}, u32[]{:S(2)}) collective-permute-start(bf16[512,1536]{1,0:T(8,128)(2,1)} %shard_map.122), channel_id=1, source_target_pairs={{0,4},{4,0},{8,12},{12,8},{16,24},{20,28},{24,16},{28,20},{1,5},{5... | collective-permute-start | bytes 4718600 | tf_op jit(solution)/shard_map/ppermute | solution.py:41
  8.1 2.9 %bitcast_dynamic-update-slice_fusion.5 = (bf16[6,512,512]{2,1,0:T(8,128)(2,1)}, bf16[512,512]{1,0:T(8,128)(2,1)}) fusion(bf16[512,512]{1,0:T(8,128)(2,1)} %collective-permute-done, bf16[512,512]{1,0:T(8,128)(2,1)} %param.11, s32[512]{0:T(512)S(1)} %fusion.75), kind=kOutput, calls=%fused_computation.125 | convolution fusion | flops 539754496 | bytes 2099200 | tf_op jit(solution)/shard_map/dot_general | solution.py:168
  21.1 3.8 %collective-permute-done.1 = bf16[512,512]{1,0:T(8,128)(2,1)} collective-permute-done((bf16[512,512]{1,0:T(8,128)(2,1)}, bf16[512,512]{1,0:T(8,128)(2,1)}, u32[]{:S(2)}, u32[]{:S(2)}) %collective-permute-start.1) | collective-permute-done | bytes 524320 | tf_op jit(solution)/shard_map/ppermute | solution.py:178
  25.0 3.1 %collective-permute-start.5 = (bf16[512,512]{1,0:T(8,128)(2,1)}, bf16[512,512]{1,0:T(8,128)(2,1)S(1)}, u32[]{:S(2)}, u32[]{:S(2)}) collective-permute-start(bf16[512,512]{1,0:T(8,128)(2,1)} %collective-permute-done.4), channel_id=1, source_target_pairs={{0,1},{1,0},{2,3},{3,2},{4,5},{5,4},{6,7},{7,6},{8,9},{9,8},{10,11... | collective-permute-start | bytes 1572872 | tf_op jit(solution)/shard_map/ppermute | solution.py:178
  30.8 8.7 %collective-permute-start.7 = (bf16[512,512]{1,0:T(8,128)(2,1)S(1)}, bf16[512,512]{1,0:T(8,128)(2,1)S(1)}, u32[]{:S(2)}, u32[]{:S(2)}) collective-permute-start(bf16[512,512]{1,0:T(8,128)(2,1)S(1)} %collective-permute-done.6), channel_id=1, source_target_pairs={{0,1},{1,0},{2,3},{3,2},{4,5},{5,4},{6,7},{7,6},{8,9},{9,8},{10,11... | collective-permute-start | bytes 1572872 | tf_op jit(solution)/shard_map/ppermute | solution.py:178
  45.4 5.4 %collective-permute-done.7 = bf16[512,512]{1,0:T(8,128)(2,1)S(1)} collective-permute-done((bf16[512,512]{1,0:T(8,128)(2,1)S(1)}, bf16[512,512]{1,0:T(8,128)(2,1)S(1)}, u32[]{:S(2)}, u32[]{:S(2)}) %collective-permute-start.7) | collective-permute-done | bytes 524320 | tf_op jit(solution)/shard_map/ppermute | solution.py:178
  55.7 2.6 %fusion.95 = f32[512,1536]{1,0:T(8,128)S(1)} fusion(bf16[512,1536]{1,0:T(8,128)(2,1)S(1)} %select_dynamic-update-slice_fusion, bf16[1536,1536]{1,0:T(8,128)(2,1)S(1)} %get-tuple-element.115), kind=kOutput, calls=%fused_computation.179 | convolution fusion | flops 2415919104 | bytes 9437184 | tf_op jit(solution)/shard_map/dot_general | solution.py:216
  58.3 2.6 %fusion.94 = f32[512,1536]{1,0:T(8,128)S(1)} fusion(bf16[512,1536]{1,0:T(8,128)(2,1)S(1)} %select_dynamic-update-slice_fusion, bf16[1536,1536]{1,0:T(8,128)(2,1)S(1)} %get-tuple-element.116), kind=kOutput, calls=%fused_computation.178 | convolution fusion | flops 2415919104 | bytes 9437184 | tf_op jit(solution)/shard_map/dot_general | solution.py:216
  70.8 2.2 %collective-permute-start.15 = (bf16[512,512]{1,0:T(8,128)(2,1)S(1)}, bf16[512,512]{1,0:T(8,128)(2,1)S(1)}, u32[]{:S(2)}, u32[]{:S(2)}) collective-permute-start(bf16[512,512]{1,0:T(8,128)(2,1)S(1)} %convolution_convert_fusion), channel_id=1, source_target_pairs={{0,1},{1,0},{2,3},{3,2},{4,5},{5,4},{6,7},{7,6},{8,9},{9,8},{10,11... | collective-permute-start | bytes 1572872 | tf_op jit(solution)/shard_map/ppermute | solution.py:338
  73.0 9.4 %collective-permute-done.12 = bf16[768,512]{1,0:T(8,128)(2,1)S(1)} collective-permute-done((bf16[768,512]{1,0:T(8,128)(2,1)S(1)}, bf16[768,512]{1,0:T(8,128)(2,1)S(1)}, u32[]{:S(2)}, u32[]{:S(2)}) %collective-permute-start.12) | collective-permute-done | bytes 786464 | tf_op jit(solution)/shard_map/ppermute | solution.py:41
  91.1 4.2 %collective-permute-done.17 = bf16[768,512]{1,0:T(8,128)(2,1)} collective-permute-done((bf16[768,512]{1,0:T(8,128)(2,1)S(1)}, bf16[768,512]{1,0:T(8,128)(2,1)}, u32[]{:S(2)}, u32[]{:S(2)}) %collective-permute-start.17) | collective-permute-done | bytes 786464 | tf_op jit(solution)/shard_map/ppermute | solution.py:41
  96.2 2.1 %collective-permute-start.21 = (bf16[256,1024]{1,0:T(8,128)(2,1)}, bf16[256,1024]{1,0:T(8,128)(2,1)}, u32[]{:S(2)}, u32[]{:S(2)}) collective-permute-start(bf16[256,1024]{1,0:T(8,128)(2,1)} %constant_dynamic-slice_fusion.4), channel_id=1, source_target_pairs={{0,4},{4,0},{8,12},{12,8},{16,24},{20,28},{24,16},{28,20},{1,5},{5... | collective-permute-start | bytes 1572872 | tf_op jit(solution)/shard_map/ppermute | solution.py:41
  98.3 5.7 %collective-permute-done.19 = bf16[512,512]{1,0:T(8,128)(2,1)} collective-permute-done((bf16[512,512]{1,0:T(8,128)(2,1)}, bf16[512,512]{1,0:T(8,128)(2,1)}, u32[]{:S(2)}, u32[]{:S(2)}) %collective-permute-start.19) | collective-permute-done | bytes 524320 | tf_op jit(solution)/shard_map/ppermute | solution.py:338
  103.9 2.1 %fusion.34 = bf16[512,512]{1,0:T(8,128)(2,1)} fusion(bf16[512,512]{1,0:T(8,128)(2,1)} %fusion.28, bf16[512,512]{1,0:T(8,128)(2,1)} %collective-permute-done.19), kind=kLoop, calls=%fused_computation.66 | loop fusion | flops 1048576 | bytes 1572864 | tf_op jit(solution)/shard_map/convert_element_type | solution.py:327
  112.5 2.9 %fusion.22 = bf16[512,512]{1,0:T(8,128)(2,1)S(1)} fusion(bf16[768,512]{1,0:T(8,128)(2,1)} %collective-permute-done.20, bf16[768,512]{1,0:T(8,128)(2,1)} %collective-permute-done.17, bf16[512,768]{1,0:T(8,128)(2,1)} %copy-done.18, bf16[512,768]{1,0:T(8,128)(2,1)} %copy-done.17), kind=kOutput, calls=%fused_computation.60 | convolution fusion | flops 811859968 | bytes 3670016 | tf_op jit(solution)/shard_map/dot_general | solution.py:216
  115.4 6.4 %collective-permute-done.23 = bf16[512,512]{1,0:T(8,128)(2,1)} collective-permute-done((bf16[512,512]{1,0:T(8,128)(2,1)}, bf16[512,512]{1,0:T(8,128)(2,1)}, u32[]{:S(2)}, u32[]{:S(2)}) %collective-permute-start.23) | collective-permute-done | bytes 524320 | tf_op jit(solution)/shard_map/ppermute | solution.py:338
  123.3 2.7 %collective-permute-start.27 = (bf16[512,512]{1,0:T(8,128)(2,1)S(1)}, bf16[512,512]{1,0:T(8,128)(2,1)S(1)}, u32[]{:S(2)}, u32[]{:S(2)}) collective-permute-start(bf16[512,512]{1,0:T(8,128)(2,1)S(1)} %add_convert_fusion), channel_id=1, source_target_pairs={{0,1},{1,0},{2,3},{3,2},{4,5},{5,4},{6,7},{7,6},{8,9},{9,8},{10,11... | collective-permute-start | bytes 1572872 | tf_op jit(solution)/shard_map/ppermute | solution.py:338
  129.6 7.0 %collective-permute-done.27 = bf16[512,512]{1,0:T(8,128)(2,1)S(1)} collective-permute-done((bf16[512,512]{1,0:T(8,128)(2,1)S(1)}, bf16[512,512]{1,0:T(8,128)(2,1)S(1)}, u32[]{:S(2)}, u32[]{:S(2)}) %collective-permute-start.27) | collective-permute-done | bytes 524320 | tf_op jit(solution)/shard_map/ppermute | solution.py:338
  136.8 4.4 %collective-permute-start.31 = (bf16[512,512]{1,0:T(8,128)(2,1)}, bf16[512,512]{1,0:T(8,128)(2,1)S(1)}, u32[]{:S(2)}, u32[]{:S(2)}) collective-permute-start(bf16[512,512]{1,0:T(8,128)(2,1)} %fusion.50), channel_id=1, source_target_pairs={{0,1},{1,0},{2,3},{3,2},{4,5},{5,4},{6,7},{7,6},{8,9},{9,8},{10,11... | collective-permute-start | bytes 1572872 | tf_op jit(solution)/shard_map/ppermute | solution.py:338
  145.1 6.4 %collective-permute-done.31 = bf16[512,512]{1,0:T(8,128)(2,1)S(1)} collective-permute-done((bf16[512,512]{1,0:T(8,128)(2,1)}, bf16[512,512]{1,0:T(8,128)(2,1)S(1)}, u32[]{:S(2)}, u32[]{:S(2)}) %collective-permute-start.31) | collective-permute-done | bytes 524320 | tf_op jit(solution)/shard_map/ppermute | solution.py:338
  154.9 3.0 %shard_map.124.refs_4_ = f32[512,1024]{1,0:T(8,128)S(1)} custom-call(s32[2]{0:T(128)S(1)} %pad_add_fusion.at_ref, bf16[512,256]{1,0:T(8,128)(2,1)S(1)} %get-tuple-element.128.refs_0_, bf16[512,256]{1,0:T(8,128)(2,1)S(1)} %get-tuple-element.127.refs_1_, bf16[512,256]{1,0:T(8,128)(2,1)S(1)} %get-tuple-element.126.refs_2_, ...), custom_call_target="tpu_custom_call" | custom-call | flops 1073741824 | bytes 7340032 | tf_op jit(solution)/shard_map/pallas_call | solution.py:122
  159.3 3.3 %collective-permute-done.32 = bf16[512,512]{1,0:T(8,128)(2,1)S(1)} collective-permute-done((bf16[512,512]{1,0:T(8,128)(2,1)S(1)}, bf16[512,512]{1,0:T(8,128)(2,1)S(1)}, u32[]{:S(2)}, u32[]{:S(2)}) %collective-permute-start.32) | collective-permute-done | bytes 524320 | tf_op jit(solution)/shard_map/ppermute | solution.py:338
  165.0 3.3 %shard_map.125 = (bf16[512,1024]{1,0:T(8,128)(2,1)}, bf16[512,512]{1,0:T(8,128)(2,1)}) custom-call(s32[2]{0:T(128)S(1)} %pad_add_fusion.at_ref, bf16[512,256]{1,0:T(8,128)(2,1)S(1)} %get-tuple-element.130.refs_0_, bf16[512,256]{1,0:T(8,128)(2,1)S(1)} %get-tuple-element.129.refs_1_, bf16[256,1024]{1,0:T(8,128)(2,1)S(1)} %collective-permute-done.28.refs_2_, ...), custom_call_target="tpu_custom_call" | custom-call | flops 536870912 | bytes 5767168 | tf_op jit(solution)/shard_map/pallas_call | solution.py:122
  (158 shorter events, 59.7 us)
Async XLA Ops:
  3.8 37.2 %collective-permute-start.2 = (bf16[512,1536]{1,0:T(8,128)(2,1)}, bf16[512,1536]{1,0:T(8,128)(2,1)}, u32[]{:S(2)}, u32[]{:S(2)}) collective-permute-start(bf16[512,1536]{1,0:T(8,128)(2,1)} %shard_map.122), channel_id=1, source_target_pairs={{0,4},{4,0},{8,12},{12,8},{16,24},{20,28},{24,16},{28,20},{1,5},{5... | collective-permute-start | bytes 4718600 | tf_op jit(solution)/shard_map/ppermute | solution.py:41
  6.5 35.3 %collective-permute-start.3 = (bf16[512,1536]{1,0:T(8,128)(2,1)}, bf16[512,1536]{1,0:T(8,128)(2,1)}, u32[]{:S(2)}, u32[]{:S(2)}) collective-permute-start(bf16[512,1536]{1,0:T(8,128)(2,1)} %shard_map.122), channel_id=1, source_target_pairs={{0,8},{4,12},{8,0},{12,4},{16,20},{20,16},{24,28},{28,24},{1,9},{5... | collective-permute-start | bytes 4718600 | tf_op jit(solution)/shard_map/ppermute | solution.py:41
  11.0 14.0 %collective-permute-start.1 = (bf16[512,512]{1,0:T(8,128)(2,1)}, bf16[512,512]{1,0:T(8,128)(2,1)}, u32[]{:S(2)}, u32[]{:S(2)}) collective-permute-start(bf16[512,512]{1,0:T(8,128)(2,1)} %get-tuple-element.150), channel_id=1, source_target_pairs={{0,1},{1,0},{2,3},{3,2},{4,5},{5,4},{6,7},{7,6},{8,9},{9,8},{10,11... | collective-permute-start | bytes 1572872 | tf_op jit(solution)/shard_map/ppermute | solution.py:178
  12.6 12.4 %collective-permute-start.4 = (bf16[512,512]{1,0:T(8,128)(2,1)}, bf16[512,512]{1,0:T(8,128)(2,1)}, u32[]{:S(2)}, u32[]{:S(2)}) collective-permute-start(bf16[512,512]{1,0:T(8,128)(2,1)} %get-tuple-element.150), channel_id=1, source_target_pairs={{1,2},{2,1},{17,18},{18,17},{0,16},{3,19},{16,0},{19,3},{5,6},{6,5... | collective-permute-start | bytes 1572872 | tf_op jit(solution)/shard_map/ppermute | solution.py:180
  25.0 15.5 %collective-permute-start.5 = (bf16[512,512]{1,0:T(8,128)(2,1)}, bf16[512,512]{1,0:T(8,128)(2,1)S(1)}, u32[]{:S(2)}, u32[]{:S(2)}) collective-permute-start(bf16[512,512]{1,0:T(8,128)(2,1)} %collective-permute-done.4), channel_id=1, source_target_pairs={{0,1},{1,0},{2,3},{3,2},{4,5},{5,4},{6,7},{7,6},{8,9},{9,8},{10,11... | collective-permute-start | bytes 1572872 | tf_op jit(solution)/shard_map/ppermute | solution.py:178
  30.8 19.9 %collective-permute-start.7 = (bf16[512,512]{1,0:T(8,128)(2,1)S(1)}, bf16[512,512]{1,0:T(8,128)(2,1)S(1)}, u32[]{:S(2)}, u32[]{:S(2)}) collective-permute-start(bf16[512,512]{1,0:T(8,128)(2,1)S(1)} %collective-permute-done.6), channel_id=1, source_target_pairs={{0,1},{1,0},{2,3},{3,2},{4,5},{5,4},{6,7},{7,6},{8,9},{9,8},{10,11... | collective-permute-start | bytes 1572872 | tf_op jit(solution)/shard_map/ppermute | solution.py:178
  41.8 13.8 %collective-permute-start.10 = (bf16[512,1536]{1,0:T(8,128)(2,1)}, bf16[512,1536]{1,0:T(8,128)(2,1)S(1)}, u32[]{:S(2)}, u32[]{:S(2)}) collective-permute-start(bf16[512,1536]{1,0:T(8,128)(2,1)} %collective-permute-done.2), channel_id=1, source_target_pairs={{0,16},{16,0},{1,17},{17,1},{2,18},{18,2},{3,19},{19,3},{4,20},{20... | collective-permute-start | bytes 4718600 | tf_op jit(solution)/shard_map/ppermute | solution.py:19
  42.1 20.6 %collective-permute-start.8 = (bf16[512,1536]{1,0:T(8,128)(2,1)}, bf16[512,1536]{1,0:T(8,128)(2,1)S(1)}, u32[]{:S(2)}, u32[]{:S(2)}) collective-permute-start(bf16[512,1536]{1,0:T(8,128)(2,1)} %collective-permute-done.2), channel_id=1, source_target_pairs={{0,8},{4,12},{8,0},{12,4},{16,20},{20,16},{24,28},{28,24},{1,9},{5... | collective-permute-start | bytes 4718600 | tf_op jit(solution)/shard_map/ppermute | solution.py:41
  62.7 19.6 %collective-permute-start.12 = (bf16[768,512]{1,0:T(8,128)(2,1)S(1)}, bf16[768,512]{1,0:T(8,128)(2,1)S(1)}, u32[]{:S(2)}, u32[]{:S(2)}) collective-permute-start(bf16[768,512]{1,0:T(8,128)(2,1)S(1)} %constant_dynamic-slice_fusion.5), channel_id=1, source_target_pairs={{0,4},{4,0},{8,12},{12,8},{16,24},{20,28},{24,16},{28,20},{1,5},{5... | collective-permute-start | bytes 2359304 | tf_op jit(solution)/shard_map/ppermute | solution.py:41
  64.7 17.9 %collective-permute-start.13 = (bf16[768,512]{1,0:T(8,128)(2,1)S(1)}, bf16[768,512]{1,0:T(8,128)(2,1)S(1)}, u32[]{:S(2)}, u32[]{:S(2)}) collective-permute-start(bf16[768,512]{1,0:T(8,128)(2,1)S(1)} %constant_dynamic-slice_fusion.5), channel_id=1, source_target_pairs={{0,8},{4,12},{8,0},{12,4},{16,20},{20,16},{24,28},{28,24},{1,9},{5... | collective-permute-start | bytes 2359304 | tf_op jit(solution)/shard_map/ppermute | solution.py:41
  70.8 14.5 %collective-permute-start.15 = (bf16[512,512]{1,0:T(8,128)(2,1)S(1)}, bf16[512,512]{1,0:T(8,128)(2,1)S(1)}, u32[]{:S(2)}, u32[]{:S(2)}) collective-permute-start(bf16[512,512]{1,0:T(8,128)(2,1)S(1)} %convolution_convert_fusion), channel_id=1, source_target_pairs={{0,1},{1,0},{2,3},{3,2},{4,5},{5,4},{6,7},{7,6},{8,9},{9,8},{10,11... | collective-permute-start | bytes 1572872 | tf_op jit(solution)/shard_map/ppermute | solution.py:338
  83.3 12.1 %collective-permute-start.17 = (bf16[768,512]{1,0:T(8,128)(2,1)S(1)}, bf16[768,512]{1,0:T(8,128)(2,1)}, u32[]{:S(2)}, u32[]{:S(2)}) collective-permute-start(bf16[768,512]{1,0:T(8,128)(2,1)S(1)} %collective-permute-done.12), channel_id=1, source_target_pairs={{0,8},{4,12},{8,0},{12,4},{16,20},{20,16},{24,28},{28,24},{1,9},{5... | collective-permute-start | bytes 2359304 | tf_op jit(solution)/shard_map/ppermute | solution.py:41
  89.5 14.5 %collective-permute-start.19 = (bf16[512,512]{1,0:T(8,128)(2,1)}, bf16[512,512]{1,0:T(8,128)(2,1)}, u32[]{:S(2)}, u32[]{:S(2)}) collective-permute-start(bf16[512,512]{1,0:T(8,128)(2,1)} %fusion.28), channel_id=1, source_target_pairs={{0,1},{1,0},{2,3},{3,2},{4,5},{5,4},{6,7},{7,6},{8,9},{9,8},{10,11... | collective-permute-start | bytes 1572872 | tf_op jit(solution)/shard_map/ppermute | solution.py:338
  91.1 14.9 %collective-permute-start.18 = (bf16[512,512]{1,0:T(8,128)(2,1)}, bf16[512,512]{1,0:T(8,128)(2,1)}, u32[]{:S(2)}, u32[]{:S(2)}) collective-permute-start(bf16[512,512]{1,0:T(8,128)(2,1)} %fusion.31), channel_id=1, source_target_pairs={{1,2},{2,1},{17,18},{18,17},{0,16},{3,19},{16,0},{19,3},{5,6},{6,5... | collective-permute-start | bytes 1572872 | tf_op jit(solution)/shard_map/ppermute | solution.py:338
  95.4 12.8 %collective-permute-start.20 = (bf16[768,512]{1,0:T(8,128)(2,1)}, bf16[768,512]{1,0:T(8,128)(2,1)}, u32[]{:S(2)}, u32[]{:S(2)}) collective-permute-start(bf16[768,512]{1,0:T(8,128)(2,1)} %collective-permute-done.17), channel_id=1, source_target_pairs={{0,16},{16,0},{1,17},{17,1},{2,18},{18,2},{3,19},{19,3},{4,20},{20... | collective-permute-start | bytes 2359304 | tf_op jit(solution)/shard_map/ppermute | solution.py:19
  96.2 11.9 %collective-permute-start.21 = (bf16[256,1024]{1,0:T(8,128)(2,1)}, bf16[256,1024]{1,0:T(8,128)(2,1)}, u32[]{:S(2)}, u32[]{:S(2)}) collective-permute-start(bf16[256,1024]{1,0:T(8,128)(2,1)} %constant_dynamic-slice_fusion.4), channel_id=1, source_target_pairs={{0,4},{4,0},{8,12},{12,8},{16,24},{20,28},{24,16},{28,20},{1,5},{5... | collective-permute-start | bytes 1572872 | tf_op jit(solution)/shard_map/ppermute | solution.py:41
  108.1 13.7 %collective-permute-start.23 = (bf16[512,512]{1,0:T(8,128)(2,1)}, bf16[512,512]{1,0:T(8,128)(2,1)}, u32[]{:S(2)}, u32[]{:S(2)}) collective-permute-start(bf16[512,512]{1,0:T(8,128)(2,1)} %add_convert_fusion.1), channel_id=1, source_target_pairs={{0,1},{1,0},{2,3},{3,2},{4,5},{5,4},{6,7},{7,6},{8,9},{9,8},{10,11... | collective-permute-start | bytes 1572872 | tf_op jit(solution)/shard_map/ppermute | solution.py:338
  109.9 13.4 %collective-permute-start.24 = (bf16[256,1024]{1,0:T(8,128)(2,1)}, bf16[256,1024]{1,0:T(8,128)(2,1)}, u32[]{:S(2)}, u32[]{:S(2)}) collective-permute-start(bf16[256,1024]{1,0:T(8,128)(2,1)} %constant_dynamic-slice_fusion.4), channel_id=1, source_target_pairs={{0,8},{4,12},{8,0},{12,4},{16,20},{20,16},{24,28},{28,24},{1,9},{5... | collective-permute-start | bytes 1572872 | tf_op jit(solution)/shard_map/ppermute | solution.py:41
  111.1 11.9 %collective-permute-start.22 = (bf16[512,512]{1,0:T(8,128)(2,1)}, bf16[512,512]{1,0:T(8,128)(2,1)S(1)}, u32[]{:S(2)}, u32[]{:S(2)}) collective-permute-start(bf16[512,512]{1,0:T(8,128)(2,1)} %fusion.34), channel_id=1, source_target_pairs={{1,2},{2,1},{17,18},{18,17},{0,16},{3,19},{16,0},{19,3},{5,6},{6,5... | collective-permute-start | bytes 1572872 | tf_op jit(solution)/shard_map/ppermute | solution.py:338
  111.1 12.1 %collective-permute-start.25 = (bf16[256,1024]{1,0:T(8,128)(2,1)}, bf16[256,1024]{1,0:T(8,128)(2,1)S(1)}, u32[]{:S(2)}, u32[]{:S(2)}) collective-permute-start(bf16[256,1024]{1,0:T(8,128)(2,1)} %collective-permute-done.21.refs_4_), channel_id=1, source_target_pairs={{0,16},{16,0},{1,17},{17,1},{2,18},{18,2},{3,19},{19,3},{4,20},{20... | collective-permute-start | bytes 1572872 | tf_op jit(solution)/shard_map/ppermute | solution.py:19
  111.6 25.1 %collective-permute-start.28 = (bf16[256,1024]{1,0:T(8,128)(2,1)}, bf16[256,1024]{1,0:T(8,128)(2,1)S(1)}, u32[]{:S(2)}, u32[]{:S(2)}) collective-permute-start(bf16[256,1024]{1,0:T(8,128)(2,1)} %collective-permute-done.21.refs_4_), channel_id=1, source_target_pairs={{0,8},{4,12},{8,0},{12,4},{16,20},{20,16},{24,28},{28,24},{1,9},{5... | collective-permute-start | bytes 1572872 | tf_op jit(solution)/shard_map/ppermute | solution.py:41
  123.3 13.3 %collective-permute-start.27 = (bf16[512,512]{1,0:T(8,128)(2,1)S(1)}, bf16[512,512]{1,0:T(8,128)(2,1)S(1)}, u32[]{:S(2)}, u32[]{:S(2)}) collective-permute-start(bf16[512,512]{1,0:T(8,128)(2,1)S(1)} %add_convert_fusion), channel_id=1, source_target_pairs={{0,1},{1,0},{2,3},{3,2},{4,5},{5,4},{6,7},{7,6},{8,9},{9,8},{10,11... | collective-permute-start | bytes 1572872 | tf_op jit(solution)/shard_map/ppermute | solution.py:338
  136.8 14.6 %collective-permute-start.31 = (bf16[512,512]{1,0:T(8,128)(2,1)}, bf16[512,512]{1,0:T(8,128)(2,1)S(1)}, u32[]{:S(2)}, u32[]{:S(2)}) collective-permute-start(bf16[512,512]{1,0:T(8,128)(2,1)} %fusion.50), channel_id=1, source_target_pairs={{0,1},{1,0},{2,3},{3,2},{4,5},{5,4},{6,7},{7,6},{8,9},{9,8},{10,11... | collective-permute-start | bytes 1572872 | tf_op jit(solution)/shard_map/ppermute | solution.py:338
  143.2 20.3 %collective-permute-start.33 = (bf16[256,1024]{1,0:T(8,128)(2,1)S(1)}, bf16[256,1024]{1,0:T(8,128)(2,1)}, u32[]{:S(2)}, u32[]{:S(2)}) collective-permute-start(bf16[256,1024]{1,0:T(8,128)(2,1)S(1)} %collective-permute-done.28.refs_2_), channel_id=1, source_target_pairs={{0,16},{16,0},{1,17},{17,1},{2,18},{18,2},{3,19},{19,3},{4,20},{20... | collective-permute-start | bytes 1572872 | tf_op jit(solution)/shard_map/ppermute | solution.py:19
  (33 other events, 298.4 us)

commit v7 on v6

--- a/solution.py
+++ b/solution.py
@@ -334,7 +334,7 @@
         flat = [store[m] for store, masks in held_now for m in masks]
         extra = [acc] if t == steps - 1 else []
         ready = barrier(tuple(v for _, v in sends) + tuple(flat) + tuple(last_step) + tuple(extra))
-        for (i, _), send in zip(sends, ready):
+        for (i, _), send in reversed(list(zip(sends, ready))):
             (by_even, by_odd)[i][t] = lax.ppermute(send, line_axes[i], (even, odd)[i])
         at = len(sends)
         for store, masks in held_now:

time: 169 us -> 169 us (level)
  no operation moved by 1% of the time
where the time goes in v7:
time: 169 us; the launch traced here: 168 us
  waiting for transfers between devices  56.3 us (33%)
  starting transfers between devices  45.2 us (27%)
  other arithmetic  17.9 us (11%)
  matrix products  16.9 us (10%)
  local copies, waits for them, and re-layouts  12.4 us (7%)
  Pallas kernels  10.6 us (6%)
  between operations  9.05 us (5%)
    ppermute x10, waiting for transfers between devices, per_device(): (by_even, by_odd)[i][t] = lax.ppermute(send, line_axes[i], (even, odd)[i])  28.9 us
    ppermute x9, waiting for transfers between devices, row_step(): return lax.ppermute(x, ('rep', 'row'), pairs)  17 us
    ppermute x9, starting transfers between devices, row_step(): return lax.ppermute(x, ('rep', 'row'), pairs)  14.9 us
    ppermute x10, starting transfers between devices, per_device(): (by_even, by_odd)[i][t] = lax.ppermute(send, line_axes[i], (even, odd)[i])  14.2 us
    dot_general x8, matrix products, dot(): return jnp.dot(x, w, preferred_element_type=f32)  13.9 us
    ppermute x3, starting transfers between devices, line_step(): by_even[step] = lax.ppermute(by_odd[step - 1], 'col', even)  13.4 us
    unnamed x54, local copies, waits for them, and re-layouts  10.2 us
    ppermute x3, waiting for transfers between devices, line_step(): by_even[step] = lax.ppermute(by_odd[step - 1], 'col', even)  10.2 us
  transfers between devices with their start and end apart: 34, of which 16 were waited for; matrix products, arithmetic and copies ran while one was open for 26% of the time, Pallas kernels for 4%

profile of v7, /device:TPU:0, one launch (start us, length us, event | category | flops | bytes accessed | tf_op | source)
XLA Modules:
  0.0 168.3 jit_solution(10104685855734447591)
XLA Ops:
  1.2 2.6 %shard_map.122 = bf16[512,1536]{1,0:T(8,128)(2,1)} custom-call(s32[1]{0:T(128)} %bitcast.2.core_ref, bf16[512,1536]{1,0:T(8,128)(2,1)} %top_ref.1, bf16[512,1536]{1,0:T(8,128)(2,1)} %bottom_ref.1), custom_call_target="tpu_custom_call" | custom-call | bytes 3145728 | tf_op jit(solution)/shard_map/pallas_call | solution.py:68
  3.8 2.7 %collective-permute-start.2 = (bf16[512,1536]{1,0:T(8,128)(2,1)}, bf16[512,1536]{1,0:T(8,128)(2,1)}, u32[]{:S(2)}, u32[]{:S(2)}) collective-permute-start(bf16[512,1536]{1,0:T(8,128)(2,1)} %shard_map.122), channel_id=1, source_target_pairs={{0,4},{4,0},{8,12},{12,8},{16,24},{20,28},{24,16},{28,20},{1,5},{5... | collective-permute-start | bytes 4718600 | tf_op jit(solution)/shard_map/ppermute | solution.py:41
  8.1 2.9 %bitcast_dynamic-update-slice_fusion.5 = (bf16[6,512,512]{2,1,0:T(8,128)(2,1)}, bf16[512,512]{1,0:T(8,128)(2,1)}) fusion(bf16[512,512]{1,0:T(8,128)(2,1)} %collective-permute-done, bf16[512,512]{1,0:T(8,128)(2,1)} %param.11, s32[512]{0:T(512)S(1)} %fusion.75), kind=kOutput, calls=%fused_computation.125 | convolution fusion | flops 539754496 | bytes 2099200 | tf_op jit(solution)/shard_map/dot_general | solution.py:168
  21.1 3.8 %collective-permute-done.1 = bf16[512,512]{1,0:T(8,128)(2,1)} collective-permute-done((bf16[512,512]{1,0:T(8,128)(2,1)}, bf16[512,512]{1,0:T(8,128)(2,1)}, u32[]{:S(2)}, u32[]{:S(2)}) %collective-permute-start.1) | collective-permute-done | bytes 524320 | tf_op jit(solution)/shard_map/ppermute | solution.py:178
  25.0 3.1 %collective-permute-start.5 = (bf16[512,512]{1,0:T(8,128)(2,1)}, bf16[512,512]{1,0:T(8,128)(2,1)S(1)}, u32[]{:S(2)}, u32[]{:S(2)}) collective-permute-start(bf16[512,512]{1,0:T(8,128)(2,1)} %collective-permute-done.4), channel_id=1, source_target_pairs={{0,1},{1,0},{2,3},{3,2},{4,5},{5,4},{6,7},{7,6},{8,9},{9,8},{10,11... | collective-permute-start | bytes 1572872 | tf_op jit(solution)/shard_map/ppermute | solution.py:178
  30.8 8.7 %collective-permute-start.7 = (bf16[512,512]{1,0:T(8,128)(2,1)S(1)}, bf16[512,512]{1,0:T(8,128)(2,1)S(1)}, u32[]{:S(2)}, u32[]{:S(2)}) collective-permute-start(bf16[512,512]{1,0:T(8,128)(2,1)S(1)} %collective-permute-done.6), channel_id=1, source_target_pairs={{0,1},{1,0},{2,3},{3,2},{4,5},{5,4},{6,7},{7,6},{8,9},{9,8},{10,11... | collective-permute-start | bytes 1572872 | tf_op jit(solution)/shard_map/ppermute | solution.py:178
  45.4 5.4 %collective-permute-done.7 = bf16[512,512]{1,0:T(8,128)(2,1)S(1)} collective-permute-done((bf16[512,512]{1,0:T(8,128)(2,1)S(1)}, bf16[512,512]{1,0:T(8,128)(2,1)S(1)}, u32[]{:S(2)}, u32[]{:S(2)}) %collective-permute-start.7) | collective-permute-done | bytes 524320 | tf_op jit(solution)/shard_map/ppermute | solution.py:178
  55.7 2.6 %fusion.95 = f32[512,1536]{1,0:T(8,128)S(1)} fusion(bf16[512,1536]{1,0:T(8,128)(2,1)S(1)} %select_dynamic-update-slice_fusion, bf16[1536,1536]{1,0:T(8,128)(2,1)S(1)} %get-tuple-element.115), kind=kOutput, calls=%fused_computation.179 | convolution fusion | flops 2415919104 | bytes 9437184 | tf_op jit(solution)/shard_map/dot_general | solution.py:216
  58.3 2.6 %fusion.94 = f32[512,1536]{1,0:T(8,128)S(1)} fusion(bf16[512,1536]{1,0:T(8,128)(2,1)S(1)} %select_dynamic-update-slice_fusion, bf16[1536,1536]{1,0:T(8,128)(2,1)S(1)} %get-tuple-element.116), kind=kOutput, calls=%fused_computation.178 | convolution fusion | flops 2415919104 | bytes 9437184 | tf_op jit(solution)/shard_map/dot_general | solution.py:216
  70.8 2.2 %collective-permute-start.15 = (bf16[512,512]{1,0:T(8,128)(2,1)S(1)}, bf16[512,512]{1,0:T(8,128)(2,1)S(1)}, u32[]{:S(2)}, u32[]{:S(2)}) collective-permute-start(bf16[512,512]{1,0:T(8,128)(2,1)S(1)} %convolution_convert_fusion), channel_id=1, source_target_pairs={{0,1},{1,0},{2,3},{3,2},{4,5},{5,4},{6,7},{7,6},{8,9},{9,8},{10,11... | collective-permute-start | bytes 1572872 | tf_op jit(solution)/shard_map/ppermute | solution.py:338
  73.0 9.4 %collective-permute-done.12 = bf16[768,512]{1,0:T(8,128)(2,1)S(1)} collective-permute-done((bf16[768,512]{1,0:T(8,128)(2,1)S(1)}, bf16[768,512]{1,0:T(8,128)(2,1)S(1)}, u32[]{:S(2)}, u32[]{:S(2)}) %collective-permute-start.12) | collective-permute-done | bytes 786464 | tf_op jit(solution)/shard_map/ppermute | solution.py:41
  91.1 4.2 %collective-permute-done.17 = bf16[768,512]{1,0:T(8,128)(2,1)} collective-permute-done((bf16[768,512]{1,0:T(8,128)(2,1)S(1)}, bf16[768,512]{1,0:T(8,128)(2,1)}, u32[]{:S(2)}, u32[]{:S(2)}) %collective-permute-start.17) | collective-permute-done | bytes 786464 | tf_op jit(solution)/shard_map/ppermute | solution.py:41
  96.2 2.1 %collective-permute-start.21 = (bf16[256,1024]{1,0:T(8,128)(2,1)}, bf16[256,1024]{1,0:T(8,128)(2,1)}, u32[]{:S(2)}, u32[]{:S(2)}) collective-permute-start(bf16[256,1024]{1,0:T(8,128)(2,1)} %constant_dynamic-slice_fusion.4), channel_id=1, source_target_pairs={{0,4},{4,0},{8,12},{12,8},{16,24},{20,28},{24,16},{28,20},{1,5},{5... | collective-permute-start | bytes 1572872 | tf_op jit(solution)/shard_map/ppermute | solution.py:41
  98.3 5.7 %collective-permute-done.19 = bf16[512,512]{1,0:T(8,128)(2,1)} collective-permute-done((bf16[512,512]{1,0:T(8,128)(2,1)}, bf16[512,512]{1,0:T(8,128)(2,1)}, u32[]{:S(2)}, u32[]{:S(2)}) %collective-permute-start.19) | collective-permute-done | bytes 524320 | tf_op jit(solution)/shard_map/ppermute | solution.py:338
  103.9 2.1 %fusion.34 = bf16[512,512]{1,0:T(8,128)(2,1)} fusion(bf16[512,512]{1,0:T(8,128)(2,1)} %fusion.28, bf16[512,512]{1,0:T(8,128)(2,1)} %collective-permute-done.19), kind=kLoop, calls=%fused_computation.66 | loop fusion | flops 1048576 | bytes 1572864 | tf_op jit(solution)/shard_map/convert_element_type | solution.py:327
  112.5 2.9 %fusion.22 = bf16[512,512]{1,0:T(8,128)(2,1)S(1)} fusion(bf16[768,512]{1,0:T(8,128)(2,1)} %collective-permute-done.20, bf16[768,512]{1,0:T(8,128)(2,1)} %collective-permute-done.17, bf16[512,768]{1,0:T(8,128)(2,1)} %copy-done.18, bf16[512,768]{1,0:T(8,128)(2,1)} %copy-done.17), kind=kOutput, calls=%fused_computation.60 | convolution fusion | flops 811859968 | bytes 3670016 | tf_op jit(solution)/shard_map/dot_general | solution.py:216
  115.4 6.4 %collective-permute-done.23 = bf16[512,512]{1,0:T(8,128)(2,1)} collective-permute-done((bf16[512,512]{1,0:T(8,128)(2,1)}, bf16[512,512]{1,0:T(8,128)(2,1)}, u32[]{:S(2)}, u32[]{:S(2)}) %collective-permute-start.23) | collective-permute-done | bytes 524320 | tf_op jit(solution)/shard_map/ppermute | solution.py:338
  123.3 2.7 %collective-permute-start.27 = (bf16[512,512]{1,0:T(8,128)(2,1)S(1)}, bf16[512,512]{1,0:T(8,128)(2,1)S(1)}, u32[]{:S(2)}, u32[]{:S(2)}) collective-permute-start(bf16[512,512]{1,0:T(8,128)(2,1)S(1)} %add_convert_fusion), channel_id=1, source_target_pairs={{0,1},{1,0},{2,3},{3,2},{4,5},{5,4},{6,7},{7,6},{8,9},{9,8},{10,11... | collective-permute-start | bytes 1572872 | tf_op jit(solution)/shard_map/ppermute | solution.py:338
  129.6 7.0 %collective-permute-done.27 = bf16[512,512]{1,0:T(8,128)(2,1)S(1)} collective-permute-done((bf16[512,512]{1,0:T(8,128)(2,1)S(1)}, bf16[512,512]{1,0:T(8,128)(2,1)S(1)}, u32[]{:S(2)}, u32[]{:S(2)}) %collective-permute-start.27) | collective-permute-done | bytes 524320 | tf_op jit(solution)/shard_map/ppermute | solution.py:338
  136.8 4.4 %collective-permute-start.31 = (bf16[512,512]{1,0:T(8,128)(2,1)}, bf16[512,512]{1,0:T(8,128)(2,1)S(1)}, u32[]{:S(2)}, u32[]{:S(2)}) collective-permute-start(bf16[512,512]{1,0:T(8,128)(2,1)} %fusion.50), channel_id=1, source_target_pairs={{0,1},{1,0},{2,3},{3,2},{4,5},{5,4},{6,7},{7,6},{8,9},{9,8},{10,11... | collective-permute-start | bytes 1572872 | tf_op jit(solution)/shard_map/ppermute | solution.py:338
  145.1 6.4 %collective-permute-done.31 = bf16[512,512]{1,0:T(8,128)(2,1)S(1)} collective-permute-done((bf16[512,512]{1,0:T(8,128)(2,1)}, bf16[512,512]{1,0:T(8,128)(2,1)S(1)}, u32[]{:S(2)}, u32[]{:S(2)}) %collective-permute-start.31) | collective-permute-done | bytes 524320 | tf_op jit(solution)/shard_map/ppermute | solution.py:338
  154.9 3.0 %shard_map.124.refs_4_ = f32[512,1024]{1,0:T(8,128)S(1)} custom-call(s32[2]{0:T(128)S(1)} %pad_add_fusion.at_ref, bf16[512,256]{1,0:T(8,128)(2,1)S(1)} %get-tuple-element.128.refs_0_, bf16[512,256]{1,0:T(8,128)(2,1)S(1)} %get-tuple-element.127.refs_1_, bf16[512,256]{1,0:T(8,128)(2,1)S(1)} %get-tuple-element.126.refs_2_, ...), custom_call_target="tpu_custom_call" | custom-call | flops 1073741824 | bytes 7340032 | tf_op jit(solution)/shard_map/pallas_call | solution.py:122
  159.3 3.3 %collective-permute-done.32 = bf16[512,512]{1,0:T(8,128)(2,1)S(1)} collective-permute-done((bf16[512,512]{1,0:T(8,128)(2,1)S(1)}, bf16[512,512]{1,0:T(8,128)(2,1)S(1)}, u32[]{:S(2)}, u32[]{:S(2)}) %collective-permute-start.32) | collective-permute-done | bytes 524320 | tf_op jit(solution)/shard_map/ppermute | solution.py:338
  165.0 3.3 %shard_map.125 = (bf16[512,1024]{1,0:T(8,128)(2,1)}, bf16[512,512]{1,0:T(8,128)(2,1)}) custom-call(s32[2]{0:T(128)S(1)} %pad_add_fusion.at_ref, bf16[512,256]{1,0:T(8,128)(2,1)S(1)} %get-tuple-element.130.refs_0_, bf16[512,256]{1,0:T(8,128)(2,1)S(1)} %get-tuple-element.129.refs_1_, bf16[256,1024]{1,0:T(8,128)(2,1)S(1)} %collective-permute-done.28.refs_2_, ...), custom_call_target="tpu_custom_call" | custom-call | flops 536870912 | bytes 5767168 | tf_op jit(solution)/shard_map/pallas_call | solution.py:122
  (158 shorter events, 59.7 us)
Async XLA Ops:
  3.8 37.2 %collective-permute-start.2 = (bf16[512,1536]{1,0:T(8,128)(2,1)}, bf16[512,1536]{1,0:T(8,128)(2,1)}, u32[]{:S(2)}, u32[]{:S(2)}) collective-permute-start(bf16[512,1536]{1,0:T(8,128)(2,1)} %shard_map.122), channel_id=1, source_target_pairs={{0,4},{4,0},{8,12},{12,8},{16,24},{20,28},{24,16},{28,20},{1,5},{5... | collective-permute-start | bytes 4718600 | tf_op jit(solution)/shard_map/ppermute | solution.py:41
  6.5 35.3 %collective-permute-start.3 = (bf16[512,1536]{1,0:T(8,128)(2,1)}, bf16[512,1536]{1,0:T(8,128)(2,1)}, u32[]{:S(2)}, u32[]{:S(2)}) collective-permute-start(bf16[512,1536]{1,0:T(8,128)(2,1)} %shard_map.122), channel_id=1, source_target_pairs={{0,8},{4,12},{8,0},{12,4},{16,20},{20,16},{24,28},{28,24},{1,9},{5... | collective-permute-start | bytes 4718600 | tf_op jit(solution)/shard_map/ppermute | solution.py:41
  11.0 14.0 %collective-permute-start.1 = (bf16[512,512]{1,0:T(8,128)(2,1)}, bf16[512,512]{1,0:T(8,128)(2,1)}, u32[]{:S(2)}, u32[]{:S(2)}) collective-permute-start(bf16[512,512]{1,0:T(8,128)(2,1)} %get-tuple-element.150), channel_id=1, source_target_pairs={{0,1},{1,0},{2,3},{3,2},{4,5},{5,4},{6,7},{7,6},{8,9},{9,8},{10,11... | collective-permute-start | bytes 1572872 | tf_op jit(solution)/shard_map/ppermute | solution.py:178
  12.6 12.4 %collective-permute-start.4 = (bf16[512,512]{1,0:T(8,128)(2,1)}, bf16[512,512]{1,0:T(8,128)(2,1)}, u32[]{:S(2)}, u32[]{:S(2)}) collective-permute-start(bf16[512,512]{1,0:T(8,128)(2,1)} %get-tuple-element.150), channel_id=1, source_target_pairs={{1,2},{2,1},{17,18},{18,17},{0,16},{3,19},{16,0},{19,3},{5,6},{6,5... | collective-permute-start | bytes 1572872 | tf_op jit(solution)/shard_map/ppermute | solution.py:180
  25.0 15.5 %collective-permute-start.5 = (bf16[512,512]{1,0:T(8,128)(2,1)}, bf16[512,512]{1,0:T(8,128)(2,1)S(1)}, u32[]{:S(2)}, u32[]{:S(2)}) collective-permute-start(bf16[512,512]{1,0:T(8,128)(2,1)} %collective-permute-done.4), channel_id=1, source_target_pairs={{0,1},{1,0},{2,3},{3,2},{4,5},{5,4},{6,7},{7,6},{8,9},{9,8},{10,11... | collective-permute-start | bytes 1572872 | tf_op jit(solution)/shard_map/ppermute | solution.py:178
  30.8 19.9 %collective-permute-start.7 = (bf16[512,512]{1,0:T(8,128)(2,1)S(1)}, bf16[512,512]{1,0:T(8,128)(2,1)S(1)}, u32[]{:S(2)}, u32[]{:S(2)}) collective-permute-start(bf16[512,512]{1,0:T(8,128)(2,1)S(1)} %collective-permute-done.6), channel_id=1, source_target_pairs={{0,1},{1,0},{2,3},{3,2},{4,5},{5,4},{6,7},{7,6},{8,9},{9,8},{10,11... | collective-permute-start | bytes 1572872 | tf_op jit(solution)/shard_map/ppermute | solution.py:178
  41.8 13.8 %collective-permute-start.10 = (bf16[512,1536]{1,0:T(8,128)(2,1)}, bf16[512,1536]{1,0:T(8,128)(2,1)S(1)}, u32[]{:S(2)}, u32[]{:S(2)}) collective-permute-start(bf16[512,1536]{1,0:T(8,128)(2,1)} %collective-permute-done.2), channel_id=1, source_target_pairs={{0,16},{16,0},{1,17},{17,1},{2,18},{18,2},{3,19},{19,3},{4,20},{20... | collective-permute-start | bytes 4718600 | tf_op jit(solution)/shard_map/ppermute | solution.py:19
  42.1 20.6 %collective-permute-start.8 = (bf16[512,1536]{1,0:T(8,128)(2,1)}, bf16[512,1536]{1,0:T(8,128)(2,1)S(1)}, u32[]{:S(2)}, u32[]{:S(2)}) collective-permute-start(bf16[512,1536]{1,0:T(8,128)(2,1)} %collective-permute-done.2), channel_id=1, source_target_pairs={{0,8},{4,12},{8,0},{12,4},{16,20},{20,16},{24,28},{28,24},{1,9},{5... | collective-permute-start | bytes 4718600 | tf_op jit(solution)/shard_map/ppermute | solution.py:41
  62.7 19.6 %collective-permute-start.12 = (bf16[768,512]{1,0:T(8,128)(2,1)S(1)}, bf16[768,512]{1,0:T(8,128)(2,1)S(1)}, u32[]{:S(2)}, u32[]{:S(2)}) collective-permute-start(bf16[768,512]{1,0:T(8,128)(2,1)S(1)} %constant_dynamic-slice_fusion.5), channel_id=1, source_target_pairs={{0,4},{4,0},{8,12},{12,8},{16,24},{20,28},{24,16},{28,20},{1,5},{5... | collective-permute-start | bytes 2359304 | tf_op jit(solution)/shard_map/ppermute | solution.py:41
  64.7 17.9 %collective-permute-start.13 = (bf16[768,512]{1,0:T(8,128)(2,1)S(1)}, bf16[768,512]{1,0:T(8,128)(2,1)S(1)}, u32[]{:S(2)}, u32[]{:S(2)}) collective-permute-start(bf16[768,512]{1,0:T(8,128)(2,1)S(1)} %constant_dynamic-slice_fusion.5), channel_id=1, source_target_pairs={{0,8},{4,12},{8,0},{12,4},{16,20},{20,16},{24,28},{28,24},{1,9},{5... | collective-permute-start | bytes 2359304 | tf_op jit(solution)/shard_map/ppermute | solution.py:41
  70.8 14.5 %collective-permute-start.15 = (bf16[512,512]{1,0:T(8,128)(2,1)S(1)}, bf16[512,512]{1,0:T(8,128)(2,1)S(1)}, u32[]{:S(2)}, u32[]{:S(2)}) collective-permute-start(bf16[512,512]{1,0:T(8,128)(2,1)S(1)} %convolution_convert_fusion), channel_id=1, source_target_pairs={{0,1},{1,0},{2,3},{3,2},{4,5},{5,4},{6,7},{7,6},{8,9},{9,8},{10,11... | collective-permute-start | bytes 1572872 | tf_op jit(solution)/shard_map/ppermute | solution.py:338
  83.3 12.1 %collective-permute-start.17 = (bf16[768,512]{1,0:T(8,128)(2,1)S(1)}, bf16[768,512]{1,0:T(8,128)(2,1)}, u32[]{:S(2)}, u32[]{:S(2)}) collective-permute-start(bf16[768,512]{1,0:T(8,128)(2,1)S(1)} %collective-permute-done.12), channel_id=1, source_target_pairs={{0,8},{4,12},{8,0},{12,4},{16,20},{20,16},{24,28},{28,24},{1,9},{5... | collective-permute-start | bytes 2359304 | tf_op jit(solution)/shard_map/ppermute | solution.py:41
  89.5 14.5 %collective-permute-start.19 = (bf16[512,512]{1,0:T(8,128)(2,1)}, bf16[512,512]{1,0:T(8,128)(2,1)}, u32[]{:S(2)}, u32[]{:S(2)}) collective-permute-start(bf16[512,512]{1,0:T(8,128)(2,1)} %fusion.28), channel_id=1, source_target_pairs={{0,1},{1,0},{2,3},{3,2},{4,5},{5,4},{6,7},{7,6},{8,9},{9,8},{10,11... | collective-permute-start | bytes 1572872 | tf_op jit(solution)/shard_map/ppermute | solution.py:338
  91.1 14.9 %collective-permute-start.18 = (bf16[512,512]{1,0:T(8,128)(2,1)}, bf16[512,512]{1,0:T(8,128)(2,1)}, u32[]{:S(2)}, u32[]{:S(2)}) collective-permute-start(bf16[512,512]{1,0:T(8,128)(2,1)} %fusion.31), channel_id=1, source_target_pairs={{1,2},{2,1},{17,18},{18,17},{0,16},{3,19},{16,0},{19,3},{5,6},{6,5... | collective-permute-start | bytes 1572872 | tf_op jit(solution)/shard_map/ppermute | solution.py:338
  95.4 12.8 %collective-permute-start.20 = (bf16[768,512]{1,0:T(8,128)(2,1)}, bf16[768,512]{1,0:T(8,128)(2,1)}, u32[]{:S(2)}, u32[]{:S(2)}) collective-permute-start(bf16[768,512]{1,0:T(8,128)(2,1)} %collective-permute-done.17), channel_id=1, source_target_pairs={{0,16},{16,0},{1,17},{17,1},{2,18},{18,2},{3,19},{19,3},{4,20},{20... | collective-permute-start | bytes 2359304 | tf_op jit(solution)/shard_map/ppermute | solution.py:19
  96.2 11.9 %collective-permute-start.21 = (bf16[256,1024]{1,0:T(8,128)(2,1)}, bf16[256,1024]{1,0:T(8,128)(2,1)}, u32[]{:S(2)}, u32[]{:S(2)}) collective-permute-start(bf16[256,1024]{1,0:T(8,128)(2,1)} %constant_dynamic-slice_fusion.4), channel_id=1, source_target_pairs={{0,4},{4,0},{8,12},{12,8},{16,24},{20,28},{24,16},{28,20},{1,5},{5... | collective-permute-start | bytes 1572872 | tf_op jit(solution)/shard_map/ppermute | solution.py:41
  108.1 13.7 %collective-permute-start.23 = (bf16[512,512]{1,0:T(8,128)(2,1)}, bf16[512,512]{1,0:T(8,128)(2,1)}, u32[]{:S(2)}, u32[]{:S(2)}) collective-permute-start(bf16[512,512]{1,0:T(8,128)(2,1)} %add_convert_fusion.1), channel_id=1, source_target_pairs={{0,1},{1,0},{2,3},{3,2},{4,5},{5,4},{6,7},{7,6},{8,9},{9,8},{10,11... | collective-permute-start | bytes 1572872 | tf_op jit(solution)/shard_map/ppermute | solution.py:338
  109.9 13.4 %collective-permute-start.24 = (bf16[256,1024]{1,0:T(8,128)(2,1)}, bf16[256,1024]{1,0:T(8,128)(2,1)}, u32[]{:S(2)}, u32[]{:S(2)}) collective-permute-start(bf16[256,1024]{1,0:T(8,128)(2,1)} %constant_dynamic-slice_fusion.4), channel_id=1, source_target_pairs={{0,8},{4,12},{8,0},{12,4},{16,20},{20,16},{24,28},{28,24},{1,9},{5... | collective-permute-start | bytes 1572872 | tf_op jit(solution)/shard_map/ppermute | solution.py:41
  111.1 11.9 %collective-permute-start.22 = (bf16[512,512]{1,0:T(8,128)(2,1)}, bf16[512,512]{1,0:T(8,128)(2,1)S(1)}, u32[]{:S(2)}, u32[]{:S(2)}) collective-permute-start(bf16[512,512]{1,0:T(8,128)(2,1)} %fusion.34), channel_id=1, source_target_pairs={{1,2},{2,1},{17,18},{18,17},{0,16},{3,19},{16,0},{19,3},{5,6},{6,5... | collective-permute-start | bytes 1572872 | tf_op jit(solution)/shard_map/ppermute | solution.py:338
  111.1 12.1 %collective-permute-start.25 = (bf16[256,1024]{1,0:T(8,128)(2,1)}, bf16[256,1024]{1,0:T(8,128)(2,1)S(1)}, u32[]{:S(2)}, u32[]{:S(2)}) collective-permute-start(bf16[256,1024]{1,0:T(8,128)(2,1)} %collective-permute-done.21.refs_4_), channel_id=1, source_target_pairs={{0,16},{16,0},{1,17},{17,1},{2,18},{18,2},{3,19},{19,3},{4,20},{20... | collective-permute-start | bytes 1572872 | tf_op jit(solution)/shard_map/ppermute | solution.py:19
  111.6 25.1 %collective-permute-start.28 = (bf16[256,1024]{1,0:T(8,128)(2,1)}, bf16[256,1024]{1,0:T(8,128)(2,1)S(1)}, u32[]{:S(2)}, u32[]{:S(2)}) collective-permute-start(bf16[256,1024]{1,0:T(8,128)(2,1)} %collective-permute-done.21.refs_4_), channel_id=1, source_target_pairs={{0,8},{4,12},{8,0},{12,4},{16,20},{20,16},{24,28},{28,24},{1,9},{5... | collective-permute-start | bytes 1572872 | tf_op jit(solution)/shard_map/ppermute | solution.py:41
  123.3 13.3 %collective-permute-start.27 = (bf16[512,512]{1,0:T(8,128)(2,1)S(1)}, bf16[512,512]{1,0:T(8,128)(2,1)S(1)}, u32[]{:S(2)}, u32[]{:S(2)}) collective-permute-start(bf16[512,512]{1,0:T(8,128)(2,1)S(1)} %add_convert_fusion), channel_id=1, source_target_pairs={{0,1},{1,0},{2,3},{3,2},{4,5},{5,4},{6,7},{7,6},{8,9},{9,8},{10,11... | collective-permute-start | bytes 1572872 | tf_op jit(solution)/shard_map/ppermute | solution.py:338
  136.8 14.6 %collective-permute-start.31 = (bf16[512,512]{1,0:T(8,128)(2,1)}, bf16[512,512]{1,0:T(8,128)(2,1)S(1)}, u32[]{:S(2)}, u32[]{:S(2)}) collective-permute-start(bf16[512,512]{1,0:T(8,128)(2,1)} %fusion.50), channel_id=1, source_target_pairs={{0,1},{1,0},{2,3},{3,2},{4,5},{5,4},{6,7},{7,6},{8,9},{9,8},{10,11... | collective-permute-start | bytes 1572872 | tf_op jit(solution)/shard_map/ppermute | solution.py:338
  143.2 20.3 %collective-permute-start.33 = (bf16[256,1024]{1,0:T(8,128)(2,1)S(1)}, bf16[256,1024]{1,0:T(8,128)(2,1)}, u32[]{:S(2)}, u32[]{:S(2)}) collective-permute-start(bf16[256,1024]{1,0:T(8,128)(2,1)S(1)} %collective-permute-done.28.refs_2_), channel_id=1, source_target_pairs={{0,16},{16,0},{1,17},{17,1},{2,18},{18,2},{3,19},{19,3},{4,20},{20... | collective-permute-start | bytes 1572872 | tf_op jit(solution)/shard_map/ppermute | solution.py:19
  (33 other events, 298.4 us)
